TPU v7x, 256 devices: a whole 4x4x8 slice. The times are simulated.
256 devices in a mesh: dp: 4 (over y_hi, core), ctx: 8 (over y_lo, x), fsdp: 8 (over z).
Axes of the slice: x: 4, y: 4 (y_hi: 2, y_lo: 2; y = y_hi * 2 + y_lo), z: 8, core: 2. Of those that a mesh axis runs over, the one named last changes fastest.
Arguments:
- layer_in: bfloat16 [128, 1024, 1024], P(('dp', 'fsdp'), 'ctx'), may hold values from -6 to 6
- repack_plan: int32 [128], P(('dp', 'fsdp')), may hold values from 0 to 3, as said below
- lengths: int32 [128], P(('dp', 'fsdp')), may hold values from 1 to 1024, 65536 in all
- stamps: int32 [128, 1024], P(('dp', 'fsdp'), 'ctx'), may hold values from 0 to 255, as said below
- w_in: bfloat16 [1024, 2048], P('fsdp'), may hold values from -0.1875 to 0.1875
- w_out: bfloat16 [512, 1024], P('fsdp'), may hold values from -0.25 to 0.25
- time_bias: bfloat16 [2, 128], replicated, may hold values from -4 to 4
- grad_out: bfloat16 [128, 1024, 1024], P(('dp', 'fsdp'), 'ctx'), may hold values from -6 to 6
Outputs:
- input_gradient: bfloat16 [128, 1024, 1024], P(('dp', 'fsdp'), 'ctx')
- grad_w_in: float32 [1024, 2048], P('fsdp')
- grad_w_out: float32 [512, 1024], P('fsdp')
- grad_bias: float32 [2, 128], replicated
Inputs may be any that keep to these rules, and one draw needn't show every extreme that they name: `repack_plan`: each aligned block of 4 entries (one device's) is a permutation of 0 to 3. `stamps`: nondecreasing along each history, and 255 at its last position. `lengths`: one history has exactly 1024 events.
All inputs are finite; a program needn't handle non-finite values. No bound on the sum of `lengths` on one device may be relied on, other than what follows from the above.
Results may differ from a plain program's by a relative error of at most 0.025.
Values may be sent and summed in bfloat16 or wider, within the bound.
No kernel may reach another device: no remote copies, remote signals or barrier semaphores. Data moves between devices by JAX's collectives and lax.ppermute only.
A program may use at most 128 MiB of HBM per device.

v0:
```python
import math

import jax
import jax.numpy as jnp
from jax import lax
from jax.sharding import PartitionSpec as P

H = 2
DH = 256


EPS = 1e-05


def layer_normalize(values):
    centred = values - jnp.mean(values, axis=-1, keepdims=True)
    inverse_permutation = lax.rsqrt(jnp.mean(centred * centred, axis=-1, keepdims=True) + EPS)
    return (centred * inverse_permutation, inverse_permutation)


def normalize_backward(grad, normalized_rows, inverse_permutation):
    return inverse_permutation * (
        grad
        - jnp.mean(grad, axis=-1, keepdims=True)
        - normalized_rows * jnp.mean(grad * normalized_rows, axis=-1, keepdims=True)
    )


def silu_slope(values):
    sigma = jax.nn.sigmoid(values)
    return sigma * (1.0 + values * (1.0 - sigma))


def contract_last(left, right):
    return lax.dot_general(
        left, right, (((1,), (1,)), ((), ())), preferred_element_type=jnp.float32
    )


def contract_first(left, right):
    return lax.dot_general(
        left, right, (((0,), (0,)), ((), ())), preferred_element_type=jnp.float32
    )


def local(layer_in, repack_plan, lengths, stamps, w_in, w_out, time_bias, grad_out):
    seqs, rows_seq, width_model = layer_in.shape
    total_rows = seqs * rows_seq
    attn_width = H * DH
    buckets = time_bias.shape[1]
    scale = DH ** (-0.5)
    peers = lax.axis_size("dp")
    ordered = layer_in[repack_plan].reshape(peers, seqs // peers, rows_seq, width_model)
    packed_rows = lax.all_to_all(ordered, "dp", split_axis=0, concat_axis=0, tiled=True).reshape(
        total_rows, width_model
    )
    centred_scaled, inverse_permutation = layer_normalize(packed_rows.astype(jnp.float32))
    normalized_rows = centred_scaled.astype(jnp.bfloat16)
    upstream = grad_out.reshape(total_rows, width_model)
    w_full = lax.all_gather(w_in, "fsdp", axis=0, tiled=True)
    hidden = jnp.dot(normalized_rows, w_full, preferred_element_type=jnp.float32)
    active = jax.nn.silu(hidden).astype(jnp.bfloat16).reshape(seqs, rows_seq, 4, H, DH)
    gate_u = active[:, :, 0].reshape(total_rows, attn_width).astype(jnp.float32)
    values = active[:, :, 1]
    query = active[:, :, 2]
    keyset = active[:, :, 3]
    stamp_wire = stamps.astype(jnp.bfloat16)
    gathered_keys, gathered_values, gathered_times = (
        lax.all_gather(keyset, "ctx", axis=1, tiled=True),
        lax.all_gather(values, "ctx", axis=1, tiled=True),
        lax.all_gather(stamp_wire, "ctx", axis=1, tiled=True),
    )
    events = gathered_keys.shape[1]
    key_times = gathered_times.astype(jnp.int32)
    first = lax.axis_index("ctx") * rows_seq
    query_pos = first + lax.iota(jnp.int32, rows_seq)
    key_pos = lax.iota(jnp.int32, events)
    live = (
        (key_pos[None, None, :] <= query_pos[None, :, None])
        & (query_pos[None, :, None] < lengths[:, None, None])
    ).astype(jnp.float32)[:, None]
    width = math.gcd(64, events)
    blocks = events // width
    bucket_ids = lax.iota(jnp.int32, buckets)

    def one_hot(block_index):
        block_times = lax.dynamic_slice_in_dim(key_times, block_index * width, width, 1)
        spacing = jnp.clip(stamps[:, :, None] - block_times[:, None, :], 0, buckets - 1)
        return (spacing[..., None] == bucket_ids).astype(jnp.bfloat16)

    def bias_block(block_index):
        return jnp.einsum(
            "sqkn,hn->shqk", one_hot(block_index), time_bias, preferred_element_type=jnp.float32
        )

    bias = lax.map(bias_block, jnp.arange(blocks, dtype=jnp.int32))
    bias = jnp.moveaxis(bias, 0, 3).reshape(seqs, H, rows_seq, events)
    scores = (
        scale
        * jnp.einsum("sqhd,skhd->shqk", query, gathered_keys, preferred_element_type=jnp.float32)
        + bias
    )
    probs = (jax.nn.silu(scores) * live).astype(jnp.bfloat16)
    mixed = jnp.einsum(
        "shqk,skhd->sqhd", probs, gathered_values, preferred_element_type=jnp.float32
    ).reshape(total_rows, attn_width)
    gated = mixed * gate_u
    zhat, ginv = layer_normalize(gated)
    zlow = zhat.astype(jnp.bfloat16)
    dz = contract_last(upstream, lax.all_gather(w_out, "fsdp", axis=0, tiled=True))
    dgated = normalize_backward(dz, zhat, ginv)
    datt = (dgated * gate_u).astype(jnp.bfloat16).reshape(seqs, rows_seq, H, DH)
    dgate_u = dgated * mixed
    dprob = jnp.einsum("sqhd,skhd->shqk", datt, gathered_values, preferred_element_type=jnp.float32)
    dlow = (dprob * silu_slope(scores) * live).astype(jnp.bfloat16)
    dquery = (
        scale
        * jnp.einsum("shqk,skhd->sqhd", dlow, gathered_keys, preferred_element_type=jnp.float32)
    ).reshape(total_rows, attn_width)
    count = rows_seq * lax.axis_size("ctx")
    slope_part = dlow
    grad_value = jnp.einsum("shqk,sqhd->kshd", probs, datt, preferred_element_type=jnp.float32)
    grad_key = scale * jnp.einsum(
        "shqk,sqhd->kshd", slope_part, query, preferred_element_type=jnp.float32
    )
    owned = lax.psum_scatter(
        jnp.concatenate(
            [
                grad_value.reshape(count, seqs, attn_width),
                grad_key.reshape(count, seqs, attn_width),
            ],
            axis=2,
        ).astype(jnp.bfloat16),
        "ctx",
        scatter_dimension=0,
        tiled=True,
    ).astype(jnp.float32)
    owned = jnp.transpose(owned, (1, 0, 2)).reshape(total_rows, 2 * attn_width)

    def bias_step(total, block_index):
        slope_part = lax.dynamic_slice_in_dim(dlow, block_index * width, width, 3)
        return (
            total
            + jnp.einsum(
                "shqk,sqkn->hn",
                slope_part,
                one_hot(block_index),
                preferred_element_type=jnp.float32,
            ),
            None,
        )

    bias_grad, _ = lax.scan(
        bias_step, jnp.zeros((H, buckets), jnp.float32), jnp.arange(blocks, dtype=jnp.int32)
    )
    dact = jnp.concatenate([dgate_u, owned[:, :attn_width], dquery, owned[:, attn_width:]], axis=1)
    dhid = (dact * silu_slope(hidden)).astype(jnp.bfloat16)
    normalized_grad = contract_last(dhid, w_full)
    input_gradient = (
        normalize_backward(normalized_grad, centred_scaled, inverse_permutation)
        .astype(jnp.bfloat16)
        .reshape(seqs, rows_seq, width_model)
    )
    shard_in = lax.psum_scatter(
        contract_first(normalized_rows, dhid).astype(jnp.bfloat16),
        "fsdp",
        scatter_dimension=0,
        tiled=True,
    )
    shard_out = lax.psum_scatter(
        contract_first(zlow, upstream).astype(jnp.bfloat16), "fsdp", scatter_dimension=0, tiled=True
    )
    summed_in, summed_out = (
        lax.psum(shard_in, ("dp", "ctx")).astype(jnp.float32),
        lax.psum(shard_out, ("dp", "ctx")).astype(jnp.float32),
    )
    summed_bias = lax.psum(bias_grad, ("dp", "ctx", "fsdp"))
    histories = seqs * peers * lax.axis_size("fsdp")
    return (input_gradient, summed_in / histories, summed_out / histories, summed_bias / histories)


def solution(mesh):
    return jax.shard_map(
        local,
        mesh=mesh,
        in_specs=(
            P(("dp", "fsdp"), "ctx", None),
            P(("dp", "fsdp")),
            P(("dp", "fsdp")),
            P(("dp", "fsdp"), "ctx"),
            P("fsdp", None),
            P("fsdp", None),
            P(),
            P(("dp", "fsdp"), "ctx", None),
        ),
        out_specs=(P(("dp", "fsdp"), "ctx", None), P("fsdp", None), P("fsdp", None), P()),
        check_vma=False,
    )
```

profile of v0, /device:TPU:1, one launch (start us, length us, event | category | flops | bytes accessed | tf_op | source)
XLA Modules:
  0.0 749.1 jit_solution(10724057152841784159)
XLA Ops:
  8.6 2.8 gather_fusion
  11.4 6.7 all-to-all-start
  18.9 14.3 %all-to-all-done = bf16[4,1,128,1024]{3,2,1,0:T(8,128)(2,1)S(1)} async-done(((bf16[4,1,128,1024]{3,2,1,0:T(8,128)(2,1)}), bf16[4,1,128,1024]{3,2,1,0:T(8,128)(2,1)S(1)}, u32[]{:S(2)}, u32[]{:S(2)}) %all-to-all-start) | async-done | bytes 1048608 | tf_op jit(solution)/shard_map/all_to_all | solution.py:54
  34.2 34.3 %all-gather.7.cloned.1.call-done = bf16[1024,2048]{1,0:T(8,128)(2,1)} async-done(((bf16[128,2048]{1,0:T(8,128)(2,1)}), bf16[1024,2048]{1,0:T(8,128)(2,1)}) %all-gather.7.cloned.1.call-update) | async-done | bytes 4194320 | tf_op jit(solution)/shard_map/all_gather | solution.py:60
  68.5 7.5 multiply_convert_fusion.3
  75.9 4.5 reshape.220
  80.4 3.4 fusion.47
  84.8 15.0 %all_gather.18 = bf16[4,1024]{1,0:T(4,128)(2,1)S(1)} all-gather(bf16[4,128]{1,0:T(4,128)(2,1)S(1)} %convert_element_type.85), channel_id=1, replica_groups=mesh['dp'=4,'ctx'=8,'fsdp'=8] {'ctx'}, dimensions={1}, use_global_device_ids=true | all-gather | bytes 9216 | tf_op jit(solution)/shard_map/all_gather | solution.py:71
  101.2 153.5 %while.22 = (s32[]{:T(128)}, f32[16,4,2,128,64]{3,4,0,2,1:T(8,128)}, s32[4,128]{1,0:T(4,128)S(1)}, s32[16]{0:T(128)S(1)}, s32[4,1024]{1,0:T(4,128)S(1)}, /*index...) while((s32[]{:T(128)}, f32[16,4,2,128,64]{3,4,0,2,1:T(8,128)}, ...), condition=%wide.region_3.4_spmd.clone, body=%wide.region_2.3_spmd.clone.sunk | while | flops 21037060 | bytes 1054383 | solution.py:96
  102.6 7.4 fusion.68
  112.2 7.4 fusion.68
  121.8 7.4 fusion.68
  131.4 7.4 fusion.68
  141.0 7.4 fusion.68
  150.5 7.4 fusion.68
  160.2 7.4 fusion.68
  169.7 7.4 fusion.68
  179.3 7.4 fusion.68
  188.9 7.4 fusion.68
  198.5 7.4 fusion.68
  208.1 7.4 fusion.68
  217.7 7.4 fusion.68
  227.3 7.4 fusion.68
  236.9 7.4 fusion.68
  246.5 7.4 fusion.68
  254.6 5.4 copy.80
  261.8 2.9 fusion.48
  264.8 2.5 copy.82
  268.9 2.3 copy.118
  271.2 8.5 %multiply_convert_fusion.2 = (bf16[4,2,128,1024]{3,2,1,0:T(8,128)(2,1)}, f32[4,2,128,1024]{3,2,1,0:T(8,128)}) fusion(f32[4,128,1024]{2,1,0:T(8,128)} %and_convert_fusion, f32[4,2,128,1024]{3,2,1,0:T(8,128)} %copy.80, bf16[4,1024,1,2,256]{4,1,3,0,2:T(8,128)(2,1)} %all-gather.13.cloned.1.call-done, bf16[4,128,1,2,256]{4,3,2,1,0:T(2,128)(2,1)} %get-tuple-element.192), kind=kOutput, calls=%fused_computation.33 | convolution fusion | flops 545259520 | bytes 17301504 | tf_op jit(solution)/shard_map/sqhd,skhd->shqk/dot_general | solution.py:100
  279.7 4.2 fusion.40
  291.8 5.0 convolution_convert_fusion.1
  296.9 6.2 copy.90
  303.1 6.3 multiply_convert_fusion.1
  310.7 3.3 multiply_convert_fusion
  314.0 6.2 copy.91
  320.2 7.8 %pad_maximum_fusion = bf16[1024,4,1024]{2,0,1:T(8,128)(2,1)} fusion(bf16[1024,4,512]{2,0,1:T(8,128)(2,1)} %copy.91, bf16[1024,4,512]{2,0,1:T(8,128)(2,1)} %copy.90), kind=kLoop, calls=%fused_computation.20 | loop fusion | flops 16777216 | bytes 16777216 | tf_op jit(solution)/shard_map/concatenate | solution.py:127
  328.2 6.2 copy.95
  334.3 2.0 multiply_convert_fusion.5
  339.6 4.4 fusion.35
  346.6 76.5 %reduce-scatter.4.cloned.1.call-done = bf16[128,4,1024]{2,0,1:T(8,128)(2,1)} async-done(((bf16[1024,4,1024]{2,0,1:T(8,128)(2,1)}), bf16[128,4,1024]{2,0,1:T(8,128)(2,1)}) %reduce-scatter.4.cloned.1.call-update) | async-done | bytes 1048592 | tf_op jit(solution)/shard_map/reduce_scatter | solution.py:126
  428.8 4.3 convolution_convert_fusion
  433.2 112.3 %while.23 = (s32[]{:T(128)}, f32[2,128]{1,0:T(2,128)S(1)}, s32[16]{0:T(128)S(1)}, bf16[4,2,128,1024]{2,1,0,3:T(2,128)(2,1)}, s32[4,128]{1,0:T(4,128)S(1)}, /*ind...) while((s32[]{:T(128)}, f32[2,128]{1,0:T(2,128)S(1)}, ...), condition=%wide.region_16.17_spmd.clone, body=%wide.region_15.16_spmd.clone.sunk | while | flops 21037576 | bytes 402617 | solution.py:153
  434.8 5.5 fusion.70
  441.8 5.5 fusion.70
  448.8 5.5 fusion.70
  455.9 5.5 fusion.70
  462.9 5.5 fusion.70
  469.9 5.5 fusion.70
  476.9 5.5 fusion.70
  483.9 5.5 fusion.70
  491.0 5.5 fusion.70
  498.0 5.5 fusion.70
  505.0 5.5 fusion.70
  512.0 5.5 fusion.70
  519.0 5.5 fusion.70
  526.1 5.5 fusion.70
  533.1 5.5 fusion.70
  540.1 5.5 fusion.70
  545.6 75.9 %psum.23 = f32[2,128]{1,0:T(2,128)S(1)} all-reduce(f32[2,128]{1,0:T(2,128)S(1)} %get-tuple-element.79), channel_id=1, replica_groups=mesh['dp'=4,'ctx'=8,'fsdp'=8] {'dp','ctx','fsdp'}, use_global_device_ids=true, to_apply=%region_17.18 | all-reduce | flops 256 | bytes 2048 | tf_op jit(solution)/shard_map/psum | solution.py:177
  622.0 6.6 fusion.45
  628.7 3.1 multiply_convert_fusion.4
  631.8 106.7 %all-reduce.3.cloned.1.call-done = (bf16[128,2048]{1,0:T(8,128)(2,1)}, bf16[64,1024]{1,0:T(8,128)(2,1)}) async-done(((bf16[128,2048]{1,0:T(8,128)(2,1)}, bf16[64,1024]{1,0:T(8,128)(2,1)}), (bf16[128,2048]{1,0:T(8,128)(2,1)}, bf16[64,1024]{1,0:T(8,128)(2,1)})) %all-reduce.3.cloned.1.call-update) | async-done | bytes 655376 | tf_op jit(solution)/shard_map/psum | solution.py:174
  740.1 2.1 convert_multiply_fusion
  (219 shorter events, 70.1 us)
Async XLA Ops:
  7.2 254.7 %copy-start = (bf16[4,128,1024]{2,1,0:T(8,128)(2,1)S(1)}, bf16[4,128,1024]{2,1,0:T(8,128)(2,1)}, u32[]{:S(2)}) copy-start(bf16[4,128,1024]{2,1,0:T(8,128)(2,1)} %param.19) | copy-start | bytes 3145732
  7.2 61.3 %all-gather.7.cloned.1.call-start = ((), (), s32[]{:S(2)}) async-start(), calls=%async_computation.4 | async-start | bytes 4718592 | tf_op jit(solution)/shard_map/all_gather | solution.py:60
  11.4 21.8 %all-to-all-start = ((bf16[4,1,128,1024]{3,2,1,0:T(8,128)(2,1)}), bf16[4,1,128,1024]{3,2,1,0:T(8,128)(2,1)S(1)}, u32[]{:S(2)}, u32[]{:S(2)}) async-start(bf16[4,1,128,1024]{3,2,1,0:T(8,128)(2,1)} %bitcast), calls=%async_computation | async-start | bytes 2097152 | tf_op jit(solution)/shard_map/all_to_all | solution.py:54
  18.1 243.7 %all-gather.9.cloned.1.call-start = ((), (), s32[]{:S(2)}) async-start(), calls=%async_computation.5 | async-start | bytes 1179648 | tf_op jit(solution)/shard_map/all_gather | solution.py:110
  18.8 252.4 %all-gather.13.cloned.1.call-start = ((), (), s32[]{:S(2)}) async-start(), calls=%async_computation.10 | async-start | bytes 4718592 | tf_op jit(solution)/shard_map/all_gather | solution.py:69
  34.2 41.7 %copy-start.9 = (bf16[512,1024]{1,0:T(8,128)(2,1)}, bf16[512,1024]{1,0:T(8,128)(2,1)S(1)}, u32[]{:S(2)}) copy-start(bf16[512,1024]{1,0:T(8,128)(2,1)S(1)} %fusion.28) | copy-start | bytes 3145732
  75.9 8.9 %copy-start.11 = (s32[4,128]{1,0:T(4,128)S(1)}, s32[4,128]{1,0:T(4,128)}, u32[]{:S(2)}) copy-start(s32[4,128]{1,0:T(4,128)} %param.15) | copy-start | bytes 6148
  80.4 20.7 %copy-start.12 = (bf16[2,128]{1,0:T(2,128)(2,1)S(1)}, bf16[2,128]{1,0:T(2,128)(2,1)}, u32[]{:S(2)}) copy-start(bf16[2,128]{1,0:T(2,128)(2,1)} %param.18) | copy-start | bytes 1540
  84.7 195.0 %all-gather.11.cloned.1.call-start = ((), (), s32[]{:S(2)}) async-start(), calls=%async_computation.9 | async-start | bytes 4718592 | tf_op jit(solution)/shard_map/all_gather | solution.py:70
  100.9 322.2 %reduce-scatter.4.cloned.1.call-start = ((), (), s32[]{:S(2)}) async-start(), calls=%async_computation.6 | async-start | bytes 9437184 | tf_op jit(solution)/shard_map/reduce_scatter | solution.py:126
  254.6 5.4 copy-start.13
  267.8 12.0 %copy-start.4 = (bf16[4,128,1,2,256]{1,4,3,0,2:T(8,128)(2,1)}, bf16[4,128,1,2,256]{1,4,3,0,2:T(8,128)(2,1)S(1)}, u32[]{:S(2)}) copy-start(bf16[4,128,1,2,256]{1,4,3,0,2:T(8,128)(2,1)S(1)} %copy.108) | copy-start | bytes 1572868
  285.2 2.7 copy-start.2
  285.2 2.7 copy-start.3
  303.1 7.6 %copy-start.8 = (bf16[4,128,1,2,256]{4,3,2,1,0:T(2,128)(2,1)S(1)}, bf16[4,128,1,2,256]{4,3,2,1,0:T(2,128)(2,1)}, u32[]{:S(2)}) copy-start(bf16[4,128,1,2,256]{4,3,2,1,0:T(2,128)(2,1)} %get-tuple-element.192) | copy-start | bytes 1572868
  309.4 1.4 copy-start.1
  328.1 300.5 %reduce-scatter.8.cloned.1.call-start = ((), (), s32[]{:S(2)}) async-start(), calls=%async_computation.8 | async-start | bytes 1179648 | tf_op jit(solution)/shard_map/reduce_scatter | solution.py:170
  339.5 289.1 %reduce-scatter.6.cloned.1.call-start = ((), (), s32[]{:S(2)}) async-start(), calls=%async_computation.7 | async-start | bytes 4718592 | tf_op jit(solution)/shard_map/reduce_scatter | solution.py:164
  423.1 2.5 copy-start.5
  423.1 2.8 copy-start.6
  425.9 2.9 copy-start.10
  427.4 1.4 copy-start.7
  433.2 305.3 %all-reduce.3.cloned.1.call-start = ((), (), s32[]{:S(2)}) async-start(), calls=%async_computation.11 | async-start | bytes 1310720 | tf_op jit(solution)/shard_map/psum | solution.py:174
Sparse Core Ops, SparseCore 0:
  9.8 58.6 all-gather.6
  70.2 32.2 all-gather.8
  104.3 58.8 all-gather.12
  164.7 59.4 all-gather.10
  328.2 94.8 reduce-scatter.3
  425.5 33.0 reduce-scatter.7
  461.1 58.6 reduce-scatter.5
  628.8 109.6 all-reduce.2
where the time goes:
time: 751 us; the launch traced here: 749 us
  matrix products  261 us (35%)
  waiting for transfers between devices  233 us (31%)
  blocking collectives  90.9 us (12%)
  local copies, waits for them, and re-layouts  90 us (12%)
  other arithmetic  31 us (4%)
  loops' own time  21.4 us (3%)
  between operations  14.4 us (2%)
    dot_general x16, matrix products, bias_block(): jnp.einsum('sqkn,hn->shqk', one_hot(block_index), time_bias, preferred_el...  119 us
    psum x1, waiting for transfers between devices, local(): lax.psum(shard_in, ('dp', 'ctx')).astype(jnp.float32)  107 us
    dot_general x16, matrix products, bias_step(): jnp.einsum('shqk,sqkn->hn', slope_part, one_hot(block_index), preferred_e...  87.2 us
    reduce_scatter x1, waiting for transfers between devices, local(): lax.psum_scatter(jnp.concatenate([grad_value.reshape(count, seqs, attn_wi...  76.5 us
    psum x1, blocking collectives, local(): summed_bias = lax.psum(bias_grad, ('dp', 'ctx', 'fsdp'))  75.9 us
    all_gather x1, waiting for transfers between devices, local(): w_full = lax.all_gather(w_in, 'fsdp', axis=0, tiled=True)  34.3 us
    dynamic_slice x32, local copies, waits for them, and re-layouts, local(): bias = lax.map(bias_block, jnp.arange(blocks, dtype=jnp.int32))  18.8 us
    unnamed x36, local copies, waits for them, and re-layouts  17.2 us
  transfers between devices with their start and end apart: 9, of which 4 were waited for; matrix products, arithmetic and copies ran while one was open for 44% of the time, Pallas kernels for 0%

commit v1 on v0

v1 whole, which is shorter than its diff:
```python
import functools

import jax
import jax.numpy as jnp
from jax import lax
from jax.experimental import pallas as pl
from jax.experimental.pallas import tpu as pltpu
from jax.sharding import Mesh
from jax.sharding import PartitionSpec as P

DH = 256
D = 1024
L = 1024
EPS = 1e-05
BF = jnp.bfloat16
F32 = jnp.float32
BQ = 256
NQ = L // BQ
SHARD = 176
PLANE = ("yh", "core", "yl", "x")
CHIPS = ("yh", "yl", "x")
ANY = pl.BlockSpec(memory_space=pl.ANY)
VM = pl.BlockSpec(memory_space=pltpu.VMEM)
SM = pl.BlockSpec(memory_space=pltpu.SMEM)


def params(mib):
    return pltpu.CompilerParams(vmem_limit_bytes=mib << 20)


def shape(dims, kind):
    return jax.ShapeDtypeStruct(dims, kind)


def nn(a, b):
    return lax.dot_general(a, b, (((1,), (0,)), ((), ())), preferred_element_type=F32)


def nt(a, b):
    return lax.dot_general(a, b, (((1,), (1,)), ((), ())), preferred_element_type=F32)


def tn(a, b):
    return lax.dot_general(a, b, (((0,), (0,)), ((), ())), preferred_element_type=F32)


def rows(start, size):
    return pl.ds(pl.multiple_of(start, size), size)


def run_copies(copies):
    for c in copies:
        c.start()
    for c in copies:
        c.wait()


def select_kernel(meta, lay, grad, small, *refs):
    outs, sem = refs[:8], refs[8]
    copies = []
    for k in range(4):
        copies.append(pltpu.make_async_copy(lay.at[meta[k]], outs[k], sem.at[3 * k]))
        other = meta[4 + k]
        copies.append(
            pltpu.make_async_copy(grad.at[other], outs[4 + k].at[pl.ds(0, 128)], sem.at[3 * k + 1])
        )
        copies.append(
            pltpu.make_async_copy(
                small.at[other], outs[4 + k].at[pl.ds(128, 16)], sem.at[3 * k + 2]
            )
        )
    run_copies(copies)


def select_chunks(meta, lay, grad, small):
    return pl.pallas_call(
        select_kernel,
        out_shape=[shape((128, D), BF)] * 4 + [shape((144, D), BF)] * 4,
        in_specs=[SM, ANY, ANY, ANY],
        out_specs=[ANY] * 8,
        scratch_shapes=[pltpu.SemaphoreType.DMA((12,))],
        name="select_chunks",
    )(meta, lay, grad, small)


def load_weights(wag, w, sem, first):
    return [
        pltpu.make_async_copy(
            wag.at[pl.ds(160 * z, 128)], w.at[pl.ds(128 * z, 128)], sem.at[first + z]
        )
        for z in range(8)
    ]


def forward_kernel(meta, tb, *refs):
    xs, gs = refs[:8], refs[8:16]
    wag, wrecv = refs[16:18]
    normed, act, slope, probs, pslope, mixed, dz, stats, grad, srow = refs[18:28]
    x, w, wo, small, scol, sem = refs[28:]
    e, p, h = meta[0], meta[1], meta[2]
    copies = load_weights(wag, w, sem, 0)
    for k in range(8):
        half = h if k < 4 else 1 - h
        bx = half * 4 + jnp.bitwise_xor(e, k % 4)
        bg = half * 4 + jnp.bitwise_xor(p, k % 4)
        copies.append(pltpu.make_async_copy(xs[k], x.at[rows(bx * 128, 128)], sem.at[8 + k]))
        copies.append(
            pltpu.make_async_copy(
                gs[k].at[pl.ds(0, 128)], grad.at[rows(bg * 128, 128)], sem.at[16 + k]
            )
        )
        copies.append(
            pltpu.make_async_copy(
                gs[k].at[pl.ds(128, 16), pl.ds(0, 128)], small.at[bg], sem.at[24 + k]
            )
        )
    for q in range(4):
        for r in range(2):
            own = wag.at[
                pl.ds(pl.multiple_of((4 * h + q) * 160 + 128, 32), 32), pl.ds(512 * r, 512)
            ]
            other = wrecv.at[q, :, pl.ds(512 * r, 512)]
            to = pl.ds(64 * q + 32 * r, 32)
            copies.append(
                pltpu.make_async_copy(own, wo.at[to, rows(h * 512, 512)], sem.at[32 + 4 * q + r])
            )
            copies.append(
                pltpu.make_async_copy(
                    other, wo.at[to, rows((1 - h) * 512, 512)], sem.at[34 + 4 * q + r]
                )
            )
    run_copies(copies)

    def project(i, carry):
        at = rows(i * BQ, BQ)
        v = x[at, :].astype(F32)
        v = v - jnp.mean(v, axis=-1, keepdims=True)
        r = lax.rsqrt(jnp.mean(v * v, axis=-1, keepdims=True) + EPS)
        n = (v * r).astype(BF)
        normed[at, :] = n
        stats[at, :] = jnp.broadcast_to(r, (BQ, 128))
        for c in range(4):
            cols = pl.ds(256 * c, 256)
            hidden = nn(n, w[:, cols])
            sg = jax.nn.sigmoid(hidden)
            act[at, cols] = (hidden * sg).astype(BF)
            slope[at, cols] = (sg * (1.0 + hidden * (1.0 - sg))).astype(BF)
        return carry

    lax.fori_loop(0, NQ, project, 0)

    for b in range(8):
        tile = small[b].astype(F32)
        srow[0:8, pl.ds(128 * b, 128)] = tile[0:8]
        full = jnp.concatenate([tile, jnp.zeros((112, 128), F32)], axis=0)
        scol[pl.ds(128 * b, 128), :] = jnp.transpose(full)

    table = jnp.broadcast_to(tb[0:1, :], (BQ, 128))
    lane = lax.broadcasted_iota(jnp.int32, (BQ, 128), 1)
    causal = (
        lax.broadcasted_iota(jnp.int32, (BQ, BQ), 1)
        <= lax.broadcasted_iota(jnp.int32, (BQ, BQ), 0)
    )
    for i in range(NQ):
        at = pl.ds(i * BQ, BQ)
        q = (act[at, 512:768].astype(F32) * (DH**-0.5)).astype(BF)
        si = scol[at, 0:1]
        lv = scol[at, 1:2]
        for j in range(i + 1):
            cols = pl.ds(j * BQ, BQ)
            s = nt(q, act[cols, 768:1024])
            near = jnp.clip(si - srow[0:1, cols], 0.0, 127.0).astype(jnp.int32)
            bias = jnp.concatenate(
                [
                    jnp.take_along_axis(table, near[:, :128], axis=1, mode="promise_in_bounds"),
                    jnp.take_along_axis(table, near[:, 128:], axis=1, mode="promise_in_bounds"),
                ],
                axis=1,
            )
            s = s + bias
            sg = jax.nn.sigmoid(s)
            live = jnp.where(causal, lv, 0.0) if j == i else lv
            sg = sg * 1.0
            probs[at, cols] = (s * sg * live).astype(BF)
            pslope[at, cols] = (sg * (1.0 + s * (1.0 - sg)) * live).astype(BF)
        upto = (i + 1) * BQ
        mix = nn(probs[at, 0:upto], act[0:upto, 256:512])
        mixed[at, :] = mix
        d = nt(grad[at, :], wo[...])
        dz[at, :] = d
        gated = mix * act[at, 0:256].astype(F32)
        m = jnp.mean(gated, axis=-1, keepdims=True)
        centred = gated - m
        m2 = jnp.sum(centred * centred, axis=-1, keepdims=True)
        s3 = jnp.sum(d, axis=-1, keepdims=True)
        s4 = jnp.sum(d * centred, axis=-1, keepdims=True)
        row = stats[at, :]
        for n, value in enumerate((m, m2, s3, s4)):
            row = jnp.where(lane == n, value, row)
        row = jnp.where(lane == 5, si, row)
        stats[at, :] = row


def forward(meta, tb, xs, gs, wag, wrecv):
    return pl.pallas_call(
        forward_kernel,
        out_shape=[
            shape((L, D), BF),
            shape((L, D), BF),
            shape((L, D), BF),
            shape((L, L), BF),
            shape((L, L), BF),
            shape((L, DH), F32),
            shape((L, DH), F32),
            shape((L, 128), F32),
            shape((L, D), BF),
            shape((8, L), F32),
        ],
        in_specs=[SM, VM] + [ANY] * 18,
        out_specs=[VM] * 10,
        scratch_shapes=[
            pltpu.VMEM((L, D), BF),
            pltpu.VMEM((D, D), BF),
            pltpu.VMEM((DH, D), BF),
            pltpu.VMEM((8, 16, 128), BF),
            pltpu.VMEM((L, 128), F32),
            pltpu.SemaphoreType.DMA((48,)),
        ],
        compiler_params=params(48),
        name="forward",
    )(meta, tb, *xs, *gs, wag, wrecv)


def middle_kernel(meta, own, peer, mixed, dz, gate, gslope, grad, datt, dhu, keep, send, zl):
    h = meta[2]

    def step(i, carry):
        at = rows(i * BQ, BQ)
        a, b = own[at, :], peer[at, :]
        m0, m1 = a[:, 0:1], b[:, 0:1]
        mean = 0.5 * (m0 + m1)
        gap = m0 - mean
        r = lax.rsqrt((a[:, 1:2] + b[:, 1:2] + 512.0 * gap * gap) * (1.0 / 512.0) + EPS)
        dmean = (a[:, 2:3] + b[:, 2:3]) * (1.0 / 512.0)
        cross = a[:, 3:4] + b[:, 3:4] + gap * (a[:, 2:3] - b[:, 2:3])
        cross = cross * r * (1.0 / 512.0)
        mix = mixed[at, :]
        u = gate[at, :].astype(F32)
        zhat = (mix * u - mean) * r
        zl[at, :] = zhat.astype(BF)
        dgated = r * (dz[at, :] - dmean - zhat * cross)
        datt[at, :] = (dgated * u).astype(BF)
        dhu[at, :] = (dgated * mix * gslope[at, :].astype(F32)).astype(BF)
        return carry

    lax.fori_loop(0, NQ, step, 0)
    for half in range(2):
        po = tn(zl[...], grad[:, 512 * half : 512 * half + 512]).astype(BF)
        for q in range(4):
            block = jnp.concatenate(
                [po[64 * q : 64 * q + 32], po[64 * q + 32 : 64 * q + 64]], axis=1
            )

            @pl.when(h == half)
            def _(block=block, q=q):
                keep[q] = block

            @pl.when(h != half)
            def _(block=block, q=q):
                send[q] = block


def middle(meta, own, peer, mixed, dz, act, slope, grad):
    first = pl.BlockSpec((L, DH), lambda i: (0, 0))

    def whole(*dims):
        return pl.BlockSpec(dims, lambda i: (0,) * len(dims))

    return pl.pallas_call(
        middle_kernel,
        grid=(1,),
        out_shape=[
            shape((L, DH), BF),
            shape((L, DH), BF),
            shape((4, 32, D), BF),
            shape((4, 32, D), BF),
        ],
        in_specs=[SM, whole(L, 128), whole(L, 128), whole(L, DH), whole(L, DH), first, first, whole(L, D)],
        out_specs=[whole(L, DH), whole(L, DH), whole(4, 32, D), whole(4, 32, D)],
        scratch_shapes=[pltpu.VMEM((L, DH), BF)],
        compiler_params=params(48),
        name="middle",
    )(meta, own, peer, mixed, dz, act, slope, grad)


def backward_kernel(
    meta, act, slope, probs, pslope, datt, dhu, normed, stats, keep, recv, part, dhid, dlow, hot
):
    h = meta[2]
    stamp_lane = lax.broadcasted_iota(jnp.int32, (L, 256), 1).astype(F32)
    hot[...] = jnp.where(stats[:, 5:6] == stamp_lane, 1.0, 0.0).astype(BF)
    dhid[:, 0:256] = dhu[...]
    bucket = lax.broadcasted_iota(jnp.int32, (BQ, 128), 1)
    time = lax.broadcasted_iota(jnp.int32, (BQ, 256), 1)
    total = jnp.zeros((BQ, 128), F32)
    for i in range(NQ):
        at = pl.ds(i * BQ, BQ)
        upto = (i + 1) * BQ
        da = datt[at, :]
        for j in range(i + 1):
            cols = pl.ds(j * BQ, BQ)
            dp = nt(da, act[cols, 256:512])
            dlow[at, cols] = (dp * pslope[at, cols].astype(F32)).astype(BF)
        low = dlow[at, 0:upto]
        dq = nn(low, act[0:upto, 768:1024]) * (DH**-0.5)
        dhid[at, 512:768] = (dq * slope[at, 512:768].astype(F32)).astype(BF)
        by_time = nn(low, hot[0:upto, :])
        si = stats[at, 5:6].astype(jnp.int32)
        when = si - bucket
        index = jnp.bitwise_and(when, 127)
        early = jnp.take_along_axis(by_time[:, :128], index, axis=1, mode="promise_in_bounds")
        late = jnp.take_along_axis(by_time[:, 128:], index, axis=1, mode="promise_in_bounds")
        picked = jnp.where(when >= 128, late, jnp.where(when >= 0, early, 0.0))
        far = jnp.sum(jnp.where(time <= si - 127, by_time, 0.0), axis=-1, keepdims=True)
        total = total + jnp.where(bucket == 127, far, picked)
    for j in range(NQ):
        cols = pl.ds(j * BQ, BQ)
        frm = j * BQ
        dv = tn(probs[frm:, cols], datt[frm:, :])
        dhid[cols, 256:512] = (dv * slope[cols, 256:512].astype(F32)).astype(BF)
        dk = tn(dlow[frm:, cols], act[frm:, 512:768]) * (DH**-0.5)
        dhid[cols, 768:1024] = (dk * slope[cols, 768:1024].astype(F32)).astype(BF)
    for b in range(4):
        for c in range(4):
            cols = pl.ds(256 * c, 256)
            pin = tn(normed[:, 256 * b : 256 * b + 256], dhid[:, cols]).astype(BF)
            part[pl.ds(2 * b * SHARD, 128), cols] = pin[:128]
            part[pl.ds((2 * b + 1) * SHARD, 128), cols] = pin[128:]
    bias = jnp.sum(total, axis=0, keepdims=True)
    high = bias.astype(BF)
    low = (bias - high.astype(F32)).astype(BF)
    line = jnp.concatenate([high.astype(F32), low.astype(F32), jnp.zeros((1, 768), F32)], axis=1)
    line = jnp.where(
        lax.broadcasted_iota(jnp.int32, (16, D), 0) == 0, jnp.broadcast_to(line, (16, D)), 0.0
    ).astype(BF)
    for z in range(8):
        part[pl.ds(z * SHARD + 160, 16), :] = line
    for q in range(4):
        part[pl.ds(pl.multiple_of((4 * h + q) * SHARD + 128, 16), 32), :] = keep[q]
        part[pl.ds(pl.multiple_of((4 * (1 - h) + q) * SHARD + 128, 16), 32), :] = recv[q]


def backward(meta, act, slope, probs, pslope, datt, dhu, normed, stats, keep, recv):
    return pl.pallas_call(
        backward_kernel,
        out_shape=[shape((8 * SHARD, D), BF), shape((L, D), BF)],
        in_specs=[SM] + [VM] * 10,
        out_specs=[VM, VM],
        scratch_shapes=[pltpu.VMEM((L, L), BF), pltpu.VMEM((L, 256), BF)],
        compiler_params=params(48),
        name="backward",
    )(meta, act, slope, probs, pslope, datt, dhu, normed, stats, keep, recv)


def input_kernel(meta, dhid, normed, stats, wag, own, other, w, sem):
    h = meta[2]
    run_copies(load_weights(wag, w, sem, 0))
    for i in range(NQ):
        at = pl.ds(i * BQ, BQ)
        dn = nt(dhid[at, :], w[...])
        n = normed[at, :].astype(F32)
        r = stats[at, 4:5]
        mean = jnp.mean(dn, axis=-1, keepdims=True)
        cross = jnp.mean(dn * n, axis=-1, keepdims=True)
        res = (r * (dn - mean - n * cross)).astype(BF)
        to = pl.ds((i % 2) * BQ, BQ)

        @pl.when(h == i // 2)
        def _(res=res, to=to):
            own[to, :] = res

        @pl.when(h != i // 2)
        def _(res=res, to=to):
            other[to, :] = res


def input_grad(meta, dhid, normed, stats, wag):
    return pl.pallas_call(
        input_kernel,
        out_shape=[shape((512, D), BF)] * 2,
        in_specs=[SM] + [VM] * 3 + [ANY],
        out_specs=[VM, VM],
        scratch_shapes=[pltpu.VMEM((D, D), BF), pltpu.SemaphoreType.DMA((8,))],
        compiler_params=params(48),
        name="input_grad",
    )(meta, dhid, normed, stats, wag)


def add_kernel(meta, a, b, *outs):
    p = meta[1]
    for k in range(4):
        at = rows(jnp.bitwise_xor(p, k) * 128, 128)
        outs[k][...] = (a[at, :].astype(F32) + b[at, :].astype(F32)).astype(BF)


def add_halves(meta, a, b):
    return pl.pallas_call(
        add_kernel,
        out_shape=[shape((128, D), BF)] * 4,
        in_specs=[SM, VM, VM],
        out_specs=[VM] * 4,
        compiler_params=params(32),
        name="add_halves",
    )(meta, a, b)


def place_kernel(meta, *refs):
    chunks, out, sem = refs[:4], refs[4], refs[5]
    run_copies(
        [
            pltpu.make_async_copy(chunks[k], out.at[jnp.bitwise_xor(meta[3], k)], sem.at[k])
            for k in range(4)
        ]
    )


def place(meta, chunks):
    return pl.pallas_call(
        place_kernel,
        out_shape=shape((4, 128, D), BF),
        in_specs=[SM] + [ANY] * 4,
        out_specs=ANY,
        scratch_shapes=[pltpu.SemaphoreType.DMA((4,))],
        name="place",
    )(meta, *chunks)


def device(yh, core, yl, x):
    return ((yh * 2 + core) * 2 + yl) * 4 + x


def unit_device(e, p, half):
    ye, ce = e >> 1, e & 1
    yp, cp = p >> 1, p & 1
    return device(ye, half, yp, 2 * (ye ^ cp) + ce)


def input_pairs(k):
    pairs = []
    for p in range(4):
        for yl in range(2):
            for x in range(4):
                pairs.append((device(p >> 1, p & 1, yl, x), unit_device(x ^ k, p, yl)))
    return pairs


def grad_pairs(k):
    pairs = []
    for e in range(4):
        for yl in range(2):
            for x in range(4):
                pairs.append((device(e >> 1, e & 1, yl, x), unit_device(e, x ^ k, yl)))
    return pairs


def back_pairs(k):
    return [(b, a) for a, b in grad_pairs(k)]


def local(layer_in, repack_plan, lengths, stamps, w_in, w_out, time_bias, grad_out):
    yh, core, yl, x = (lax.axis_index(n).astype(jnp.int32) for n in PLANE)
    swap = functools.partial(lax.ppermute, axis_name="core", perm=[(0, 1), (1, 0)])
    first = core == 0
    unit_e = 2 * yh + jnp.bitwise_and(x, 1)
    unit_p = 2 * yl + jnp.bitwise_xor(lax.shift_right_logical(x, 1), yh)
    meta = jnp.stack([unit_e, unit_p, core, x])

    w5 = w_in.reshape(128, 4, 2, DH)
    w_half = jnp.where(first, w5[:, :, 0], w5[:, :, 1]).reshape(128, D)
    o_half = jnp.where(first, w_out[:, :512], w_out[:, 512:])
    o_half = jnp.concatenate([o_half[:32], o_half[32:]], axis=1)
    wag = lax.all_gather(jnp.concatenate([w_half, o_half], axis=0), "z", axis=0, tiled=True)
    w3 = wag.reshape(8, 160, D)
    wrecv = swap(jnp.where(first, w3[4:, 128:], w3[:4, 128:]))

    here = (yl * 4 + x) * 128 + lax.iota(jnp.int32, 128)
    alive = here[None, :] < lengths[:, None]
    small = jnp.stack([stamps.astype(BF), alive.astype(BF)], axis=1)
    small = jnp.pad(small, ((0, 0), (0, 14), (0, D - 128)))
    others = [jnp.bitwise_xor(x, k) for k in range(4)]
    slots = [
        sum(jnp.where(o == t, repack_plan[t], 0) for t in range(4)).astype(jnp.int32)
        for o in others
    ]
    chunks = select_chunks(jnp.stack(slots + others), layer_in, grad_out, small)
    xs = [lax.ppermute(chunks[k], PLANE, input_pairs(k)) for k in range(4)]
    gs = [lax.ppermute(chunks[4 + k], PLANE, grad_pairs(k)) for k in range(4)]
    xs = xs + [swap(c) for c in xs]
    gs = gs + [swap(c) for c in gs]
    tb = jnp.where(first, time_bias[0:1], time_bias[1:2]).astype(F32)

    normed, act, slope, probs, pslope, mixed, dz, stats, grad, _ = forward(
        meta, tb, xs, gs, wag, wrecv
    )
    datt, dhu, keep, send = middle(meta, stats, swap(stats), mixed, dz, act, slope, grad)
    part, dhid = backward(
        meta, act, slope, probs, pslope, datt, dhu, normed, stats, keep, swap(send)
    )
    mine = lax.psum_scatter(part, "z", scatter_dimension=0, tiled=True)
    own, other = input_grad(meta, dhid, normed, stats, wag)
    pieces = add_halves(meta, own, swap(other))
    back = [lax.ppermute(pieces[k], PLANE, back_pairs(k)) for k in range(4)]
    input_gradient = place(meta, back)

    def exchange(v):
        return lax.all_to_all(v, CHIPS, split_axis=0, concat_axis=0, tiled=True)

    spread = exchange(mine.reshape(16, SHARD // 16, D))
    summed = jnp.sum(spread.astype(F32), axis=0, keepdims=True).astype(BF)
    mine = exchange(jnp.broadcast_to(summed, (16, SHARD // 16, D))).reshape(SHARD, D)
    theirs = swap(mine)
    pair0 = jnp.where(first, mine, theirs).astype(F32) * (1.0 / 128.0)
    pair1 = jnp.where(first, theirs, mine).astype(F32) * (1.0 / 128.0)
    grad_w_in = jnp.stack(
        [pair0[:128].reshape(128, 4, DH), pair1[:128].reshape(128, 4, DH)], axis=2
    ).reshape(128, 2 * D)

    def unfold(v):
        return jnp.concatenate([v[128:160, :512], v[128:160, 512:]], axis=0)

    grad_w_out = jnp.concatenate([unfold(pair0), unfold(pair1)], axis=1)
    grad_bias = jnp.stack([v[160, :128] + v[160, 128:256] for v in (pair0, pair1)])
    return input_gradient, grad_w_in, grad_w_out, grad_bias


def solution(mesh):
    fine = Mesh(mesh.devices.reshape(2, 2, 2, 4, 8), ("yh", "core", "yl", "x", "z"))
    events = P(("yh", "core", "z"), ("yl", "x"), None)
    slots = P(("yh", "core", "z"))
    return jax.shard_map(
        local,
        mesh=fine,
        in_specs=(
            events,
            slots,
            slots,
            P(("yh", "core", "z"), ("yl", "x")),
            P("z", None),
            P("z", None),
            P(),
            events,
        ),
        out_specs=(events, P("z", None), P("z", None), P()),
        check_vma=False,
    )
```

time: 751 us -> 339 us (0.45)
  matrix products: 261 us -> 0 us
  waiting for transfers between devices: 233 us -> 52.8 us
  Pallas kernels: 0 us -> 142 us
  local copies, waits for them, and re-layouts: 90 us -> 13.9 us
  blocking collectives: 90.9 us -> 27.1 us
  starting transfers between devices: 7.19 us -> 70.4 us
  other arithmetic: 31 us -> 6.52 us
  loops' own time: 21.4 us -> 0 us
  between operations: 14.4 us -> 25.2 us
    dot_general x43 -> x0, matrix products: 261 us -> none  [the longest x16 119 us: bias_block(): jnp.einsum('sqkn,hn->shqk', one_hot(block_index), time_bias, preferred_el...]
    pallas_call x0 -> x7, Pallas kernels: none -> 142 us  [the longest x1 69.4 us: select_chunks(): pl.pallas_call(select_kernel, out_shape=[shape((128, D), BF)] * 4 + [shap...]
    psum x1 -> x0, waiting for transfers between devices: 107 us -> none  [local(): lax.psum(shard_in, ('dp', 'ctx')).astype(jnp.float32)]
    psum x1 -> x0, blocking collectives: 75.9 us -> none  [local(): summed_bias = lax.psum(bias_grad, ('dp', 'ctx', 'fsdp'))]
    ppermute x0 -> x25, starting transfers between devices: none -> 70.3 us  [the longest x4 22.1 us: local(): gs = [lax.ppermute(chunks[4 + k], PLANE, grad_pairs(k)) for k in range(4)]]
    reduce_scatter x3 -> x1, waiting for transfers between devices: 76.5 us -> 31.3 us  [local(): mine = lax.psum_scatter(part, 'z', scatter_dimension=0, tiled=True)]
    all_gather x4 -> x1, waiting for transfers between devices: 34.3 us -> 0.01 us  [local(): lax.all_gather(jnp.concatenate([w_half, o_half], axis=0), 'z', axis=0, ti...]
    all_to_all x0 -> x2, blocking collectives: none -> 27.1 us  [exchange(): return lax.all_to_all(v, CHIPS, split_axis=0, concat_axis=0, tiled=True)]
  transfers between devices with their start and end apart: 9 -> 27, of which waited for: 4 -> 10; matrix products, arithmetic and copies ran while one was open for 44% -> 1% of each run, Pallas kernels for 0% -> 33%
where the time goes in v1:
time: 339 us; the launch traced here: 338 us
  Pallas kernels  142 us (42%)
  starting transfers between devices  70.4 us (21%)
  waiting for transfers between devices  52.8 us (16%)
  blocking collectives  27.1 us (8%)
  between operations  25.2 us (7%)
  local copies, waits for them, and re-layouts  13.9 us (4%)
  other arithmetic  6.52 us (2%)
    pallas_call x1, Pallas kernels, select_chunks(): pl.pallas_call(select_kernel, out_shape=[shape((128, D), BF)] * 4 + [shap...  69.4 us
    pallas_call x1, Pallas kernels, place(): pl.pallas_call(place_kernel, out_shape=shape((4, 128, D), BF), in_specs=[...  33.6 us
    reduce_scatter x1, waiting for transfers between devices, local(): mine = lax.psum_scatter(part, 'z', scatter_dimension=0, tiled=True)  31.3 us
    all_to_all x2, blocking collectives, exchange(): return lax.all_to_all(v, CHIPS, split_axis=0, concat_axis=0, tiled=True)  27.1 us
    ppermute x4, starting transfers between devices, local(): gs = [lax.ppermute(chunks[4 + k], PLANE, grad_pairs(k)) for k in range(4)]  22.1 us
    ppermute x4, starting transfers between devices, local(): xs = [lax.ppermute(chunks[k], PLANE, input_pairs(k)) for k in range(4)]  20.5 us
    ppermute x4, waiting for transfers between devices, local(): back = [lax.ppermute(pieces[k], PLANE, back_pairs(k)) for k in range(4)]  14.5 us
    pallas_call x1, Pallas kernels, forward(): pl.pallas_call(forward_kernel, out_shape=[shape((L, D), BF), shape((L, D)...  13.9 us
  transfers between devices with their start and end apart: 27, of which 10 were waited for; matrix products, arithmetic and copies ran while one was open for 1% of the time, Pallas kernels for 33%

profile of v1, /device:TPU:1, one launch (start us, length us, event | category | flops | bytes accessed | tf_op | source)
XLA Modules:
  0.0 338.3 jit_solution(698979343209908665)
XLA Ops:
  7.2 0.9 slice_select_fusion.1
  8.1 1.4 reshape.78
  9.6 0.7 fusion.9
  10.3 0.2 copy_select_fusion
  10.6 0.8 maximum_maximum_fusion
  11.5 0.7 fusion.11
  22.8 0.7 stack.67.meta
  23.6 0.7 fusion.5.small
  24.3 69.4 %select_chunks.1 = (bf16[128,1024]{1,0:T(8,128)(2,1)}, bf16[128,1024]{1,0:T(8,128)(2,1)}, bf16[128,1024]{1,0:T(8,128)(2,1)}, bf16[128,1024]{1,0:T(8,128)(2,1)}, ...) custom-call(s32[8]{0:T(128)} %stack.67.meta, ...), custom_call_target="tpu_custom_call" | custom-call | tf_op jit(solution)/shard_map/select_chunks/pallas_call | solution.py:76
  93.6 15.7 %collective-permute-start = (bf16[128,1024]{1,0:T(8,128)(2,1)}, bf16[128,1024]{1,0:T(8,128)(2,1)S(1)}, u32[]{:S(2)}, u32[]{:S(2)}) collective-permute-start(bf16[128,1024]{1,0:T(8,128)(2,1)} %get-tuple-element.33), channel_id=1, source_target_pairs={{0,0},{8,8},{16,144},{24,152},{32,64},{40,72},{48,208},{56,216},{6... | collective-permute-start | bytes 786440 | tf_op jit(solution)/shard_map/ppermute | solution.py:496
  109.4 2.8 collective-permute-start.1
  112.2 1.9 collective-permute-start.2
  114.1 3.9 %collective-permute-start.8 = (bf16[144,1024]{1,0:T(8,128)(2,1)}, bf16[144,1024]{1,0:T(8,128)(2,1)S(1)}, u32[]{:S(2)}, u32[]{:S(2)}) collective-permute-start(bf16[144,1024]{1,0:T(8,128)(2,1)} %get-tuple-element.37), channel_id=1, source_target_pairs={{0,0},{8,16},{16,32},{24,48},{32,64},{40,80},{48,96},{56,112},{64,... | collective-permute-start | bytes 884744 | tf_op jit(solution)/shard_map/ppermute | solution.py:497
  118.0 4.7 %collective-permute-start.9 = (bf16[144,1024]{1,0:T(8,128)(2,1)}, bf16[144,1024]{1,0:T(8,128)(2,1)S(1)}, u32[]{:S(2)}, u32[]{:S(2)}) collective-permute-start(bf16[144,1024]{1,0:T(8,128)(2,1)} %get-tuple-element.38), channel_id=1, source_target_pairs={{0,16},{8,0},{16,48},{24,32},{32,80},{40,64},{48,112},{56,96},{64,... | collective-permute-start | bytes 884744 | tf_op jit(solution)/shard_map/ppermute | solution.py:497
  122.6 8.6 %collective-permute-start.10 = (bf16[144,1024]{1,0:T(8,128)(2,1)}, bf16[144,1024]{1,0:T(8,128)(2,1)S(1)}, u32[]{:S(2)}, u32[]{:S(2)}) collective-permute-start(bf16[144,1024]{1,0:T(8,128)(2,1)} %get-tuple-element.39), channel_id=1, source_target_pairs={{0,32},{8,48},{16,0},{24,16},{32,96},{40,112},{48,64},{56,80},{64,... | collective-permute-start | bytes 884744 | tf_op jit(solution)/shard_map/ppermute | solution.py:497
  131.4 0.8 collective-permute-done.2.refs_2_
  132.2 4.9 %collective-permute-start.11 = (bf16[144,1024]{1,0:T(8,128)(2,1)}, bf16[144,1024]{1,0:T(8,128)(2,1)S(1)}, u32[]{:S(2)}, u32[]{:S(2)}) collective-permute-start(bf16[144,1024]{1,0:T(8,128)(2,1)} %get-tuple-element.40), channel_id=1, source_target_pairs={{0,48},{8,32},{16,16},{24,0},{32,112},{40,96},{48,80},{56,64},{64,... | collective-permute-start | bytes 884744 | tf_op jit(solution)/shard_map/ppermute | solution.py:497
  137.1 2.4 collective-permute-done.3.refs_3_
  139.5 3.0 collective-permute-start.4
  142.6 0.5 collective-permute-start.6
  143.2 1.1 slice_select_fusion
  144.2 2.0 collective-permute-start.12
  146.3 0.5 collective-permute-start.14
  146.9 0.7 copy-done.4
  147.6 0.4 collective-permute-start.16
  148.1 0.2 collective-permute-done.14.refs_14_
  148.3 0.4 collective-permute-done.15.refs_15_
  148.7 0.4 collective-permute-done.16.refs_17_
  149.2 0.9 copy-done.5
  150.1 13.9 %forward.1 = (bf16[1024,1024]{1,0:T(8,128)(2,1)}, bf16[1024,1024]{1,0:T(8,128)(2,1)}, bf16[1024,1024]{1,0:T(8,128)(2,1)}, bf16[1024,1024]{1,0:T(8,128)(2,1)}, bf...) custom-call(s32[4]{0:T(128)S(1)} %pad_add_fusion.meta, ...), custom_call_target="tpu_custom_call" | custom-call | tf_op jit(solution)/shard_map/forward/pallas_call | solution.py:205
  164.0 0.5 collective-permute-start.17
  164.5 1.5 collective-permute-done.17.peer
  166.0 1.2 copy-done
  167.3 1.2 copy-done.1
  168.5 4.8 %middle.1 = (bf16[1024,256]{1,0:T(8,128)(2,1)S(1)}, bf16[1024,256]{1,0:T(8,128)(2,1)S(1)}, bf16[4,32,1024]{2,1,0:T(8,128)(2,1)S(1)}, bf16[4,32,1024]{2,1,0:T(8,128)(2,1)S(1)}) custom-call(s32[4]{0:T(128)S(1)} %pad_add_fusion.meta, f32[1024,128]{1,0:T(8,128)S(1)} %get-tuple-element.45.own.stats, f32[1024,128]{1,0:T(8,128)S(1)} %collective-permute-done.17.peer, ...), custom_call_target="tpu_custom_call" | custom-call | tf_op jit(solution)/shard_map/middle/pallas_call | solution.py:279
  173.3 0.7 collective-permute-start.18
  174.0 1.2 collective-permute-done.18.recv
  175.1 11.6 %backward.1 = (bf16[1408,1024]{1,0:T(8,128)(2,1)}, bf16[1024,1024]{1,0:T(8,128)(2,1)S(1)}) custom-call(s32[4]{0:T(128)S(1)} %pad_add_fusion.meta, bf16[1024,1024]{1,0:T(8,128)(2,1)} %get-tuple-element.41.gate.act, bf16[1024,1024]{1,0:T(8,128)(2,1)} %get-tuple-element.42.gslope.slope, bf16[1024,1024]{1,0:T(8,128)(2,1)} %get-tuple-element.43.probs, ...), custom_call_target="tpu_custom_call" | custom-call | tf_op jit(solution)/shard_map/backward/pallas_call | solution.py:354
  186.8 8.3 %input_grad.1 = (bf16[512,1024]{1,0:T(8,128)(2,1)S(1)}, bf16[512,1024]{1,0:T(8,128)(2,1)}) custom-call(s32[4]{0:T(128)S(1)} %pad_add_fusion.meta, bf16[1024,1024]{1,0:T(8,128)(2,1)S(1)} %get-tuple-element.54.dhid, bf16[1024,1024]{1,0:T(8,128)(2,1)} %get-tuple-element.51.normed, f32[1024,128]{1,0:T(8,128)S(1)} %get-tuple-element.45.own.stats, ...), custom_call_target="tpu_custom_call" | custom-call | tf_op jit(solution)/shard_map/input_grad/pallas_call | solution.py:388
  195.1 1.0 copy-done.2
  196.1 0.4 collective-permute-start.19
  196.4 31.3 %reduce-scatter.2.cloned.1.call-done = bf16[176,1024]{1,0:T(8,128)(2,1)} async-done(((bf16[1408,1024]{1,0:T(8,128)(2,1)}), bf16[176,1024]{1,0:T(8,128)(2,1)}) %reduce-scatter.2.cloned.1.call-update) | async-done | bytes 360464 | tf_op jit(solution)/shard_map/reduce_scatter | solution.py:509
  227.7 1.1 reshape.80
  228.9 15.4 %all_to_all.10 = bf16[16,11,1024]{2,1,0:T(8,128)(2,1)S(1)} all-to-all(bf16[16,11,1024]{2,1,0:T(8,128)(2,1)S(1)} %reshape.80), channel_id=1, replica_groups=mesh['yh'=2,'core'=2,'yl'=2,'x'=4,'z'=8] {'yh','yl','x'}, dimensions={0} | all-to-all | bytes 720896 | tf_op jit(solution)/shard_map/all_to_all | solution.py:516
  244.5 11.7 %all_to_all.11 = bf16[16,11,1024]{2,1,0:T(8,128)(2,1)S(1)} all-to-all(bf16[16,11,1024]{2,1,0:T(8,128)(2,1)S(1)} %broadcast_in_dim.2), channel_id=1, replica_groups=mesh['yh'=2,'core'=2,'yl'=2,'x'=4,'z'=8] {'yh','yl','x'}, dimensions={0} | all-to-all | bytes 720896 | tf_op jit(solution)/shard_map/all_to_all | solution.py:516
  256.1 0.1 reshape.81
  256.3 7.4 %collective-permute-start.24 = (bf16[176,1024]{1,0:T(8,128)(2,1)S(1)}, bf16[176,1024]{1,0:T(8,128)(2,1)}, u32[]{:S(2)}, u32[]{:S(2)}) collective-permute-start(bf16[176,1024]{1,0:T(8,128)(2,1)S(1)} %reshape.81), channel_id=1, source_target_pairs={{0,64},{64,0},{1,65},{65,1},{2,66},{66,2},{3,67},{67,3},{4,68},{68... | collective-permute-start | bytes 1081352 | tf_op jit(solution)/shard_map/ppermute | solution.py:521
  263.7 0.8 add_halves.1
  264.5 1.9 collective-permute-start.20
  266.4 3.3 collective-permute-start.21
  269.7 4.3 %collective-permute-start.22 = (bf16[128,1024]{1,0:T(8,128)(2,1)S(1)}, bf16[128,1024]{1,0:T(8,128)(2,1)S(1)}, u32[]{:S(2)}, u32[]{:S(2)}) collective-permute-start(bf16[128,1024]{1,0:T(8,128)(2,1)S(1)} %get-tuple-element.59), channel_id=1, source_target_pairs={{32,0},{48,8},{0,16},{16,24},{96,32},{112,40},{64,48},{80,56},{40,... | collective-permute-start | bytes 786440 | tf_op jit(solution)/shard_map/ppermute | solution.py:512
  273.9 2.7 collective-permute-start.23
  276.7 6.6 %collective-permute-done.21.refs_1_ = bf16[128,1024]{1,0:T(8,128)(2,1)S(1)} collective-permute-done((bf16[128,1024]{1,0:T(8,128)(2,1)S(1)}, bf16[128,1024]{1,0:T(8,128)(2,1)S(1)}, u32[]{:S(2)}, u32[]{:S(2)}) %collective-permute-start.21) | collective-permute-done | bytes 262176 | tf_op jit(solution)/shard_map/ppermute | solution.py:512
  283.3 7.9 %collective-permute-done.23.refs_3_ = bf16[128,1024]{1,0:T(8,128)(2,1)S(1)} collective-permute-done((bf16[128,1024]{1,0:T(8,128)(2,1)S(1)}, bf16[128,1024]{1,0:T(8,128)(2,1)S(1)}, u32[]{:S(2)}, u32[]{:S(2)}) %collective-permute-start.23) | collective-permute-done | bytes 262176 | tf_op jit(solution)/shard_map/ppermute | solution.py:512
  291.2 0.7 copy-done.10
  291.9 33.6 %place.1 = bf16[4,128,1024]{2,1,0:T(8,128)(2,1)} custom-call(s32[4]{0:T(128)} %copy-done.6, bf16[128,1024]{1,0:T(8,128)(2,1)} %copy-done.7, bf16[128,1024]{1,0:T(8,128)(2,1)} %copy-done.8, bf16[128,1024]{1,0:T(8,128)(2,1)} %copy-done.9, bf16[128,1024]{1,0:T(8,128)(2,1)} %copy-done.10), custom_call_target="tpu_custom_call" | custom-call | tf_op jit(solution)/shard_map/place/pallas_call | solution.py:428
  325.5 1.2 convert_multiply_fusion.1
  326.8 0.2 stack_reshape.6
  327.1 0.2 stack_reshape.7
  327.3 0.2 pad_maximum_fusion
  327.6 0.8 copy.23
  328.4 1.8 reshape.82
  330.2 0.6 pad_maximum_fusion.1
  330.8 0.7 maximum_maximum_fusion.1
  (65 shorter events, 1.0 us)
Async XLA Ops:
  7.2 136.0 %all-gather.2.cloned.1.call-start = ((), (), s32[]{:S(2)}) async-start(), calls=%async_computation.3 | async-start | bytes 2949120 | tf_op jit(solution)/shard_map/all_gather | solution.py:482
  9.5 1.9 copy-start.12
  9.6 1.9 copy-start.11
  9.6 13.9 %copy-start.14 = (s32[4]{0:T(128)S(1)}, s32[4]{0:T(128)}, u32[]{:S(2)}) copy-start(s32[4]{0:T(128)} %param.10) | copy-start | bytes 52
  10.6 137.5 %copy-start.13 = (bf16[2,128]{1,0:T(2,128)(2,1)S(1)}, bf16[2,128]{1,0:T(2,128)(2,1)}, u32[]{:S(2)}) copy-start(bf16[2,128]{1,0:T(2,128)(2,1)} %param.14) | copy-start | bytes 1540
  11.4 216.4 %reduce-scatter.2.cloned.1.call-start = ((), (), s32[]{:S(2)}) async-start(), calls=%async_computation.4 | async-start | bytes 3244032 | tf_op jit(solution)/shard_map/reduce_scatter | solution.py:509
  93.6 29.0 %collective-permute-start = (bf16[128,1024]{1,0:T(8,128)(2,1)}, bf16[128,1024]{1,0:T(8,128)(2,1)S(1)}, u32[]{:S(2)}, u32[]{:S(2)}) collective-permute-start(bf16[128,1024]{1,0:T(8,128)(2,1)} %get-tuple-element.33), channel_id=1, source_target_pairs={{0,0},{8,8},{16,144},{24,152},{32,64},{40,72},{48,208},{56,216},{6... | collective-permute-start | bytes 786440 | tf_op jit(solution)/shard_map/ppermute | solution.py:496
  109.4 21.9 %collective-permute-start.1 = (bf16[128,1024]{1,0:T(8,128)(2,1)}, bf16[128,1024]{1,0:T(8,128)(2,1)S(1)}, u32[]{:S(2)}, u32[]{:S(2)}) collective-permute-start(bf16[128,1024]{1,0:T(8,128)(2,1)} %get-tuple-element.34), channel_id=1, source_target_pairs={{0,8},{8,0},{16,152},{24,144},{32,72},{40,64},{48,216},{56,208},{6... | collective-permute-start | bytes 786440 | tf_op jit(solution)/shard_map/ppermute | solution.py:496
  112.2 20.1 %collective-permute-start.2 = (bf16[128,1024]{1,0:T(8,128)(2,1)}, bf16[128,1024]{1,0:T(8,128)(2,1)S(1)}, u32[]{:S(2)}, u32[]{:S(2)}) collective-permute-start(bf16[128,1024]{1,0:T(8,128)(2,1)} %get-tuple-element.35), channel_id=1, source_target_pairs={{0,144},{8,152},{16,0},{24,8},{32,208},{40,216},{48,64},{56,72},{6... | collective-permute-start | bytes 786440 | tf_op jit(solution)/shard_map/ppermute | solution.py:496
  114.1 28.5 %collective-permute-start.8 = (bf16[144,1024]{1,0:T(8,128)(2,1)}, bf16[144,1024]{1,0:T(8,128)(2,1)S(1)}, u32[]{:S(2)}, u32[]{:S(2)}) collective-permute-start(bf16[144,1024]{1,0:T(8,128)(2,1)} %get-tuple-element.37), channel_id=1, source_target_pairs={{0,0},{8,16},{16,32},{24,48},{32,64},{40,80},{48,96},{56,112},{64,... | collective-permute-start | bytes 884744 | tf_op jit(solution)/shard_map/ppermute | solution.py:497
  118.0 24.6 %collective-permute-start.9 = (bf16[144,1024]{1,0:T(8,128)(2,1)}, bf16[144,1024]{1,0:T(8,128)(2,1)S(1)}, u32[]{:S(2)}, u32[]{:S(2)}) collective-permute-start(bf16[144,1024]{1,0:T(8,128)(2,1)} %get-tuple-element.38), channel_id=1, source_target_pairs={{0,16},{8,0},{16,48},{24,32},{32,80},{40,64},{48,112},{56,96},{64,... | collective-permute-start | bytes 884744 | tf_op jit(solution)/shard_map/ppermute | solution.py:497
  122.6 20.4 %collective-permute-start.10 = (bf16[144,1024]{1,0:T(8,128)(2,1)}, bf16[144,1024]{1,0:T(8,128)(2,1)S(1)}, u32[]{:S(2)}, u32[]{:S(2)}) collective-permute-start(bf16[144,1024]{1,0:T(8,128)(2,1)} %get-tuple-element.39), channel_id=1, source_target_pairs={{0,32},{8,48},{16,0},{24,16},{32,96},{40,112},{48,64},{56,80},{64,... | collective-permute-start | bytes 884744 | tf_op jit(solution)/shard_map/ppermute | solution.py:497
  131.3 8.2 %collective-permute-start.3 = (bf16[128,1024]{1,0:T(8,128)(2,1)}, bf16[128,1024]{1,0:T(8,128)(2,1)S(1)}, u32[]{:S(2)}, u32[]{:S(2)}) collective-permute-start(bf16[128,1024]{1,0:T(8,128)(2,1)} %get-tuple-element.36), channel_id=1, source_target_pairs={{0,152},{8,144},{16,8},{24,0},{32,216},{40,208},{48,72},{56,64},{6... | collective-permute-start | bytes 786440 | tf_op jit(solution)/shard_map/ppermute | solution.py:496
  132.2 12.0 %collective-permute-start.11 = (bf16[144,1024]{1,0:T(8,128)(2,1)}, bf16[144,1024]{1,0:T(8,128)(2,1)S(1)}, u32[]{:S(2)}, u32[]{:S(2)}) collective-permute-start(bf16[144,1024]{1,0:T(8,128)(2,1)} %get-tuple-element.40), channel_id=1, source_target_pairs={{0,48},{8,32},{16,16},{24,0},{32,112},{40,96},{48,80},{56,64},{64,... | collective-permute-start | bytes 884744 | tf_op jit(solution)/shard_map/ppermute | solution.py:497
  139.5 6.8 %collective-permute-start.4 = (bf16[128,1024]{1,0:T(8,128)(2,1)S(1)}, bf16[128,1024]{1,0:T(8,128)(2,1)S(1)}, u32[]{:S(2)}, u32[]{:S(2)}) collective-permute-start(bf16[128,1024]{1,0:T(8,128)(2,1)S(1)} %collective-permute-done.refs_0_), channel_id=1, source_target_pairs={{0,64},{64,0},{1,65},{65,1},{2,66},{66,2},{3,67},{67,3},{4,68},{68... | collective-permute-start | bytes 786440 | tf_op jit(solution)/shard_map/ppermute | solution.py:498
  142.6 3.7 %collective-permute-start.5 = (bf16[128,1024]{1,0:T(8,128)(2,1)S(1)}, bf16[128,1024]{1,0:T(8,128)(2,1)S(1)}, u32[]{:S(2)}, u32[]{:S(2)}) collective-permute-start(bf16[128,1024]{1,0:T(8,128)(2,1)S(1)} %collective-permute-done.1.refs_1_), channel_id=1, source_target_pairs={{0,64},{64,0},{1,65},{65,1},{2,66},{66,2},{3,67},{67,3},{4,68},{68... | collective-permute-start | bytes 786440 | tf_op jit(solution)/shard_map/ppermute | solution.py:498
  142.6 4.2 %collective-permute-start.6 = (bf16[128,1024]{1,0:T(8,128)(2,1)S(1)}, bf16[128,1024]{1,0:T(8,128)(2,1)S(1)}, u32[]{:S(2)}, u32[]{:S(2)}) collective-permute-start(bf16[128,1024]{1,0:T(8,128)(2,1)S(1)} %collective-permute-done.2.refs_2_), channel_id=1, source_target_pairs={{0,64},{64,0},{1,65},{65,1},{2,66},{66,2},{3,67},{67,3},{4,68},{68... | collective-permute-start | bytes 786440 | tf_op jit(solution)/shard_map/ppermute | solution.py:498
  143.1 3.8 %collective-permute-start.7 = (bf16[128,1024]{1,0:T(8,128)(2,1)S(1)}, bf16[128,1024]{1,0:T(8,128)(2,1)S(1)}, u32[]{:S(2)}, u32[]{:S(2)}) collective-permute-start(bf16[128,1024]{1,0:T(8,128)(2,1)S(1)} %collective-permute-done.3.refs_3_), channel_id=1, source_target_pairs={{0,64},{64,0},{1,65},{65,1},{2,66},{66,2},{3,67},{67,3},{4,68},{68... | collective-permute-start | bytes 786440 | tf_op jit(solution)/shard_map/ppermute | solution.py:498
  144.2 3.8 %collective-permute-start.12 = (bf16[144,1024]{1,0:T(8,128)(2,1)S(1)}, bf16[144,1024]{1,0:T(8,128)(2,1)S(1)}, u32[]{:S(2)}, u32[]{:S(2)}) collective-permute-start(bf16[144,1024]{1,0:T(8,128)(2,1)S(1)} %collective-permute-done.8.refs_8_), channel_id=1, source_target_pairs={{0,64},{64,0},{1,65},{65,1},{2,66},{66,2},{3,67},{67,3},{4,68},{68... | collective-permute-start | bytes 884744 | tf_op jit(solution)/shard_map/ppermute | solution.py:499
  146.3 1.8 collective-permute-start.13
  146.3 2.0 collective-permute-start.14
  146.8 2.0 collective-permute-start.15
  146.9 0.7 copy-start.4
  147.6 1.6 collective-permute-start.16
  148.1 115.6 %copy-start.6 = (s32[4]{0:T(128)}, s32[4]{0:T(128)S(1)}, u32[]{:S(2)}) copy-start(s32[4]{0:T(128)S(1)} %pad_add_fusion.meta) | copy-start | bytes 52
  149.2 0.9 copy-start.5
  164.0 2.0 collective-permute-start.17
  166.0 1.2 copy-start
  167.3 1.2 copy-start.1
  173.3 1.8 collective-permute-start.18
  195.1 1.0 copy-start.2
  196.1 67.6 %collective-permute-start.19 = (bf16[512,1024]{1,0:T(8,128)(2,1)}, bf16[512,1024]{1,0:T(8,128)(2,1)S(1)}, u32[]{:S(2)}, u32[]{:S(2)}) collective-permute-start(bf16[512,1024]{1,0:T(8,128)(2,1)} %get-tuple-element.56), channel_id=1, source_target_pairs={{0,64},{64,0},{1,65},{65,1},{2,66},{66,2},{3,67},{67,3},{4,68},{68... | collective-permute-start | bytes 3145736 | tf_op jit(solution)/shard_map/ppermute | solution.py:511
  228.9 34.8 %copy-start.3 = (bf16[512,1024]{1,0:T(8,128)(2,1)S(1)}, bf16[512,1024]{1,0:T(8,128)(2,1)}, u32[]{:S(2)}) copy-start(bf16[512,1024]{1,0:T(8,128)(2,1)} %copy-done.2) | copy-start | bytes 3145732
  256.3 69.2 %collective-permute-start.24 = (bf16[176,1024]{1,0:T(8,128)(2,1)S(1)}, bf16[176,1024]{1,0:T(8,128)(2,1)}, u32[]{:S(2)}, u32[]{:S(2)}) collective-permute-start(bf16[176,1024]{1,0:T(8,128)(2,1)S(1)} %reshape.81), channel_id=1, source_target_pairs={{0,64},{64,0},{1,65},{65,1},{2,66},{66,2},{3,67},{67,3},{4,68},{68... | collective-permute-start | bytes 1081352 | tf_op jit(solution)/shard_map/ppermute | solution.py:521
  264.5 12.2 %collective-permute-start.20 = (bf16[128,1024]{1,0:T(8,128)(2,1)S(1)}, bf16[128,1024]{1,0:T(8,128)(2,1)S(1)}, u32[]{:S(2)}, u32[]{:S(2)}) collective-permute-start(bf16[128,1024]{1,0:T(8,128)(2,1)S(1)} %get-tuple-element.57), channel_id=1, source_target_pairs={{0,0},{16,8},{32,16},{48,24},{64,32},{80,40},{96,48},{112,56},{8,6... | collective-permute-start | bytes 786440 | tf_op jit(solution)/shard_map/ppermute | solution.py:512
  266.4 16.9 %collective-permute-start.21 = (bf16[128,1024]{1,0:T(8,128)(2,1)S(1)}, bf16[128,1024]{1,0:T(8,128)(2,1)S(1)}, u32[]{:S(2)}, u32[]{:S(2)}) collective-permute-start(bf16[128,1024]{1,0:T(8,128)(2,1)S(1)} %get-tuple-element.58), channel_id=1, source_target_pairs={{16,0},{0,8},{48,16},{32,24},{80,32},{64,40},{112,48},{96,56},{24,... | collective-permute-start | bytes 786440 | tf_op jit(solution)/shard_map/ppermute | solution.py:512
  269.7 13.6 %collective-permute-start.22 = (bf16[128,1024]{1,0:T(8,128)(2,1)S(1)}, bf16[128,1024]{1,0:T(8,128)(2,1)S(1)}, u32[]{:S(2)}, u32[]{:S(2)}) collective-permute-start(bf16[128,1024]{1,0:T(8,128)(2,1)S(1)} %get-tuple-element.59), channel_id=1, source_target_pairs={{32,0},{48,8},{0,16},{16,24},{96,32},{112,40},{64,48},{80,56},{40,... | collective-permute-start | bytes 786440 | tf_op jit(solution)/shard_map/ppermute | solution.py:512
  273.9 17.3 %collective-permute-start.23 = (bf16[128,1024]{1,0:T(8,128)(2,1)S(1)}, bf16[128,1024]{1,0:T(8,128)(2,1)S(1)}, u32[]{:S(2)}, u32[]{:S(2)}) collective-permute-start(bf16[128,1024]{1,0:T(8,128)(2,1)S(1)} %get-tuple-element.60), channel_id=1, source_target_pairs={{48,0},{32,8},{16,16},{0,24},{112,32},{96,40},{80,48},{64,56},{56,... | collective-permute-start | bytes 786440 | tf_op jit(solution)/shard_map/ppermute | solution.py:512
  276.7 14.5 %copy-start.7 = (bf16[128,1024]{1,0:T(8,128)(2,1)}, bf16[128,1024]{1,0:T(8,128)(2,1)S(1)}, u32[]{:S(2)}) copy-start(bf16[128,1024]{1,0:T(8,128)(2,1)S(1)} %collective-permute-done.20.refs_0_) | copy-start | bytes 786436
  283.3 7.9 %copy-start.8 = (bf16[128,1024]{1,0:T(8,128)(2,1)}, bf16[128,1024]{1,0:T(8,128)(2,1)S(1)}, u32[]{:S(2)}) copy-start(bf16[128,1024]{1,0:T(8,128)(2,1)S(1)} %collective-permute-done.21.refs_1_) | copy-start | bytes 786436
  283.3 7.9 %copy-start.9 = (bf16[128,1024]{1,0:T(8,128)(2,1)}, bf16[128,1024]{1,0:T(8,128)(2,1)S(1)}, u32[]{:S(2)}) copy-start(bf16[128,1024]{1,0:T(8,128)(2,1)S(1)} %collective-permute-done.22.refs_2_) | copy-start | bytes 786436
  291.2 0.7 copy-start.10
Sparse Core Ops, SparseCore 0:
  11.5 92.2 all-gather.1
  186.9 40.7 reduce-scatter.1

commit v2 on v1

--- a/solution.py
+++ b/solution.py
@@ -77,8 +77,9 @@
         select_kernel,
         out_shape=[shape((128, D), BF)] * 4 + [shape((144, D), BF)] * 4,
         in_specs=[SM, ANY, ANY, ANY],
-        out_specs=[ANY] * 8,
+        out_specs=[VM] * 8,
         scratch_shapes=[pltpu.SemaphoreType.DMA((12,))],
+        compiler_params=params(32),
         name="select_chunks",
     )(meta, lay, grad, small)
 
@@ -429,8 +430,9 @@
         place_kernel,
         out_shape=shape((4, 128, D), BF),
         in_specs=[SM] + [ANY] * 4,
-        out_specs=ANY,
+        out_specs=VM,
         scratch_shapes=[pltpu.SemaphoreType.DMA((4,))],
+        compiler_params=params(32),
         name="place",
     )(meta, *chunks)
 
@@ -511,6 +513,7 @@
     pieces = add_halves(meta, own, swap(other))
     back = [lax.ppermute(pieces[k], PLANE, back_pairs(k)) for k in range(4)]
     input_gradient = place(meta, back)
+    mine = lax.optimization_barrier((mine, *back))[0]
 
     def exchange(v):
         return lax.all_to_all(v, CHIPS, split_axis=0, concat_axis=0, tiled=True)

time: 339 us -> 200 us (0.59)
  Pallas kernels: 142 us -> 42.1 us
  waiting for transfers between devices: 52.8 us -> 25.8 us
  starting transfers between devices: 70.4 us -> 62.8 us
    pallas_call x1, Pallas kernels: 69.4 us -> 1.72 us  [select_chunks(): pl.pallas_call(select_kernel, out_shape=[shape((128, D), BF)] * 4 + [shap...]
    pallas_call x1, Pallas kernels: 33.6 us -> 1.63 us  [place(): pl.pallas_call(place_kernel, out_shape=shape((4, 128, D), BF), in_specs=[...]
    reduce_scatter x1, waiting for transfers between devices: 31.3 us -> 4.2 us  [local(): mine = lax.psum_scatter(part, 'z', scatter_dimension=0, tiled=True)]
    ppermute x4, starting transfers between devices: 20.5 us -> 11.1 us  [local(): xs = [lax.ppermute(chunks[k], PLANE, input_pairs(k)) for k in range(4)]]
  transfers between devices with their start and end apart: 27 -> 27, of which waited for: 10 -> 13; matrix products, arithmetic and copies ran while one was open for 1% -> 1% of each run, Pallas kernels for 33% -> 6%
where the time goes in v2:
time: 200 us; the launch traced here: 199 us
  starting transfers between devices  62.8 us (31%)
  Pallas kernels  42.1 us (21%)
  blocking collectives  27 us (14%)
  waiting for transfers between devices  25.8 us (13%)
  between operations  24.7 us (12%)
  local copies, waits for them, and re-layouts  11.6 us (6%)
  other arithmetic  4.89 us (2%)
    all_to_all x2, blocking collectives, exchange(): return lax.all_to_all(v, CHIPS, split_axis=0, concat_axis=0, tiled=True)  27 us
    ppermute x4, starting transfers between devices, local(): gs = [lax.ppermute(chunks[4 + k], PLANE, grad_pairs(k)) for k in range(4)]  22 us
    ppermute x4, starting transfers between devices, local(): back = [lax.ppermute(pieces[k], PLANE, back_pairs(k)) for k in range(4)]  14.4 us
    pallas_call x1, Pallas kernels, forward(): pl.pallas_call(forward_kernel, out_shape=[shape((L, D), BF), shape((L, D)...  13.9 us
    ppermute x4, waiting for transfers between devices, local(): back = [lax.ppermute(pieces[k], PLANE, back_pairs(k)) for k in range(4)]  12.6 us
    pallas_call x1, Pallas kernels, backward(): pl.pallas_call(backward_kernel, out_shape=[shape((8 * SHARD, D), BF), sha...  11.8 us
    ppermute x4, starting transfers between devices, local(): xs = [lax.ppermute(chunks[k], PLANE, input_pairs(k)) for k in range(4)]  11.1 us
    ppermute x1, starting transfers between devices, local(): theirs = swap(mine)  7.49 us
  transfers between devices with their start and end apart: 27, of which 13 were waited for; matrix products, arithmetic and copies ran while one was open for 1% of the time, Pallas kernels for 6%

profile of v2, /device:TPU:1, one launch (start us, length us, event | category | flops | bytes accessed | tf_op | source)
XLA Modules:
  0.0 198.9 jit_solution(4093874274995656907)
XLA Ops:
  7.2 0.9 slice_select_fusion.1
  8.1 1.4 reshape.78
  9.6 0.7 fusion.9
  10.3 0.2 copy_select_fusion
  10.6 0.8 maximum_maximum_fusion
  11.5 0.6 fusion.11
  22.6 1.7 select_chunks.1
  24.3 6.0 %collective-permute-start = (bf16[128,1024]{1,0:T(8,128)(2,1)S(1)}, bf16[128,1024]{1,0:T(8,128)(2,1)S(1)}, u32[]{:S(2)}, u32[]{:S(2)}) collective-permute-start(bf16[128,1024]{1,0:T(8,128)(2,1)S(1)} %get-tuple-element.34), channel_id=1, source_target_pairs={{0,0},{8,8},{16,144},{24,152},{32,64},{40,72},{48,208},{56,216},{6... | collective-permute-start | bytes 786440 | tf_op jit(solution)/shard_map/ppermute | solution.py:498
  30.4 3.0 %collective-permute-start.1 = (bf16[128,1024]{1,0:T(8,128)(2,1)S(1)}, bf16[128,1024]{1,0:T(8,128)(2,1)S(1)}, u32[]{:S(2)}, u32[]{:S(2)}) collective-permute-start(bf16[128,1024]{1,0:T(8,128)(2,1)S(1)} %get-tuple-element.35), channel_id=1, source_target_pairs={{0,8},{8,0},{16,152},{24,144},{32,72},{40,64},{48,216},{56,208},{6... | collective-permute-start | bytes 786440 | tf_op jit(solution)/shard_map/ppermute | solution.py:498
  33.4 1.9 collective-permute-start.2
  35.3 3.8 %collective-permute-start.8 = (bf16[144,1024]{1,0:T(8,128)(2,1)S(1)}, bf16[144,1024]{1,0:T(8,128)(2,1)S(1)}, u32[]{:S(2)}, u32[]{:S(2)}) collective-permute-start(bf16[144,1024]{1,0:T(8,128)(2,1)S(1)} %get-tuple-element.38), channel_id=1, source_target_pairs={{0,0},{8,16},{16,32},{24,48},{32,64},{40,80},{48,96},{56,112},{64,... | collective-permute-start | bytes 884744 | tf_op jit(solution)/shard_map/ppermute | solution.py:499
  39.1 4.8 %collective-permute-start.9 = (bf16[144,1024]{1,0:T(8,128)(2,1)S(1)}, bf16[144,1024]{1,0:T(8,128)(2,1)S(1)}, u32[]{:S(2)}, u32[]{:S(2)}) collective-permute-start(bf16[144,1024]{1,0:T(8,128)(2,1)S(1)} %get-tuple-element.39), channel_id=1, source_target_pairs={{0,16},{8,0},{16,48},{24,32},{32,80},{40,64},{48,112},{56,96},{64,... | collective-permute-start | bytes 884744 | tf_op jit(solution)/shard_map/ppermute | solution.py:499
  43.9 8.3 %collective-permute-start.10 = (bf16[144,1024]{1,0:T(8,128)(2,1)S(1)}, bf16[144,1024]{1,0:T(8,128)(2,1)S(1)}, u32[]{:S(2)}, u32[]{:S(2)}) collective-permute-start(bf16[144,1024]{1,0:T(8,128)(2,1)S(1)} %get-tuple-element.40), channel_id=1, source_target_pairs={{0,32},{8,48},{16,0},{24,16},{32,96},{40,112},{48,64},{56,80},{64,... | collective-permute-start | bytes 884744 | tf_op jit(solution)/shard_map/ppermute | solution.py:499
  52.3 0.5 collective-permute-done.2.refs_2_
  52.8 5.2 %collective-permute-start.11 = (bf16[144,1024]{1,0:T(8,128)(2,1)}, bf16[144,1024]{1,0:T(8,128)(2,1)S(1)}, u32[]{:S(2)}, u32[]{:S(2)}) collective-permute-start(bf16[144,1024]{1,0:T(8,128)(2,1)} %get-tuple-element.41), channel_id=1, source_target_pairs={{0,48},{8,32},{16,16},{24,0},{32,112},{40,96},{48,80},{56,64},{64,... | collective-permute-start | bytes 884744 | tf_op jit(solution)/shard_map/ppermute | solution.py:499
  58.0 2.1 %collective-permute-done.3.refs_3_ = bf16[128,1024]{1,0:T(8,128)(2,1)S(1)} collective-permute-done((bf16[128,1024]{1,0:T(8,128)(2,1)S(1)}, bf16[128,1024]{1,0:T(8,128)(2,1)S(1)}, u32[]{:S(2)}, u32[]{:S(2)}) %collective-permute-start.3) | collective-permute-done | bytes 262176 | tf_op jit(solution)/shard_map/ppermute | solution.py:498
  60.2 1.3 collective-permute-start.4
  61.5 0.5 collective-permute-start.6
  62.1 1.1 slice_select_fusion
  63.2 0.1 collective-permute-done.11.refs_11_
  63.3 3.2 %collective-permute-start.12 = (bf16[144,1024]{1,0:T(8,128)(2,1)S(1)}, bf16[144,1024]{1,0:T(8,128)(2,1)S(1)}, u32[]{:S(2)}, u32[]{:S(2)}) collective-permute-start(bf16[144,1024]{1,0:T(8,128)(2,1)S(1)} %collective-permute-done.8.refs_8_), channel_id=1, source_target_pairs={{0,64},{64,0},{1,65},{65,1},{2,66},{66,2},{3,67},{67,3},{4,68},{68... | collective-permute-start | bytes 884744 | tf_op jit(solution)/shard_map/ppermute | solution.py:501
  66.5 0.5 collective-permute-start.14
  67.1 0.7 copy-done.4
  67.8 0.4 collective-permute-start.16
  68.3 0.2 collective-permute-done.14.refs_14_
  68.5 0.4 collective-permute-done.15.refs_15_
  69.0 0.4 collective-permute-done.16.refs_17_
  69.4 0.9 copy-done.5
  70.3 13.9 %forward.1 = (bf16[1024,1024]{1,0:T(8,128)(2,1)}, bf16[1024,1024]{1,0:T(8,128)(2,1)}, bf16[1024,1024]{1,0:T(8,128)(2,1)}, bf16[1024,1024]{1,0:T(8,128)(2,1)}, bf...) custom-call(s32[4]{0:T(128)S(1)} %pad_add_fusion.meta, ...), custom_call_target="tpu_custom_call" | custom-call | tf_op jit(solution)/shard_map/forward/pallas_call | solution.py:206
  84.3 0.4 collective-permute-start.17
  84.7 1.5 collective-permute-done.17.peer
  86.3 1.2 copy-done
  87.5 1.2 copy-done.1
  88.7 4.8 %middle.1 = (bf16[1024,256]{1,0:T(8,128)(2,1)S(1)}, bf16[1024,256]{1,0:T(8,128)(2,1)S(1)}, bf16[4,32,1024]{2,1,0:T(8,128)(2,1)S(1)}, bf16[4,32,1024]{2,1,0:T(8,128)(2,1)S(1)}) custom-call(s32[4]{0:T(128)S(1)} %pad_add_fusion.meta, f32[1024,128]{1,0:T(8,128)S(1)} %get-tuple-element.46.own.stats, f32[1024,128]{1,0:T(8,128)S(1)} %collective-permute-done.17.peer, ...), custom_call_target="tpu_custom_call" | custom-call | tf_op jit(solution)/shard_map/middle/pallas_call | solution.py:280
  93.5 0.7 collective-permute-start.18
  94.2 1.2 collective-permute-done.18.recv
  95.4 11.8 %backward.1 = (bf16[1408,1024]{1,0:T(8,128)(2,1)}, bf16[1024,1024]{1,0:T(8,128)(2,1)S(1)}) custom-call(s32[4]{0:T(128)S(1)} %pad_add_fusion.meta, bf16[1024,1024]{1,0:T(8,128)(2,1)} %get-tuple-element.42.gate.act, bf16[1024,1024]{1,0:T(8,128)(2,1)} %get-tuple-element.43.gslope.slope, bf16[1024,1024]{1,0:T(8,128)(2,1)} %get-tuple-element.44.probs, ...), custom_call_target="tpu_custom_call" | custom-call | tf_op jit(solution)/shard_map/backward/pallas_call | solution.py:355
  107.2 7.4 %input_grad.1 = (bf16[512,1024]{1,0:T(8,128)(2,1)S(1)}, bf16[512,1024]{1,0:T(8,128)(2,1)S(1)}) custom-call(s32[4]{0:T(128)S(1)} %pad_add_fusion.meta, bf16[1024,1024]{1,0:T(8,128)(2,1)S(1)} %get-tuple-element.55.dhid, bf16[1024,1024]{1,0:T(8,128)(2,1)} %get-tuple-element.52.normed, f32[1024,128]{1,0:T(8,128)S(1)} %get-tuple-element.46.own.stats, ...), custom_call_target="tpu_custom_call" | custom-call | tf_op jit(solution)/shard_map/input_grad/pallas_call | solution.py:389
  114.6 0.4 collective-permute-start.19
  115.1 2.3 %collective-permute-done.19.b = bf16[512,1024]{1,0:T(8,128)(2,1)S(1)} collective-permute-done((bf16[512,1024]{1,0:T(8,128)(2,1)S(1)}, bf16[512,1024]{1,0:T(8,128)(2,1)S(1)}, u32[]{:S(2)}, u32[]{:S(2)}) %collective-permute-start.19) | collective-permute-done | bytes 1048608 | tf_op jit(solution)/shard_map/ppermute | solution.py:513
  117.4 0.8 add_halves.1
  118.2 2.5 %collective-permute-start.20 = (bf16[128,1024]{1,0:T(8,128)(2,1)S(1)}, bf16[128,1024]{1,0:T(8,128)(2,1)S(1)}, u32[]{:S(2)}, u32[]{:S(2)}) collective-permute-start(bf16[128,1024]{1,0:T(8,128)(2,1)S(1)} %get-tuple-element.58), channel_id=1, source_target_pairs={{0,0},{16,8},{32,16},{48,24},{64,32},{80,40},{96,48},{112,56},{8,6... | collective-permute-start | bytes 786440 | tf_op jit(solution)/shard_map/ppermute | solution.py:514
  120.7 1.9 collective-permute-start.21
  122.7 5.4 %collective-permute-start.22 = (bf16[128,1024]{1,0:T(8,128)(2,1)S(1)}, bf16[128,1024]{1,0:T(8,128)(2,1)S(1)}, u32[]{:S(2)}, u32[]{:S(2)}) collective-permute-start(bf16[128,1024]{1,0:T(8,128)(2,1)S(1)} %get-tuple-element.60), channel_id=1, source_target_pairs={{32,0},{48,8},{0,16},{16,24},{96,32},{112,40},{64,48},{80,56},{40,... | collective-permute-start | bytes 786440 | tf_op jit(solution)/shard_map/ppermute | solution.py:514
  128.1 4.5 %collective-permute-start.23 = (bf16[128,1024]{1,0:T(8,128)(2,1)S(1)}, bf16[128,1024]{1,0:T(8,128)(2,1)S(1)}, u32[]{:S(2)}, u32[]{:S(2)}) collective-permute-start(bf16[128,1024]{1,0:T(8,128)(2,1)S(1)} %get-tuple-element.61), channel_id=1, source_target_pairs={{48,0},{32,8},{16,16},{0,24},{112,32},{96,40},{80,48},{64,56},{56,... | collective-permute-start | bytes 786440 | tf_op jit(solution)/shard_map/ppermute | solution.py:514
  132.6 4.8 %collective-permute-done.21.refs_1_ = bf16[128,1024]{1,0:T(8,128)(2,1)S(1)} collective-permute-done((bf16[128,1024]{1,0:T(8,128)(2,1)S(1)}, bf16[128,1024]{1,0:T(8,128)(2,1)S(1)}, u32[]{:S(2)}, u32[]{:S(2)}) %collective-permute-start.21) | collective-permute-done | bytes 262176 | tf_op jit(solution)/shard_map/ppermute | solution.py:514
  137.5 0.2 collective-permute-done.22.refs_2_
  137.7 7.6 %collective-permute-done.23.refs_3_ = bf16[128,1024]{1,0:T(8,128)(2,1)S(1)} collective-permute-done((bf16[128,1024]{1,0:T(8,128)(2,1)S(1)}, bf16[128,1024]{1,0:T(8,128)(2,1)S(1)}, u32[]{:S(2)}, u32[]{:S(2)}) %collective-permute-start.23) | collective-permute-done | bytes 262176 | tf_op jit(solution)/shard_map/ppermute | solution.py:514
  145.3 4.2 %reduce-scatter.2.cloned.1.call-done = bf16[176,1024]{1,0:T(8,128)(2,1)} async-done(((bf16[1408,1024]{1,0:T(8,128)(2,1)}), bf16[176,1024]{1,0:T(8,128)(2,1)}) %reduce-scatter.2.cloned.1.call-update) | async-done | bytes 360464 | tf_op jit(solution)/shard_map/reduce_scatter | solution.py:511
  149.5 1.1 reshape.80
  150.6 15.4 %all_to_all.10 = bf16[16,11,1024]{2,1,0:T(8,128)(2,1)S(1)} all-to-all(bf16[16,11,1024]{2,1,0:T(8,128)(2,1)S(1)} %reshape.80), channel_id=1, replica_groups=mesh['yh'=2,'core'=2,'yl'=2,'x'=4,'z'=8] {'yh','yl','x'}, dimensions={0} | all-to-all | bytes 720896 | tf_op jit(solution)/shard_map/all_to_all | solution.py:519
  166.0 0.1 reduce_sum.12
  166.1 11.6 %all_to_all.11 = bf16[16,11,1024]{2,1,0:T(8,128)(2,1)S(1)} all-to-all(bf16[16,11,1024]{2,1,0:T(8,128)(2,1)S(1)} %broadcast_in_dim.2), channel_id=1, replica_groups=mesh['yh'=2,'core'=2,'yl'=2,'x'=4,'z'=8] {'yh','yl','x'}, dimensions={0} | all-to-all | bytes 720896 | tf_op jit(solution)/shard_map/all_to_all | solution.py:519
  177.8 0.1 reshape.81
  177.9 7.5 %collective-permute-start.24 = (bf16[176,1024]{1,0:T(8,128)(2,1)S(1)}, bf16[176,1024]{1,0:T(8,128)(2,1)S(1)}, u32[]{:S(2)}, u32[]{:S(2)}) collective-permute-start(bf16[176,1024]{1,0:T(8,128)(2,1)S(1)} %reshape.81), channel_id=1, source_target_pairs={{0,64},{64,0},{1,65},{65,1},{2,66},{66,2},{3,67},{67,3},{4,68},{68... | collective-permute-start | bytes 1081352 | tf_op jit(solution)/shard_map/ppermute | solution.py:524
  185.4 1.6 place.1
  187.1 0.2 convert_multiply_fusion.1
  187.4 0.2 stack_reshape.6
  187.7 0.2 stack_reshape.7
  187.9 0.2 pad_maximum_fusion
  188.1 0.8 copy.23
  189.0 1.8 reshape.82
  190.8 0.6 pad_maximum_fusion.1
  191.3 0.7 maximum_maximum_fusion.1
  (55 shorter events, 0.9 us)
Async XLA Ops:
  7.2 55.0 %all-gather.2.cloned.1.call-start = ((), (), s32[]{:S(2)}) async-start(), calls=%async_computation.3 | async-start | bytes 2949120 | tf_op jit(solution)/shard_map/all_gather | solution.py:484
  9.5 1.9 copy-start.7
  9.6 2.0 copy-start.6
  9.6 12.9 %copy-start.9 = (s32[4]{0:T(128)S(1)}, s32[4]{0:T(128)}, u32[]{:S(2)}) copy-start(s32[4]{0:T(128)} %param.10) | copy-start | bytes 52
  9.6 13.0 %copy-start.2 = (bf16[4,128,1024]{2,1,0:T(8,128)(2,1)S(1)}, bf16[4,128,1024]{2,1,0:T(8,128)(2,1)}, u32[]{:S(2)}) copy-start(bf16[4,128,1024]{2,1,0:T(8,128)(2,1)} %lay.1) | copy-start | bytes 3145732
  9.6 13.0 %copy-start.3 = (bf16[4,128,1024]{2,1,0:T(8,128)(2,1)S(1)}, bf16[4,128,1024]{2,1,0:T(8,128)(2,1)}, u32[]{:S(2)}) copy-start(bf16[4,128,1024]{2,1,0:T(8,128)(2,1)} %grad.1) | copy-start | bytes 3145732
  10.6 57.7 %copy-start.8 = (bf16[2,128]{1,0:T(2,128)(2,1)S(1)}, bf16[2,128]{1,0:T(2,128)(2,1)}, u32[]{:S(2)}) copy-start(bf16[2,128]{1,0:T(2,128)(2,1)} %param.14) | copy-start | bytes 1540
  11.4 138.1 %reduce-scatter.2.cloned.1.call-start = ((), (), s32[]{:S(2)}) async-start(), calls=%async_computation.4 | async-start | bytes 3244032 | tf_op jit(solution)/shard_map/reduce_scatter | solution.py:511
  24.3 19.5 %collective-permute-start = (bf16[128,1024]{1,0:T(8,128)(2,1)S(1)}, bf16[128,1024]{1,0:T(8,128)(2,1)S(1)}, u32[]{:S(2)}, u32[]{:S(2)}) collective-permute-start(bf16[128,1024]{1,0:T(8,128)(2,1)S(1)} %get-tuple-element.34), channel_id=1, source_target_pairs={{0,0},{8,8},{16,144},{24,152},{32,64},{40,72},{48,208},{56,216},{6... | collective-permute-start | bytes 786440 | tf_op jit(solution)/shard_map/ppermute | solution.py:498
  30.4 21.8 %collective-permute-start.1 = (bf16[128,1024]{1,0:T(8,128)(2,1)S(1)}, bf16[128,1024]{1,0:T(8,128)(2,1)S(1)}, u32[]{:S(2)}, u32[]{:S(2)}) collective-permute-start(bf16[128,1024]{1,0:T(8,128)(2,1)S(1)} %get-tuple-element.35), channel_id=1, source_target_pairs={{0,8},{8,0},{16,152},{24,144},{32,72},{40,64},{48,216},{56,208},{6... | collective-permute-start | bytes 786440 | tf_op jit(solution)/shard_map/ppermute | solution.py:498
  33.4 19.4 %collective-permute-start.2 = (bf16[128,1024]{1,0:T(8,128)(2,1)S(1)}, bf16[128,1024]{1,0:T(8,128)(2,1)S(1)}, u32[]{:S(2)}, u32[]{:S(2)}) collective-permute-start(bf16[128,1024]{1,0:T(8,128)(2,1)S(1)} %get-tuple-element.36), channel_id=1, source_target_pairs={{0,144},{8,152},{16,0},{24,8},{32,208},{40,216},{48,64},{56,72},{6... | collective-permute-start | bytes 786440 | tf_op jit(solution)/shard_map/ppermute | solution.py:498
  35.3 26.2 %collective-permute-start.8 = (bf16[144,1024]{1,0:T(8,128)(2,1)S(1)}, bf16[144,1024]{1,0:T(8,128)(2,1)S(1)}, u32[]{:S(2)}, u32[]{:S(2)}) collective-permute-start(bf16[144,1024]{1,0:T(8,128)(2,1)S(1)} %get-tuple-element.38), channel_id=1, source_target_pairs={{0,0},{8,16},{16,32},{24,48},{32,64},{40,80},{48,96},{56,112},{64,... | collective-permute-start | bytes 884744 | tf_op jit(solution)/shard_map/ppermute | solution.py:499
  39.1 22.4 %collective-permute-start.9 = (bf16[144,1024]{1,0:T(8,128)(2,1)S(1)}, bf16[144,1024]{1,0:T(8,128)(2,1)S(1)}, u32[]{:S(2)}, u32[]{:S(2)}) collective-permute-start(bf16[144,1024]{1,0:T(8,128)(2,1)S(1)} %get-tuple-element.39), channel_id=1, source_target_pairs={{0,16},{8,0},{16,48},{24,32},{32,80},{40,64},{48,112},{56,96},{64,... | collective-permute-start | bytes 884744 | tf_op jit(solution)/shard_map/ppermute | solution.py:499
  43.9 18.2 %collective-permute-start.10 = (bf16[144,1024]{1,0:T(8,128)(2,1)S(1)}, bf16[144,1024]{1,0:T(8,128)(2,1)S(1)}, u32[]{:S(2)}, u32[]{:S(2)}) collective-permute-start(bf16[144,1024]{1,0:T(8,128)(2,1)S(1)} %get-tuple-element.40), channel_id=1, source_target_pairs={{0,32},{8,48},{16,0},{24,16},{32,96},{40,112},{48,64},{56,80},{64,... | collective-permute-start | bytes 884744 | tf_op jit(solution)/shard_map/ppermute | solution.py:499
  52.2 8.0 %collective-permute-start.3 = (bf16[128,1024]{1,0:T(8,128)(2,1)S(1)}, bf16[128,1024]{1,0:T(8,128)(2,1)S(1)}, u32[]{:S(2)}, u32[]{:S(2)}) collective-permute-start(bf16[128,1024]{1,0:T(8,128)(2,1)S(1)} %get-tuple-element.37), channel_id=1, source_target_pairs={{0,152},{8,144},{16,8},{24,0},{32,216},{40,208},{48,72},{56,64},{6... | collective-permute-start | bytes 786440 | tf_op jit(solution)/shard_map/ppermute | solution.py:498
  52.8 10.5 %collective-permute-start.11 = (bf16[144,1024]{1,0:T(8,128)(2,1)}, bf16[144,1024]{1,0:T(8,128)(2,1)S(1)}, u32[]{:S(2)}, u32[]{:S(2)}) collective-permute-start(bf16[144,1024]{1,0:T(8,128)(2,1)} %get-tuple-element.41), channel_id=1, source_target_pairs={{0,48},{8,32},{16,16},{24,0},{32,112},{40,96},{48,80},{56,64},{64,... | collective-permute-start | bytes 884744 | tf_op jit(solution)/shard_map/ppermute | solution.py:499
  60.2 6.3 %collective-permute-start.4 = (bf16[128,1024]{1,0:T(8,128)(2,1)S(1)}, bf16[128,1024]{1,0:T(8,128)(2,1)S(1)}, u32[]{:S(2)}, u32[]{:S(2)}) collective-permute-start(bf16[128,1024]{1,0:T(8,128)(2,1)S(1)} %collective-permute-done.refs_0_), channel_id=1, source_target_pairs={{0,64},{64,0},{1,65},{65,1},{2,66},{66,2},{3,67},{67,3},{4,68},{68... | collective-permute-start | bytes 786440 | tf_op jit(solution)/shard_map/ppermute | solution.py:500
  61.5 5.0 %collective-permute-start.5 = (bf16[128,1024]{1,0:T(8,128)(2,1)S(1)}, bf16[128,1024]{1,0:T(8,128)(2,1)S(1)}, u32[]{:S(2)}, u32[]{:S(2)}) collective-permute-start(bf16[128,1024]{1,0:T(8,128)(2,1)S(1)} %collective-permute-done.1.refs_1_), channel_id=1, source_target_pairs={{0,64},{64,0},{1,65},{65,1},{2,66},{66,2},{3,67},{67,3},{4,68},{68... | collective-permute-start | bytes 786440 | tf_op jit(solution)/shard_map/ppermute | solution.py:500
  61.5 5.5 %collective-permute-start.6 = (bf16[128,1024]{1,0:T(8,128)(2,1)S(1)}, bf16[128,1024]{1,0:T(8,128)(2,1)S(1)}, u32[]{:S(2)}, u32[]{:S(2)}) collective-permute-start(bf16[128,1024]{1,0:T(8,128)(2,1)S(1)} %collective-permute-done.2.refs_2_), channel_id=1, source_target_pairs={{0,64},{64,0},{1,65},{65,1},{2,66},{66,2},{3,67},{67,3},{4,68},{68... | collective-permute-start | bytes 786440 | tf_op jit(solution)/shard_map/ppermute | solution.py:500
  62.0 5.1 %collective-permute-start.7 = (bf16[128,1024]{1,0:T(8,128)(2,1)S(1)}, bf16[128,1024]{1,0:T(8,128)(2,1)S(1)}, u32[]{:S(2)}, u32[]{:S(2)}) collective-permute-start(bf16[128,1024]{1,0:T(8,128)(2,1)S(1)} %collective-permute-done.3.refs_3_), channel_id=1, source_target_pairs={{0,64},{64,0},{1,65},{65,1},{2,66},{66,2},{3,67},{67,3},{4,68},{68... | collective-permute-start | bytes 786440 | tf_op jit(solution)/shard_map/ppermute | solution.py:500
  63.3 5.0 %collective-permute-start.12 = (bf16[144,1024]{1,0:T(8,128)(2,1)S(1)}, bf16[144,1024]{1,0:T(8,128)(2,1)S(1)}, u32[]{:S(2)}, u32[]{:S(2)}) collective-permute-start(bf16[144,1024]{1,0:T(8,128)(2,1)S(1)} %collective-permute-done.8.refs_8_), channel_id=1, source_target_pairs={{0,64},{64,0},{1,65},{65,1},{2,66},{66,2},{3,67},{67,3},{4,68},{68... | collective-permute-start | bytes 884744 | tf_op jit(solution)/shard_map/ppermute | solution.py:501
  66.5 1.8 collective-permute-start.13
  66.5 2.0 %collective-permute-start.14 = (bf16[144,1024]{1,0:T(8,128)(2,1)S(1)}, bf16[144,1024]{1,0:T(8,128)(2,1)S(1)}, u32[]{:S(2)}, u32[]{:S(2)}) collective-permute-start(bf16[144,1024]{1,0:T(8,128)(2,1)S(1)} %collective-permute-done.10.refs_10_), channel_id=1, source_target_pairs={{0,64},{64,0},{1,65},{65,1},{2,66},{66,2},{3,67},{67,3},{4,68},{68... | collective-permute-start | bytes 884744 | tf_op jit(solution)/shard_map/ppermute | solution.py:501
  67.0 2.0 collective-permute-start.15
  67.1 0.7 copy-start.4
  67.8 1.6 collective-permute-start.16
  69.4 0.9 copy-start.5
  84.3 2.0 %collective-permute-start.17 = (f32[1024,128]{1,0:T(8,128)S(1)}, f32[1024,128]{1,0:T(8,128)S(1)}, u32[]{:S(2)}, u32[]{:S(2)}) collective-permute-start(f32[1024,128]{1,0:T(8,128)S(1)} %get-tuple-element.46.own.stats), channel_id=1, source_target_pairs={{0,64},{64,0},{1,65},{65,1},{2,66},{66,2},{3,67},{67,3},{4,68},{68... | collective-permute-start | bytes 1572872 | tf_op jit(solution)/shard_map/ppermute | solution.py:507
  86.3 1.2 copy-start
  87.5 1.2 copy-start.1
  93.5 1.8 collective-permute-start.18
  114.6 2.7 %collective-permute-start.19 = (bf16[512,1024]{1,0:T(8,128)(2,1)S(1)}, bf16[512,1024]{1,0:T(8,128)(2,1)S(1)}, u32[]{:S(2)}, u32[]{:S(2)}) collective-permute-start(bf16[512,1024]{1,0:T(8,128)(2,1)S(1)} %get-tuple-element.57), channel_id=1, source_target_pairs={{0,64},{64,0},{1,65},{65,1},{2,66},{66,2},{3,67},{67,3},{4,68},{68... | collective-permute-start | bytes 3145736 | tf_op jit(solution)/shard_map/ppermute | solution.py:513
  118.2 14.5 %collective-permute-start.20 = (bf16[128,1024]{1,0:T(8,128)(2,1)S(1)}, bf16[128,1024]{1,0:T(8,128)(2,1)S(1)}, u32[]{:S(2)}, u32[]{:S(2)}) collective-permute-start(bf16[128,1024]{1,0:T(8,128)(2,1)S(1)} %get-tuple-element.58), channel_id=1, source_target_pairs={{0,0},{16,8},{32,16},{48,24},{64,32},{80,40},{96,48},{112,56},{8,6... | collective-permute-start | bytes 786440 | tf_op jit(solution)/shard_map/ppermute | solution.py:514
  120.7 16.8 %collective-permute-start.21 = (bf16[128,1024]{1,0:T(8,128)(2,1)S(1)}, bf16[128,1024]{1,0:T(8,128)(2,1)S(1)}, u32[]{:S(2)}, u32[]{:S(2)}) collective-permute-start(bf16[128,1024]{1,0:T(8,128)(2,1)S(1)} %get-tuple-element.59), channel_id=1, source_target_pairs={{16,0},{0,8},{48,16},{32,24},{80,32},{64,40},{112,48},{96,56},{24,... | collective-permute-start | bytes 786440 | tf_op jit(solution)/shard_map/ppermute | solution.py:514
  122.7 15.0 %collective-permute-start.22 = (bf16[128,1024]{1,0:T(8,128)(2,1)S(1)}, bf16[128,1024]{1,0:T(8,128)(2,1)S(1)}, u32[]{:S(2)}, u32[]{:S(2)}) collective-permute-start(bf16[128,1024]{1,0:T(8,128)(2,1)S(1)} %get-tuple-element.60), channel_id=1, source_target_pairs={{32,0},{48,8},{0,16},{16,24},{96,32},{112,40},{64,48},{80,56},{40,... | collective-permute-start | bytes 786440 | tf_op jit(solution)/shard_map/ppermute | solution.py:514
  128.1 17.2 %collective-permute-start.23 = (bf16[128,1024]{1,0:T(8,128)(2,1)S(1)}, bf16[128,1024]{1,0:T(8,128)(2,1)S(1)}, u32[]{:S(2)}, u32[]{:S(2)}) collective-permute-start(bf16[128,1024]{1,0:T(8,128)(2,1)S(1)} %get-tuple-element.61), channel_id=1, source_target_pairs={{48,0},{32,8},{16,16},{0,24},{112,32},{96,40},{80,48},{64,56},{56,... | collective-permute-start | bytes 786440 | tf_op jit(solution)/shard_map/ppermute | solution.py:514
  177.9 9.1 %collective-permute-start.24 = (bf16[176,1024]{1,0:T(8,128)(2,1)S(1)}, bf16[176,1024]{1,0:T(8,128)(2,1)S(1)}, u32[]{:S(2)}, u32[]{:S(2)}) collective-permute-start(bf16[176,1024]{1,0:T(8,128)(2,1)S(1)} %reshape.81), channel_id=1, source_target_pairs={{0,64},{64,0},{1,65},{65,1},{2,66},{66,2},{3,67},{67,3},{4,68},{68... | collective-permute-start | bytes 1081352 | tf_op jit(solution)/shard_map/ppermute | solution.py:524
Sparse Core Ops, SparseCore 0:
  11.5 43.1 all-gather.1
  107.4 42.0 reduce-scatter.1

commit v3 on v1

v3 whole, which is shorter than its diff:
```python
import functools

import jax
import jax.numpy as jnp
from jax import lax
from jax.experimental import pallas as pl
from jax.experimental.pallas import tpu as pltpu
from jax.sharding import Mesh
from jax.sharding import PartitionSpec as P

DH = 256
D = 1024
L = 1024
EPS = 1e-05
BF = jnp.bfloat16
F32 = jnp.float32
BQ = 256
NQ = L // BQ
SHARD = 1408
PLANE = ("yh", "core", "yl", "x")
CHIPS = ("yh", "yl", "x")
ANY = pl.BlockSpec(memory_space=pl.ANY)
VM = pl.BlockSpec(memory_space=pltpu.VMEM)
SM = pl.BlockSpec(memory_space=pltpu.SMEM)


def params(mib):
    return pltpu.CompilerParams(vmem_limit_bytes=mib << 20)


def shape(dims, kind):
    return jax.ShapeDtypeStruct(dims, kind)


def nn(a, b):
    return lax.dot_general(a, b, (((1,), (0,)), ((), ())), preferred_element_type=F32)


def nt(a, b):
    return lax.dot_general(a, b, (((1,), (1,)), ((), ())), preferred_element_type=F32)


def tn(a, b):
    return lax.dot_general(a, b, (((0,), (0,)), ((), ())), preferred_element_type=F32)


def rows(start, size):
    return pl.ds(pl.multiple_of(start, size), size)


def run_copies(copies):
    for c in copies:
        c.start()
    for c in copies:
        c.wait()


def unit_of(raw):
    yh, core, yl, x = raw[0], raw[1], raw[2], raw[3]
    e = 2 * yh + jnp.bitwise_and(x, 1)
    p = 2 * yl + jnp.bitwise_xor(lax.shift_right_logical(x, 1), yh)
    return e, p, core


def prepare_kernel(raw, plan, lay, w_in, w_out, *refs):
    outs, wsel, sem = refs[:4], refs[4], refs[5]
    copies = [
        pltpu.make_async_copy(
            lay.at[plan[jnp.bitwise_xor(raw[3], k)]], outs[k], sem.at[k]
        )
        for k in range(4)
    ]
    for c in copies:
        c.start()
    for head in range(2):

        @pl.when(raw[1] == head)
        def _(head=head):
            for c in range(4):
                wsel[0:128, 256 * c : 256 * c + 256] = w_in[
                    :, 512 * c + 256 * head : 512 * c + 256 * head + 256
                ]
            cols = slice(512 * head, 512 * head + 512)
            wsel[128:160, 0:512] = w_out[0:32, cols]
            wsel[128:160, 512:1024] = w_out[32:64, cols]

    for c in copies:
        c.wait()


def prepare(raw, plan, lay, w_in, w_out):
    return pl.pallas_call(
        prepare_kernel,
        out_shape=[shape((128, D), BF)] * 4 + [shape((160, D), BF)],
        in_specs=[SM, SM, ANY, VM, VM],
        out_specs=[VM] * 5,
        scratch_shapes=[pltpu.SemaphoreType.DMA((4,))],
        compiler_params=params(48),
        name="prepare",
    )(raw, plan, lay, w_in, w_out)


def pick_kernel(raw, lengths, grad, stamps, *refs):
    outs, sem = refs[:4], refs[4]
    slots = [jnp.bitwise_xor(raw[3], k) for k in range(4)]
    copies = [
        pltpu.make_async_copy(grad.at[slots[k]], outs[k].at[pl.ds(0, 128)], sem.at[k])
        for k in range(4)
    ]
    for c in copies:
        c.start()
    here = (raw[2] * 4 + raw[3]) * 128 + lax.broadcasted_iota(jnp.int32, (16, 128), 1)
    line = lax.broadcasted_iota(jnp.int32, (16, 128), 0)
    for k in range(4):
        time = jnp.broadcast_to(stamps[pl.ds(slots[k], 1), :].astype(F32), (16, 128))
        alive = jnp.where(here < lengths[slots[k]], 1.0, 0.0)
        value = jnp.where(line == 0, time, jnp.where(line == 1, alive, 0.0))
        outs[k][128:144, 0:128] = value.astype(BF)
        outs[k][128:144, 128:1024] = jnp.zeros((16, 896), BF)
    for c in copies:
        c.wait()


def pick(raw, lengths, grad, stamps):
    return pl.pallas_call(
        pick_kernel,
        out_shape=[shape((144, D), BF)] * 4,
        in_specs=[SM, SM, ANY, VM],
        out_specs=[VM] * 4,
        scratch_shapes=[pltpu.SemaphoreType.DMA((4,))],
        compiler_params=params(48),
        name="pick",
    )(raw, lengths, grad, stamps)


def block_of(h, other, k):
    half = h if k < 4 else 1 - h
    return half * 4 + jnp.bitwise_xor(other, k % 4)


def load_grad(gs, grad, p, h, sem, first):
    return [
        pltpu.make_async_copy(
            gs[k].at[pl.ds(0, 128)],
            grad.at[rows(block_of(h, p, k) * 128, 128)],
            sem.at[first + k],
        )
        for k in range(8)
    ]


def load_weights(wag, w, sem, first):
    return [
        pltpu.make_async_copy(
            wag.at[pl.ds(160 * z, 128)], w.at[pl.ds(128 * z, 128)], sem.at[first + z]
        )
        for z in range(8)
    ]


def forward_kernel(raw, tb, *refs):
    xs, gs, wag = refs[:8], refs[8:16], refs[16]
    normed, act, slope, probs, pslope, mixed, stats = refs[17:24]
    x, w, nv, av, sv, pv, qv, small, scol, srow, sem, out_sem = refs[24:]
    e, p, h = unit_of(raw)
    copies = load_weights(wag, w, sem, 0)
    for k in range(8):
        copies.append(
            pltpu.make_async_copy(
                xs[k], x.at[rows(block_of(h, e, k) * 128, 128)], sem.at[8 + k]
            )
        )
        copies.append(
            pltpu.make_async_copy(
                gs[k].at[pl.ds(128, 16), pl.ds(0, 128)],
                small.at[block_of(h, p, k)],
                sem.at[16 + k],
            )
        )
    run_copies(copies)
    leaving = []

    def leave(source, target):
        c = pltpu.make_async_copy(source, target, out_sem.at[len(leaving)])
        c.start()
        leaving.append(c)

    for i in range(NQ):
        at = pl.ds(i * BQ, BQ)
        v = x[at, :].astype(F32)
        v = v - jnp.mean(v, axis=-1, keepdims=True)
        r = lax.rsqrt(jnp.mean(v * v, axis=-1, keepdims=True) + EPS)
        n = (v * r).astype(BF)
        nv[at, :] = n
        stats[at, :] = jnp.broadcast_to(r, (BQ, 128))
        for c in range(4):
            cols = pl.ds(256 * c, 256)
            hidden = nn(n, w[:, cols])
            sg = jax.nn.sigmoid(hidden)
            av[at, cols] = (hidden * sg).astype(BF)
            sv[at, cols] = (sg * (1.0 + hidden * (1.0 - sg))).astype(BF)
        for source, target in ((nv, normed), (av, act), (sv, slope)):
            leave(source.at[at], target.at[at])

    for b in range(8):
        tile = small[b].astype(F32)
        srow[0:8, pl.ds(128 * b, 128)] = tile[0:8]
        full = jnp.concatenate([tile, jnp.zeros((112, 128), F32)], axis=0)
        scol[pl.ds(128 * b, 128), :] = jnp.transpose(full)

    both = tb[...].astype(F32)
    table = jnp.broadcast_to(jnp.where(h == 0, both[0:1], both[1:2]), (BQ, 128))
    lane = lax.broadcasted_iota(jnp.int32, (BQ, 128), 1)
    causal = (
        lax.broadcasted_iota(jnp.int32, (BQ, BQ), 1)
        <= lax.broadcasted_iota(jnp.int32, (BQ, BQ), 0)
    )
    for i in range(NQ):
        at = pl.ds(i * BQ, BQ)
        q = (av[at, 512:768].astype(F32) * (DH**-0.5)).astype(BF)
        si = scol[at, 0:1]
        lv = scol[at, 1:2]
        for j in range(i + 1):
            cols = pl.ds(j * BQ, BQ)
            s = nt(q, av[cols, 768:1024])
            near = jnp.clip(si - srow[0:1, cols], 0.0, 127.0).astype(jnp.int32)
            bias = jnp.concatenate(
                [
                    jnp.take_along_axis(table, near[:, :128], axis=1, mode="promise_in_bounds"),
                    jnp.take_along_axis(table, near[:, 128:], axis=1, mode="promise_in_bounds"),
                ],
                axis=1,
            )
            s = s + bias
            sg = jax.nn.sigmoid(s)
            live = jnp.where(causal, lv, 0.0) if j == i else lv
            pv[at, cols] = (s * sg * live).astype(BF)
            qv[at, cols] = (sg * (1.0 + s * (1.0 - sg)) * live).astype(BF)
        upto = (i + 1) * BQ
        for source, target in ((pv, probs), (qv, pslope)):
            leave(source.at[at, pl.ds(0, upto)], target.at[at, pl.ds(0, upto)])
        mixed[at, :] = nn(pv[at, 0:upto], av[0:upto, 256:512])
        stats[at, :] = jnp.where(lane == 5, si, stats[at, :])
    for c in leaving:
        c.wait()


def forward(raw, tb, xs, gs, wag):
    return pl.pallas_call(
        forward_kernel,
        out_shape=[shape((L, D), BF)] * 3
        + [shape((L, L), BF)] * 2
        + [shape((L, DH), F32), shape((L, 128), F32)],
        in_specs=[SM, VM] + [ANY] * 17,
        out_specs=[ANY] * 5 + [VM] * 2,
        scratch_shapes=[
            pltpu.VMEM((L, D), BF),
            pltpu.VMEM((D, D), BF),
            pltpu.VMEM((L, D), BF),
            pltpu.VMEM((L, D), BF),
            pltpu.VMEM((L, D), BF),
            pltpu.VMEM((L, L), BF),
            pltpu.VMEM((L, L), BF),
            pltpu.VMEM((8, 16, 128), BF),
            pltpu.VMEM((L, 128), F32),
            pltpu.VMEM((8, L), F32),
            pltpu.SemaphoreType.DMA((24,)),
            pltpu.SemaphoreType.DMA((20,)),
        ],
        compiler_params=params(56),
        name="forward",
    )(raw, tb, *xs, *gs, wag)


def whole(*dims):
    return pl.BlockSpec(dims, lambda i: (0,) * len(dims))


FIRST = pl.BlockSpec((L, DH), lambda i: (0, 0))


def statistics_kernel(raw, mixed, gate, base, *refs):
    gs, wag, wrecv = refs[:8], refs[8], refs[9]
    dz, stats, grad, wo, sem = refs[10:]
    _, p, h = unit_of(raw)
    copies = load_grad(gs, grad, p, h, sem, 0)
    for q in range(4):
        for r in range(2):
            own = wag.at[
                pl.ds(pl.multiple_of((4 * h + q) * 160 + 128, 32), 32), pl.ds(512 * r, 512)
            ]
            other = wrecv.at[q, :, pl.ds(512 * r, 512)]
            to = pl.ds(64 * q + 32 * r, 32)
            copies.append(
                pltpu.make_async_copy(own, wo.at[to, rows(h * 512, 512)], sem.at[8 + 4 * q + r])
            )
            copies.append(
                pltpu.make_async_copy(
                    other, wo.at[to, rows((1 - h) * 512, 512)], sem.at[10 + 4 * q + r]
                )
            )
    run_copies(copies)
    lane = lax.broadcasted_iota(jnp.int32, (BQ, 128), 1)
    for i in range(NQ):
        at = pl.ds(i * BQ, BQ)
        d = nt(grad[at, :], wo[...])
        dz[at, :] = d
        gated = mixed[at, :] * gate[at, :].astype(F32)
        m = jnp.mean(gated, axis=-1, keepdims=True)
        centred = gated - m
        m2 = jnp.sum(centred * centred, axis=-1, keepdims=True)
        s3 = jnp.sum(d, axis=-1, keepdims=True)
        s4 = jnp.sum(d * centred, axis=-1, keepdims=True)
        row = base[at, :]
        for n, value in enumerate((m, m2, s3, s4)):
            row = jnp.where(lane == n, value, row)
        stats[at, :] = row


def statistics(raw, mixed, act, base, gs, wag, wrecv):
    return pl.pallas_call(
        statistics_kernel,
        grid=(1,),
        out_shape=[shape((L, DH), F32), shape((L, 128), F32)],
        in_specs=[SM, whole(L, DH), FIRST, whole(L, 128)] + [ANY] * 10,
        out_specs=[whole(L, DH), whole(L, 128)],
        scratch_shapes=[
            pltpu.VMEM((L, D), BF),
            pltpu.VMEM((DH, D), BF),
            pltpu.SemaphoreType.DMA((24,)),
        ],
        compiler_params=params(56),
        name="statistics",
    )(raw, mixed, act, base, *gs, wag, wrecv)


def middle_kernel(raw, own, peer, mixed, dz, gate, gslope, *refs):
    gs = refs[:8]
    datt, dhu, keep, send, zl, grad, sem = refs[8:]
    _, p, h = unit_of(raw)
    copies = load_grad(gs, grad, p, h, sem, 0)
    for c in copies:
        c.start()
    for i in range(NQ):
        at = pl.ds(i * BQ, BQ)
        a, b = own[at, :], peer[at, :]
        m0, m1 = a[:, 0:1], b[:, 0:1]
        mean = 0.5 * (m0 + m1)
        gap = m0 - mean
        r = lax.rsqrt((a[:, 1:2] + b[:, 1:2] + 512.0 * gap * gap) * (1.0 / 512.0) + EPS)
        dmean = (a[:, 2:3] + b[:, 2:3]) * (1.0 / 512.0)
        cross = a[:, 3:4] + b[:, 3:4] + gap * (a[:, 2:3] - b[:, 2:3])
        cross = cross * r * (1.0 / 512.0)
        mix = mixed[at, :]
        u = gate[at, :].astype(F32)
        zhat = (mix * u - mean) * r
        zl[at, :] = zhat.astype(BF)
        dgated = r * (dz[at, :] - dmean - zhat * cross)
        datt[at, :] = (dgated * u).astype(BF)
        dhu[at, :] = (dgated * mix * gslope[at, :].astype(F32)).astype(BF)
    for c in copies:
        c.wait()
    for half in range(2):
        po = tn(zl[...], grad[:, 512 * half : 512 * half + 512]).astype(BF)
        for q in range(4):
            block = jnp.concatenate(
                [po[64 * q : 64 * q + 32], po[64 * q + 32 : 64 * q + 64]], axis=1
            )

            @pl.when(h == half)
            def _(block=block, q=q):
                keep[q] = block

            @pl.when(h != half)
            def _(block=block, q=q):
                send[q] = block


def middle(raw, own, peer, mixed, dz, act, slope, gs):
    return pl.pallas_call(
        middle_kernel,
        grid=(1,),
        out_shape=[shape((L, DH), BF)] * 2 + [shape((4, 32, D), BF)] * 2,
        in_specs=[SM, whole(L, 128), whole(L, 128), whole(L, DH), whole(L, DH), FIRST, FIRST]
        + [ANY] * 8,
        out_specs=[whole(L, DH), whole(L, DH), whole(4, 32, D), whole(4, 32, D)],
        scratch_shapes=[
            pltpu.VMEM((L, DH), BF),
            pltpu.VMEM((L, D), BF),
            pltpu.SemaphoreType.DMA((8,)),
        ],
        compiler_params=params(56),
        name="middle",
    )(raw, own, peer, mixed, dz, act, slope, *gs)


def backward_kernel(
    raw, act_in, slope_in, probs_in, pslope_in, normed_in, datt, dhu, stats, keep, recv, *refs
):
    part, dhid_out, act, slope, probs, pslope, normed, dhid, dlow, hot, sem = refs
    h = raw[1]
    sources = (act_in, pslope_in, slope_in, probs_in, normed_in)
    targets = (act, pslope, slope, probs, normed)
    copies = [
        pltpu.make_async_copy(a, b, sem.at[n]) for n, (a, b) in enumerate(zip(sources, targets))
    ]
    for c in copies:
        c.start()
    stamp_lane = lax.broadcasted_iota(jnp.int32, (L, 256), 1).astype(F32)
    hot[...] = jnp.where(stats[:, 5:6] == stamp_lane, 1.0, 0.0).astype(BF)
    dhid[:, 0:256] = dhu[...]
    bucket = lax.broadcasted_iota(jnp.int32, (BQ, 128), 1)
    time = lax.broadcasted_iota(jnp.int32, (BQ, 256), 1)
    total = jnp.zeros((BQ, 128), F32)
    for c in copies[:3]:
        c.wait()
    for i in range(NQ):
        at = pl.ds(i * BQ, BQ)
        upto = (i + 1) * BQ
        da = datt[at, :]
        for j in range(i + 1):
            cols = pl.ds(j * BQ, BQ)
            dp = nt(da, act[cols, 256:512])
            dlow[at, cols] = (dp * pslope[at, cols].astype(F32)).astype(BF)
        low = dlow[at, 0:upto]
        dq = nn(low, act[0:upto, 768:1024]) * (DH**-0.5)
        dhid[at, 512:768] = (dq * slope[at, 512:768].astype(F32)).astype(BF)
        by_time = nn(low, hot[0:upto, :])
        si = stats[at, 5:6].astype(jnp.int32)
        when = si - bucket
        index = jnp.bitwise_and(when, 127)
        early = jnp.take_along_axis(by_time[:, :128], index, axis=1, mode="promise_in_bounds")
        late = jnp.take_along_axis(by_time[:, 128:], index, axis=1, mode="promise_in_bounds")
        picked = jnp.where(when >= 128, late, jnp.where(when >= 0, early, 0.0))
        far = jnp.sum(jnp.where(time <= si - 127, by_time, 0.0), axis=-1, keepdims=True)
        total = total + jnp.where(bucket == 127, far, picked)
    copies[3].wait()
    for j in range(NQ):
        cols = pl.ds(j * BQ, BQ)
        frm = j * BQ
        dv = tn(probs[frm:, cols], datt[frm:, :])
        dhid[cols, 256:512] = (dv * slope[cols, 256:512].astype(F32)).astype(BF)
        dk = tn(dlow[frm:, cols], act[frm:, 512:768]) * (DH**-0.5)
        dhid[cols, 768:1024] = (dk * slope[cols, 768:1024].astype(F32)).astype(BF)
    leaving = pltpu.make_async_copy(dhid, dhid_out, sem.at[5])
    leaving.start()
    copies[4].wait()
    for b in range(4):
        for c in range(4):
            pin = tn(normed[:, 256 * b : 256 * b + 256], dhid[:, pl.ds(256 * c, 256)]).astype(BF)
            for z in range(2):
                for t in range(2):
                    start = (2 * b + z) * SHARD + 128 * (2 * c + t)
                    part[pl.ds(start, 128), :] = pin[
                        128 * z : 128 * z + 128, 128 * t : 128 * t + 128
                    ]
    bias = jnp.sum(total, axis=0, keepdims=True)
    high = bias.astype(BF).astype(F32)
    line = lax.broadcasted_iota(jnp.int32, (128, 128), 0)
    tile = jnp.where(line == 0, high, jnp.where(line == 1, bias - high, 0.0)).astype(BF)
    for z in range(8):
        part[pl.ds(z * SHARD + 1280, 128), :] = tile
    for q in range(4):
        for t in range(8):
            mine = pl.multiple_of((4 * h + q) * SHARD + 1024 + 32 * t, 32)
            theirs = pl.multiple_of((4 * (1 - h) + q) * SHARD + 1024 + 32 * t, 32)
            part[pl.ds(mine, 32), :] = keep[q, :, 128 * t : 128 * t + 128]
            part[pl.ds(theirs, 32), :] = recv[q, :, 128 * t : 128 * t + 128]
    leaving.wait()


def backward(raw, act, slope, probs, pslope, normed, datt, dhu, stats, keep, recv):
    return pl.pallas_call(
        backward_kernel,
        out_shape=[shape((8 * SHARD, 128), BF), shape((L, D), BF)],
        in_specs=[SM] + [ANY] * 5 + [VM] * 5,
        out_specs=[VM, ANY],
        scratch_shapes=[
            pltpu.VMEM((L, D), BF),
            pltpu.VMEM((L, D), BF),
            pltpu.VMEM((L, L), BF),
            pltpu.VMEM((L, L), BF),
            pltpu.VMEM((L, D), BF),
            pltpu.VMEM((L, D), BF),
            pltpu.VMEM((L, L), BF),
            pltpu.VMEM((L, 256), BF),
            pltpu.SemaphoreType.DMA((6,)),
        ],
        compiler_params=params(56),
        name="backward",
    )(raw, act, slope, probs, pslope, normed, datt, dhu, stats, keep, recv)


def input_kernel(raw, dhid, normed, stats, wag, own, other, w, sem):
    h = raw[1]
    run_copies(load_weights(wag, w, sem, 0))
    for i in range(NQ):
        at = pl.ds(i * BQ, BQ)
        dn = nt(dhid[at, :], w[...])
        n = normed[at, :].astype(F32)
        r = stats[at, 4:5]
        mean = jnp.mean(dn, axis=-1, keepdims=True)
        cross = jnp.mean(dn * n, axis=-1, keepdims=True)
        res = (r * (dn - mean - n * cross)).astype(BF)
        to = pl.ds((i % 2) * BQ, BQ)

        @pl.when(h == i // 2)
        def _(res=res, to=to):
            own[to, :] = res

        @pl.when(h != i // 2)
        def _(res=res, to=to):
            other[to, :] = res


def input_grad(raw, dhid, normed, stats, wag):
    return pl.pallas_call(
        input_kernel,
        out_shape=[shape((512, D), BF)] * 2,
        in_specs=[SM] + [VM] * 3 + [ANY],
        out_specs=[VM, VM],
        scratch_shapes=[pltpu.VMEM((D, D), BF), pltpu.SemaphoreType.DMA((8,))],
        compiler_params=params(48),
        name="input_grad",
    )(raw, dhid, normed, stats, wag)


def add_kernel(raw, a, b, *outs):
    _, p, _ = unit_of(raw)
    for k in range(4):
        at = rows(jnp.bitwise_xor(p, k) * 128, 128)
        outs[k][...] = (a[at, :].astype(F32) + b[at, :].astype(F32)).astype(BF)


def add_halves(raw, a, b):
    return pl.pallas_call(
        add_kernel,
        out_shape=[shape((128, D), BF)] * 4,
        in_specs=[SM, VM, VM],
        out_specs=[VM] * 4,
        compiler_params=params(48),
        name="add_halves",
    )(raw, a, b)


def place_kernel(raw, *refs):
    chunks, out, sem = refs[:4], refs[4], refs[5]
    run_copies(
        [
            pltpu.make_async_copy(chunks[k], out.at[jnp.bitwise_xor(raw[3], k)], sem.at[k])
            for k in range(4)
        ]
    )


def place(raw, chunks):
    return pl.pallas_call(
        place_kernel,
        out_shape=shape((4, 128, D), BF),
        in_specs=[SM] + [ANY] * 4,
        out_specs=VM,
        scratch_shapes=[pltpu.SemaphoreType.DMA((4,))],
        compiler_params=params(48),
        name="place",
    )(raw, *chunks)


def finish_kernel(raw, mine, theirs, w_in, w_out, bias):
    for core in range(2):

        @pl.when(raw[1] == core)
        def _(core=core):
            for side, src in ((core, mine), (1 - core, theirs)):
                for t in range(8):
                    col = 512 * (t // 2) + 256 * side + 128 * (t % 2)
                    w_in[:, col : col + 128] = src[128 * t : 128 * t + 128, :].astype(F32) / 128.0
                    at = 1024 + 32 * t
                    row, col = 32 * (t // 4), 512 * side + 128 * (t % 4)
                    w_out[row : row + 32, col : col + 128] = (
                        src[at : at + 32, :].astype(F32) / 128.0
                    )
                tail = src[1280:1296, :].astype(F32)
                bias[side : side + 1, :] = (tail[0:1] + tail[1:2]) / 128.0


def finish(raw, mine, theirs):
    return pl.pallas_call(
        finish_kernel,
        out_shape=[shape((128, 2 * D), F32), shape((64, D), F32), shape((2, 128), F32)],
        in_specs=[SM, VM, VM],
        out_specs=[VM] * 3,
        compiler_params=params(48),
        name="finish",
    )(raw, mine, theirs)


def device(yh, core, yl, x):
    return ((yh * 2 + core) * 2 + yl) * 4 + x


def unit_device(e, p, half):
    ye, ce = e >> 1, e & 1
    yp, cp = p >> 1, p & 1
    return device(ye, half, yp, 2 * (ye ^ cp) + ce)


def input_pairs(k):
    pairs = []
    for p in range(4):
        for yl in range(2):
            for x in range(4):
                pairs.append((device(p >> 1, p & 1, yl, x), unit_device(x ^ k, p, yl)))
    return pairs


def grad_pairs(k):
    pairs = []
    for e in range(4):
        for yl in range(2):
            for x in range(4):
                pairs.append((device(e >> 1, e & 1, yl, x), unit_device(e, x ^ k, yl)))
    return pairs


def back_pairs(k):
    return [(b, a) for a, b in grad_pairs(k)]


def local(layer_in, repack_plan, lengths, stamps, w_in, w_out, time_bias, grad_out):
    raw = jnp.stack([lax.axis_index(n).astype(jnp.int32) for n in PLANE])
    first = lax.axis_index("core") == 0
    swap = functools.partial(lax.ppermute, axis_name="core", perm=[(0, 1), (1, 0)])

    *chunks, wsel = prepare(raw, repack_plan, layer_in, w_in, w_out)
    wag = lax.all_gather(wsel, "z", axis=0, tiled=True)
    xs = [lax.ppermute(c, PLANE, input_pairs(k)) for k, c in enumerate(chunks)]
    picked = pick(raw, lengths, grad_out, stamps)
    gs = [lax.ppermute(c, PLANE, grad_pairs(k)) for k, c in enumerate(picked)]
    xs = xs + [swap(c) for c in xs]
    gs = gs + [swap(c) for c in gs]
    w3 = wag.reshape(8, 160, D)
    wrecv = swap(jnp.where(first, w3[4:, 128:], w3[:4, 128:]))

    normed, act, slope, probs, pslope, mixed, base = forward(raw, time_bias, xs, gs, wag)
    dz, stats = statistics(raw, mixed, act, base, gs, wag, wrecv)
    datt, dhu, keep, send = middle(raw, stats, swap(stats), mixed, dz, act, slope, gs)
    part, dhid = backward(
        raw, act, slope, probs, pslope, normed, datt, dhu, stats, keep, swap(send)
    )
    mine = lax.psum_scatter(part, "z", scatter_dimension=0, tiled=True)
    own, other = input_grad(raw, dhid, normed, stats, wag)
    pieces = add_halves(raw, own, swap(other))
    back = [lax.ppermute(pieces[k], PLANE, back_pairs(k)) for k in range(4)]
    input_gradient = place(raw, back)
    mine, input_gradient = lax.optimization_barrier((mine, input_gradient))

    def exchange(v):
        return lax.all_to_all(v, CHIPS, split_axis=0, concat_axis=0, tiled=True)

    spread = exchange(mine.reshape(16, SHARD // 16, 128))
    summed = jnp.sum(spread.astype(F32), axis=0, keepdims=True).astype(BF)
    mine = exchange(jnp.broadcast_to(summed, spread.shape)).reshape(SHARD, 128)
    grad_w_in, grad_w_out, grad_bias = finish(raw, mine, swap(mine))
    return input_gradient, grad_w_in, grad_w_out, grad_bias


def solution(mesh):
    fine = Mesh(mesh.devices.reshape(2, 2, 2, 4, 8), ("yh", "core", "yl", "x", "z"))
    events = P(("yh", "core", "z"), ("yl", "x"), None)
    slots = P(("yh", "core", "z"))
    return jax.shard_map(
        local,
        mesh=fine,
        in_specs=(
            events,
            slots,
            slots,
            P(("yh", "core", "z"), ("yl", "x")),
            P("z", None),
            P("z", None),
            P(),
            events,
        ),
        out_specs=(events, P("z", None), P("z", None), P()),
        check_vma=False,
    )
```

time: 339 us -> 189 us (0.56)
  Pallas kernels: 142 us -> 48.8 us
  waiting for transfers between devices: 52.8 us -> 21.6 us
  between operations: 25.2 us -> 14.5 us
  other arithmetic: 6.52 us -> 1.19 us
  starting transfers between devices: 70.4 us -> 66.3 us
    pallas_call x4 -> x7, Pallas kernels: 99.7 us -> 39.1 us  [the longest x1 12.2 us: backward(): pl.pallas_call(backward_kernel, out_shape=[shape((8 * SHARD, 128), BF), s...]
    pallas_call x1, Pallas kernels: 33.6 us -> 1.63 us  [place(): pl.pallas_call(place_kernel, out_shape=shape((4, 128, D), BF), in_specs=[...]
    reduce_scatter x1, waiting for transfers between devices: 31.3 us -> 0.02 us  [local(): mine = lax.psum_scatter(part, 'z', scatter_dimension=0, tiled=True)]
    ppermute x10, starting transfers between devices: 50.3 us -> 38 us  [the longest x4 15.7 us: local(): gs = [lax.ppermute(c, PLANE, grad_pairs(k)) for k, c in enumerate(picked)]]
    ppermute x4, starting transfers between devices: 3.65 us -> 9.33 us  [local(): xs = xs + [swap(c) for c in xs]]
    unnamed x31 -> x52, local copies, waits for them, and re-layouts: 5.85 us -> 10.9 us
    reshape x4 -> x0, local copies, waits for them, and re-layouts: 4.5 us -> none  [the longest x1 1.81 us: local(): grad_w_in = jnp.stack([pair0[:128].reshape(128, 4, DH), pair1[:128].resha...]
  transfers between devices with their start and end apart: 27 -> 27, of which waited for: 10 -> 8; matrix products, arithmetic and copies ran while one was open for 1% -> 1% of each run, Pallas kernels for 33% -> 11%
where the time goes in v3:
time: 189 us; the launch traced here: 188 us
  starting transfers between devices  66.3 us (35%)
  Pallas kernels  48.8 us (26%)
  blocking collectives  24.5 us (13%)
  waiting for transfers between devices  21.6 us (11%)
  between operations  14.5 us (8%)
  local copies, waits for them, and re-layouts  11 us (6%)
    all_to_all x2, blocking collectives, exchange(): return lax.all_to_all(v, CHIPS, split_axis=0, concat_axis=0, tiled=True)  24.5 us
    ppermute x4, starting transfers between devices, local(): gs = [lax.ppermute(c, PLANE, grad_pairs(k)) for k, c in enumerate(picked)]  15.7 us
    ppermute x4, starting transfers between devices, local(): xs = [lax.ppermute(c, PLANE, input_pairs(k)) for k, c in enumerate(chunks)]  14.9 us
    ppermute x4, starting transfers between devices, local(): back = [lax.ppermute(pieces[k], PLANE, back_pairs(k)) for k in range(4)]  14.8 us
    ppermute x4, waiting for transfers between devices, local(): back = [lax.ppermute(pieces[k], PLANE, back_pairs(k)) for k in range(4)]  12.7 us
    pallas_call x1, Pallas kernels, backward(): pl.pallas_call(backward_kernel, out_shape=[shape((8 * SHARD, 128), BF), s...  12.2 us
    unnamed x52, local copies, waits for them, and re-layouts  10.9 us
    pallas_call x1, Pallas kernels, forward(): pl.pallas_call(forward_kernel, out_shape=[shape((L, D), BF)] * 3 + [shape...  10.8 us
  transfers between devices with their start and end apart: 27, of which 8 were waited for; matrix products, arithmetic and copies ran while one was open for 1% of the time, Pallas kernels for 11%

profile of v3, /device:TPU:1, one launch (start us, length us, event | category | flops | bytes accessed | tf_op | source)
XLA Modules:
  0.0 187.9 jit_solution(16151770668050906971)
XLA Ops:
  7.2 0.1 pad_add_fusion.raw
  7.3 1.3 copy-done.3
  8.6 1.0 copy-done.4
  9.7 0.9 copy-done.5
  10.6 0.7 copy-done.10
  11.2 1.4 prepare.1
  12.7 6.0 %collective-permute-start = (bf16[128,1024]{1,0:T(8,128)(2,1)S(1)}, bf16[128,1024]{1,0:T(8,128)(2,1)S(1)}, u32[]{:S(2)}, u32[]{:S(2)}) collective-permute-start(bf16[128,1024]{1,0:T(8,128)(2,1)S(1)} %get-tuple-element.39), channel_id=1, source_target_pairs={{0,0},{8,8},{16,144},{24,152},{32,64},{40,72},{48,208},{56,216},{6... | collective-permute-start | bytes 786440 | tf_op jit(solution)/shard_map/ppermute | solution.py:636
  18.8 3.0 %collective-permute-start.1 = (bf16[128,1024]{1,0:T(8,128)(2,1)S(1)}, bf16[128,1024]{1,0:T(8,128)(2,1)S(1)}, u32[]{:S(2)}, u32[]{:S(2)}) collective-permute-start(bf16[128,1024]{1,0:T(8,128)(2,1)S(1)} %get-tuple-element.40), channel_id=1, source_target_pairs={{0,8},{8,0},{16,152},{24,144},{32,72},{40,64},{48,216},{56,208},{6... | collective-permute-start | bytes 786440 | tf_op jit(solution)/shard_map/ppermute | solution.py:636
  21.8 1.9 %collective-permute-start.2 = (bf16[128,1024]{1,0:T(8,128)(2,1)S(1)}, bf16[128,1024]{1,0:T(8,128)(2,1)}, u32[]{:S(2)}, u32[]{:S(2)}) collective-permute-start(bf16[128,1024]{1,0:T(8,128)(2,1)S(1)} %get-tuple-element.41), channel_id=1, source_target_pairs={{0,144},{8,152},{16,0},{24,8},{32,208},{40,216},{48,64},{56,72},{6... | collective-permute-start | bytes 786440 | tf_op jit(solution)/shard_map/ppermute | solution.py:636
  23.7 0.7 copy-done.8
  24.4 0.7 copy-done.9
  25.0 0.7 pick.1
  25.7 3.8 %collective-permute-start.8 = (bf16[144,1024]{1,0:T(8,128)(2,1)S(1)}, bf16[144,1024]{1,0:T(8,128)(2,1)S(1)}, u32[]{:S(2)}, u32[]{:S(2)}) collective-permute-start(bf16[144,1024]{1,0:T(8,128)(2,1)S(1)} %get-tuple-element.43), channel_id=1, source_target_pairs={{0,0},{8,16},{16,32},{24,48},{32,64},{40,80},{48,96},{56,112},{64,... | collective-permute-start | bytes 884744 | tf_op jit(solution)/shard_map/ppermute | solution.py:638
  29.5 4.8 %collective-permute-start.9 = (bf16[144,1024]{1,0:T(8,128)(2,1)S(1)}, bf16[144,1024]{1,0:T(8,128)(2,1)S(1)}, u32[]{:S(2)}, u32[]{:S(2)}) collective-permute-start(bf16[144,1024]{1,0:T(8,128)(2,1)S(1)} %get-tuple-element.44), channel_id=1, source_target_pairs={{0,16},{8,0},{16,48},{24,32},{32,80},{40,64},{48,112},{56,96},{64,... | collective-permute-start | bytes 884744 | tf_op jit(solution)/shard_map/ppermute | solution.py:638
  34.3 3.9 %collective-permute-start.3 = (bf16[128,1024]{1,0:T(8,128)(2,1)S(1)}, bf16[128,1024]{1,0:T(8,128)(2,1)S(1)}, u32[]{:S(2)}, u32[]{:S(2)}) collective-permute-start(bf16[128,1024]{1,0:T(8,128)(2,1)S(1)} %get-tuple-element.42), channel_id=1, source_target_pairs={{0,152},{8,144},{16,8},{24,0},{32,216},{40,208},{48,72},{56,64},{6... | collective-permute-start | bytes 786440 | tf_op jit(solution)/shard_map/ppermute | solution.py:636
  38.2 3.5 %collective-permute-start.10 = (bf16[144,1024]{1,0:T(8,128)(2,1)S(1)}, bf16[144,1024]{1,0:T(8,128)(2,1)S(1)}, u32[]{:S(2)}, u32[]{:S(2)}) collective-permute-start(bf16[144,1024]{1,0:T(8,128)(2,1)S(1)} %get-tuple-element.45), channel_id=1, source_target_pairs={{0,32},{8,48},{16,0},{24,16},{32,96},{40,112},{48,64},{56,80},{64,... | collective-permute-start | bytes 884744 | tf_op jit(solution)/shard_map/ppermute | solution.py:638
  41.7 1.3 collective-permute-done.2.refs_2_
  43.0 3.7 %collective-permute-start.11 = (bf16[144,1024]{1,0:T(8,128)(2,1)S(1)}, bf16[144,1024]{1,0:T(8,128)(2,1)S(1)}, u32[]{:S(2)}, u32[]{:S(2)}) collective-permute-start(bf16[144,1024]{1,0:T(8,128)(2,1)S(1)} %get-tuple-element.46), channel_id=1, source_target_pairs={{0,48},{8,32},{16,16},{24,0},{32,112},{40,96},{48,80},{56,64},{64,... | collective-permute-start | bytes 884744 | tf_op jit(solution)/shard_map/ppermute | solution.py:638
  46.7 2.2 %collective-permute-start.4 = (bf16[128,1024]{1,0:T(8,128)(2,1)S(1)}, bf16[128,1024]{1,0:T(8,128)(2,1)S(1)}, u32[]{:S(2)}, u32[]{:S(2)}) collective-permute-start(bf16[128,1024]{1,0:T(8,128)(2,1)S(1)} %collective-permute-done.refs_0_), channel_id=1, source_target_pairs={{0,64},{64,0},{1,65},{65,1},{2,66},{66,2},{3,67},{67,3},{4,68},{68... | collective-permute-start | bytes 786440 | tf_op jit(solution)/shard_map/ppermute | solution.py:639
  48.9 0.1 collective-permute-start.5
  49.0 0.4 collective-permute-start.6
  49.4 6.6 %collective-permute-start.7 = (bf16[128,1024]{1,0:T(8,128)(2,1)S(1)}, bf16[128,1024]{1,0:T(8,128)(2,1)}, u32[]{:S(2)}, u32[]{:S(2)}) collective-permute-start(bf16[128,1024]{1,0:T(8,128)(2,1)S(1)} %collective-permute-done.3.refs_3_), channel_id=1, source_target_pairs={{0,64},{64,0},{1,65},{65,1},{2,66},{66,2},{3,67},{67,3},{4,68},{68... | collective-permute-start | bytes 786440 | tf_op jit(solution)/shard_map/ppermute | solution.py:639
  56.1 2.2 %collective-permute-start.12 = (bf16[144,1024]{1,0:T(8,128)(2,1)S(1)}, bf16[144,1024]{1,0:T(8,128)(2,1)S(1)}, u32[]{:S(2)}, u32[]{:S(2)}) collective-permute-start(bf16[144,1024]{1,0:T(8,128)(2,1)S(1)} %collective-permute-done.8.refs_8_.refs_0_), channel_id=1, source_target_pairs={{0,64},{64,0},{1,65},{65,1},{2,66},{66,2},{3,67},{67,3},{4,68},{68... | collective-permute-start | bytes 884744 | tf_op jit(solution)/shard_map/ppermute | solution.py:640
  58.3 0.1 collective-permute-start.13
  58.4 0.4 collective-permute-start.14
  58.8 0.2 copy-done.25
  59.0 0.1 collective-permute-start.15
  59.1 1.1 slice_select_fusion
  60.1 0.8 collective-permute-start.16
  61.1 0.6 copy-done.15
  61.6 0.1 copy-done.16
  61.7 0.1 copy-done.17
  61.9 0.7 copy-done.18
  62.6 10.8 %forward.1 = (bf16[1024,1024]{1,0:T(8,128)(2,1)}, bf16[1024,1024]{1,0:T(8,128)(2,1)}, bf16[1024,1024]{1,0:T(8,128)(2,1)}, bf16[1024,1024]{1,0:T(8,128)(2,1)}, bf...) custom-call(s32[4]{0:T(128)} %copy-done.6, bf16[2,128]{1,0:T(2,128)(2,1)} %tb.1, ...), custom_call_target="tpu_custom_call" | custom-call | tf_op jit(solution)/shard_map/forward/pallas_call | solution.py:249
  73.4 0.7 copy-done.20
  74.1 5.3 %statistics.1 = (f32[1024,256]{1,0:T(8,128)}, f32[1024,128]{1,0:T(8,128)}) custom-call(s32[4]{0:T(128)} %copy-done.6, f32[1024,256]{1,0:T(8,128)} %get-tuple-element.53.mixed, bf16[1024,1024]{1,0:T(8,128)(2,1)} %get-tuple-element.48.gate.act_in, f32[1024,128]{1,0:T(8,128)} %get-tuple-element.54.base, bf16[144,1024]{1,0:T(8,128)(2,1)} %copy-done.11, ...), custom_call_target="tpu_custom_call" | custom-call | tf_op jit(solution)/shard_map/statistics/pallas_call | solution.py:321
  79.4 0.2 collective-permute-start.17
  79.6 2.1 %collective-permute-done.17.peer = f32[1024,128]{1,0:T(8,128)S(1)} collective-permute-done((f32[1024,128]{1,0:T(8,128)}, f32[1024,128]{1,0:T(8,128)S(1)}, u32[]{:S(2)}, u32[]{:S(2)}) %collective-permute-start.17) | collective-permute-done | bytes 524320 | tf_op jit(solution)/shard_map/ppermute | solution.py:646
  81.6 0.8 copy-done.19
  82.4 7.0 %middle.1 = (bf16[1024,256]{1,0:T(8,128)(2,1)}, bf16[1024,256]{1,0:T(8,128)(2,1)}, bf16[4,32,1024]{2,1,0:T(8,128)(2,1)}, bf16[4,32,1024]{2,1,0:T(8,128)(2,1)}) custom-call(s32[4]{0:T(128)} %copy-done.6, f32[1024,128]{1,0:T(8,128)} %get-tuple-element.55.own.stats, f32[1024,128]{1,0:T(8,128)} %copy-done.19, f32[1024,256]{1,0:T(8,128)} %get-tuple-element.53.mixed, ...), custom_call_target="tpu_custom_call" | custom-call | tf_op jit(solution)/shard_map/middle/pallas_call | solution.py:380
  89.4 0.5 collective-permute-start.18
  89.9 1.6 collective-permute-done.18.recv
  91.5 0.7 copy-done.21
  92.2 12.2 %backward.1 = (bf16[11264,128]{1,0:T(8,128)(2,1)}, bf16[1024,1024]{1,0:T(8,128)(2,1)}) custom-call(s32[4]{0:T(128)} %copy-done.6, bf16[1024,1024]{1,0:T(8,128)(2,1)} %get-tuple-element.48.gate.act_in, bf16[1024,1024]{1,0:T(8,128)(2,1)} %get-tuple-element.49.gslope.slope_in, bf16[1024,1024]{1,0:T(8,128)(2,1)} %get-tuple-element.50.probs_in, ...), custom_call_target="tpu_custom_call" | custom-call | tf_op jit(solution)/shard_map/backward/pallas_call | solution.py:473
  104.4 1.0 copy-done
  105.4 0.7 copy-done.1
  106.1 7.3 %input_grad.1 = (bf16[512,1024]{1,0:T(8,128)(2,1)S(1)}, bf16[512,1024]{1,0:T(8,128)(2,1)S(1)}) custom-call(s32[4]{0:T(128)S(1)} %copy-done.7, bf16[1024,1024]{1,0:T(8,128)(2,1)S(1)} %copy-done.1, bf16[1024,1024]{1,0:T(8,128)(2,1)} %get-tuple-element.52.normed_in.normed, f32[1024,128]{1,0:T(8,128)S(1)} %copy-done, ...), custom_call_target="tpu_custom_call" | custom-call | tf_op jit(solution)/shard_map/input_grad/pallas_call | solution.py:517
  113.4 0.2 collective-permute-start.19
  113.7 2.5 %collective-permute-done.19.b = bf16[512,1024]{1,0:T(8,128)(2,1)S(1)} collective-permute-done((bf16[512,1024]{1,0:T(8,128)(2,1)S(1)}, bf16[512,1024]{1,0:T(8,128)(2,1)S(1)}, u32[]{:S(2)}, u32[]{:S(2)}) %collective-permute-start.19) | collective-permute-done | bytes 1048608 | tf_op jit(solution)/shard_map/ppermute | solution.py:652
  116.2 0.8 add_halves.1
  117.0 3.1 %collective-permute-start.20 = (bf16[128,1024]{1,0:T(8,128)(2,1)S(1)}, bf16[128,1024]{1,0:T(8,128)(2,1)S(1)}, u32[]{:S(2)}, u32[]{:S(2)}) collective-permute-start(bf16[128,1024]{1,0:T(8,128)(2,1)S(1)} %get-tuple-element.65), channel_id=1, source_target_pairs={{0,0},{16,8},{32,16},{48,24},{64,32},{80,40},{96,48},{112,56},{8,6... | collective-permute-start | bytes 786440 | tf_op jit(solution)/shard_map/ppermute | solution.py:653
  120.1 4.2 %collective-permute-start.21 = (bf16[128,1024]{1,0:T(8,128)(2,1)S(1)}, bf16[128,1024]{1,0:T(8,128)(2,1)S(1)}, u32[]{:S(2)}, u32[]{:S(2)}) collective-permute-start(bf16[128,1024]{1,0:T(8,128)(2,1)S(1)} %get-tuple-element.66), channel_id=1, source_target_pairs={{16,0},{0,8},{48,16},{32,24},{80,32},{64,40},{112,48},{96,56},{24,... | collective-permute-start | bytes 786440 | tf_op jit(solution)/shard_map/ppermute | solution.py:653
  124.4 3.2 %collective-permute-start.22 = (bf16[128,1024]{1,0:T(8,128)(2,1)S(1)}, bf16[128,1024]{1,0:T(8,128)(2,1)S(1)}, u32[]{:S(2)}, u32[]{:S(2)}) collective-permute-start(bf16[128,1024]{1,0:T(8,128)(2,1)S(1)} %get-tuple-element.67), channel_id=1, source_target_pairs={{32,0},{48,8},{0,16},{16,24},{96,32},{112,40},{64,48},{80,56},{40,... | collective-permute-start | bytes 786440 | tf_op jit(solution)/shard_map/ppermute | solution.py:653
  127.5 4.2 %collective-permute-start.23 = (bf16[128,1024]{1,0:T(8,128)(2,1)S(1)}, bf16[128,1024]{1,0:T(8,128)(2,1)S(1)}, u32[]{:S(2)}, u32[]{:S(2)}) collective-permute-start(bf16[128,1024]{1,0:T(8,128)(2,1)S(1)} %get-tuple-element.68), channel_id=1, source_target_pairs={{48,0},{32,8},{16,16},{0,24},{112,32},{96,40},{80,48},{64,56},{56,... | collective-permute-start | bytes 786440 | tf_op jit(solution)/shard_map/ppermute | solution.py:653
  131.8 5.0 %collective-permute-done.21.refs_1_ = bf16[128,1024]{1,0:T(8,128)(2,1)S(1)} collective-permute-done((bf16[128,1024]{1,0:T(8,128)(2,1)S(1)}, bf16[128,1024]{1,0:T(8,128)(2,1)S(1)}, u32[]{:S(2)}, u32[]{:S(2)}) %collective-permute-start.21) | collective-permute-done | bytes 262176 | tf_op jit(solution)/shard_map/ppermute | solution.py:653
  136.8 1.5 collective-permute-done.22.refs_2_
  138.3 6.2 %collective-permute-done.23.refs_3_ = bf16[128,1024]{1,0:T(8,128)(2,1)S(1)} collective-permute-done((bf16[128,1024]{1,0:T(8,128)(2,1)S(1)}, bf16[128,1024]{1,0:T(8,128)(2,1)S(1)}, u32[]{:S(2)}, u32[]{:S(2)}) %collective-permute-start.23) | collective-permute-done | bytes 262176 | tf_op jit(solution)/shard_map/ppermute | solution.py:653
  144.5 1.6 place.1
  146.2 13.8 %all_to_all.10 = bf16[16,88,128]{2,1,0:T(8,128)(2,1)S(1)} all-to-all(bf16[16,88,128]{2,1,0:T(8,128)(2,1)} %bitcast.10), channel_id=1, replica_groups=mesh['yh'=2,'core'=2,'yl'=2,'x'=4,'z'=8] {'yh','yl','x'}, dimensions={0} | all-to-all | bytes 720896 | tf_op jit(solution)/shard_map/all_to_all | solution.py:658
  160.1 0.1 reduce_sum.12
  160.2 10.7 %all_to_all.11 = bf16[16,88,128]{2,1,0:T(8,128)(2,1)S(1)} all-to-all(bf16[16,88,128]{2,1,0:T(8,128)(2,1)S(1)} %broadcast_in_dim.2), channel_id=1, replica_groups=mesh['yh'=2,'core'=2,'yl'=2,'x'=4,'z'=8] {'yh','yl','x'}, dimensions={0} | all-to-all | bytes 720896 | tf_op jit(solution)/shard_map/all_to_all | solution.py:658
  170.8 7.1 %collective-permute-start.24 = (bf16[1408,128]{1,0:T(8,128)(2,1)S(1)}, bf16[1408,128]{1,0:T(8,128)(2,1)S(1)}, u32[]{:S(2)}, u32[]{:S(2)}) collective-permute-start(bf16[1408,128]{1,0:T(8,128)(2,1)S(1)} %bitcast.7), channel_id=1, source_target_pairs={{0,64},{64,0},{1,65},{65,1},{2,66},{66,2},{3,67},{67,3},{4,68},{68... | collective-permute-start | bytes 1081352 | tf_op jit(solution)/shard_map/ppermute | solution.py:663
  178.0 1.3 collective-permute-done.24.theirs
  179.3 1.7 finish.1
  (60 shorter events, 0.3 us)
Async XLA Ops:
  7.2 16.5 %copy-start.2 = (bf16[4,128,1024]{2,1,0:T(8,128)(2,1)S(1)}, bf16[4,128,1024]{2,1,0:T(8,128)(2,1)}, u32[]{:S(2)}) copy-start(bf16[4,128,1024]{2,1,0:T(8,128)(2,1)} %grad.1) | copy-start | bytes 3145732
  7.2 51.9 %all-gather.2.cloned.1.call-start = ((), (), s32[]{:S(2)}) async-start(), calls=%async_computation.3 | async-start | bytes 2949120 | tf_op jit(solution)/shard_map/all_gather | solution.py:635
  7.3 1.3 copy-start.3
  8.6 1.0 copy-start.4
  9.7 0.9 copy-start.5
  10.6 0.7 copy-start.10
  11.2 49.8 %copy-start.6 = (s32[4]{0:T(128)}, s32[4]{0:T(128)S(1)}, u32[]{:S(2)}) copy-start(s32[4]{0:T(128)S(1)} %pad_add_fusion.raw) | copy-start | bytes 52
  12.7 133.5 %reduce-scatter.2.cloned.1.call-start = ((), (), s32[]{:S(2)}) async-start(), calls=%async_computation.4 | async-start | bytes 3244032 | tf_op jit(solution)/shard_map/reduce_scatter | solution.py:650
  12.7 21.5 %collective-permute-start = (bf16[128,1024]{1,0:T(8,128)(2,1)S(1)}, bf16[128,1024]{1,0:T(8,128)(2,1)S(1)}, u32[]{:S(2)}, u32[]{:S(2)}) collective-permute-start(bf16[128,1024]{1,0:T(8,128)(2,1)S(1)} %get-tuple-element.39), channel_id=1, source_target_pairs={{0,0},{8,8},{16,144},{24,152},{32,64},{40,72},{48,208},{56,216},{6... | collective-permute-start | bytes 786440 | tf_op jit(solution)/shard_map/ppermute | solution.py:636
  18.8 19.5 %collective-permute-start.1 = (bf16[128,1024]{1,0:T(8,128)(2,1)S(1)}, bf16[128,1024]{1,0:T(8,128)(2,1)S(1)}, u32[]{:S(2)}, u32[]{:S(2)}) collective-permute-start(bf16[128,1024]{1,0:T(8,128)(2,1)S(1)} %get-tuple-element.40), channel_id=1, source_target_pairs={{0,8},{8,0},{16,152},{24,144},{32,72},{40,64},{48,216},{56,208},{6... | collective-permute-start | bytes 786440 | tf_op jit(solution)/shard_map/ppermute | solution.py:636
  21.8 21.2 %collective-permute-start.2 = (bf16[128,1024]{1,0:T(8,128)(2,1)S(1)}, bf16[128,1024]{1,0:T(8,128)(2,1)}, u32[]{:S(2)}, u32[]{:S(2)}) collective-permute-start(bf16[128,1024]{1,0:T(8,128)(2,1)S(1)} %get-tuple-element.41), channel_id=1, source_target_pairs={{0,144},{8,152},{16,0},{24,8},{32,208},{40,216},{48,64},{56,72},{6... | collective-permute-start | bytes 786440 | tf_op jit(solution)/shard_map/ppermute | solution.py:636
  23.7 0.7 copy-start.8
  24.4 0.7 copy-start.9
  25.7 23.2 %collective-permute-start.8 = (bf16[144,1024]{1,0:T(8,128)(2,1)S(1)}, bf16[144,1024]{1,0:T(8,128)(2,1)S(1)}, u32[]{:S(2)}, u32[]{:S(2)}) collective-permute-start(bf16[144,1024]{1,0:T(8,128)(2,1)S(1)} %get-tuple-element.43), channel_id=1, source_target_pairs={{0,0},{8,16},{16,32},{24,48},{32,64},{40,80},{48,96},{56,112},{64,... | collective-permute-start | bytes 884744 | tf_op jit(solution)/shard_map/ppermute | solution.py:638
  29.5 19.5 %collective-permute-start.9 = (bf16[144,1024]{1,0:T(8,128)(2,1)S(1)}, bf16[144,1024]{1,0:T(8,128)(2,1)S(1)}, u32[]{:S(2)}, u32[]{:S(2)}) collective-permute-start(bf16[144,1024]{1,0:T(8,128)(2,1)S(1)} %get-tuple-element.44), channel_id=1, source_target_pairs={{0,16},{8,0},{16,48},{24,32},{32,80},{40,64},{48,112},{56,96},{64,... | collective-permute-start | bytes 884744 | tf_op jit(solution)/shard_map/ppermute | solution.py:638
  34.3 26.7 %copy-start.22 = (bf16[128,1024]{1,0:T(8,128)(2,1)}, bf16[128,1024]{1,0:T(8,128)(2,1)S(1)}, u32[]{:S(2)}) copy-start(bf16[128,1024]{1,0:T(8,128)(2,1)S(1)} %collective-permute-done.refs_0_) | copy-start | bytes 786436
  34.3 12.4 %collective-permute-start.3 = (bf16[128,1024]{1,0:T(8,128)(2,1)S(1)}, bf16[128,1024]{1,0:T(8,128)(2,1)S(1)}, u32[]{:S(2)}, u32[]{:S(2)}) collective-permute-start(bf16[128,1024]{1,0:T(8,128)(2,1)S(1)} %get-tuple-element.42), channel_id=1, source_target_pairs={{0,152},{8,144},{16,8},{24,0},{32,216},{40,208},{48,72},{56,64},{6... | collective-permute-start | bytes 786440 | tf_op jit(solution)/shard_map/ppermute | solution.py:636
  38.2 22.8 %copy-start.23 = (bf16[128,1024]{1,0:T(8,128)(2,1)}, bf16[128,1024]{1,0:T(8,128)(2,1)S(1)}, u32[]{:S(2)}) copy-start(bf16[128,1024]{1,0:T(8,128)(2,1)S(1)} %collective-permute-done.1.refs_1_) | copy-start | bytes 786436
  38.2 11.2 %collective-permute-start.10 = (bf16[144,1024]{1,0:T(8,128)(2,1)S(1)}, bf16[144,1024]{1,0:T(8,128)(2,1)S(1)}, u32[]{:S(2)}, u32[]{:S(2)}) collective-permute-start(bf16[144,1024]{1,0:T(8,128)(2,1)S(1)} %get-tuple-element.45), channel_id=1, source_target_pairs={{0,32},{8,48},{16,0},{24,16},{32,96},{40,112},{48,64},{56,80},{64,... | collective-permute-start | bytes 884744 | tf_op jit(solution)/shard_map/ppermute | solution.py:638
  43.0 13.1 %collective-permute-start.11 = (bf16[144,1024]{1,0:T(8,128)(2,1)S(1)}, bf16[144,1024]{1,0:T(8,128)(2,1)S(1)}, u32[]{:S(2)}, u32[]{:S(2)}) collective-permute-start(bf16[144,1024]{1,0:T(8,128)(2,1)S(1)} %get-tuple-element.46), channel_id=1, source_target_pairs={{0,48},{8,32},{16,16},{24,0},{32,112},{40,96},{48,80},{56,64},{64,... | collective-permute-start | bytes 884744 | tf_op jit(solution)/shard_map/ppermute | solution.py:638
  46.7 14.3 %copy-start.24 = (bf16[128,1024]{1,0:T(8,128)(2,1)}, bf16[128,1024]{1,0:T(8,128)(2,1)S(1)}, u32[]{:S(2)}) copy-start(bf16[128,1024]{1,0:T(8,128)(2,1)S(1)} %collective-permute-done.3.refs_3_) | copy-start | bytes 786436
  46.7 11.6 %collective-permute-start.4 = (bf16[128,1024]{1,0:T(8,128)(2,1)S(1)}, bf16[128,1024]{1,0:T(8,128)(2,1)S(1)}, u32[]{:S(2)}, u32[]{:S(2)}) collective-permute-start(bf16[128,1024]{1,0:T(8,128)(2,1)S(1)} %collective-permute-done.refs_0_), channel_id=1, source_target_pairs={{0,64},{64,0},{1,65},{65,1},{2,66},{66,2},{3,67},{67,3},{4,68},{68... | collective-permute-start | bytes 786440 | tf_op jit(solution)/shard_map/ppermute | solution.py:639
  48.9 12.1 %copy-start.11 = (bf16[144,1024]{1,0:T(8,128)(2,1)}, bf16[144,1024]{1,0:T(8,128)(2,1)S(1)}, u32[]{:S(2)}) copy-start(bf16[144,1024]{1,0:T(8,128)(2,1)S(1)} %collective-permute-done.8.refs_8_.refs_0_) | copy-start | bytes 884740
  48.9 9.5 %collective-permute-start.5 = (bf16[128,1024]{1,0:T(8,128)(2,1)S(1)}, bf16[128,1024]{1,0:T(8,128)(2,1)}, u32[]{:S(2)}, u32[]{:S(2)}) collective-permute-start(bf16[128,1024]{1,0:T(8,128)(2,1)S(1)} %collective-permute-done.1.refs_1_), channel_id=1, source_target_pairs={{0,64},{64,0},{1,65},{65,1},{2,66},{66,2},{3,67},{67,3},{4,68},{68... | collective-permute-start | bytes 786440 | tf_op jit(solution)/shard_map/ppermute | solution.py:639
  49.0 12.0 %copy-start.12 = (bf16[144,1024]{1,0:T(8,128)(2,1)}, bf16[144,1024]{1,0:T(8,128)(2,1)S(1)}, u32[]{:S(2)}) copy-start(bf16[144,1024]{1,0:T(8,128)(2,1)S(1)} %collective-permute-done.9.refs_9_.refs_1_) | copy-start | bytes 884740
  49.0 10.0 %collective-permute-start.6 = (bf16[128,1024]{1,0:T(8,128)(2,1)}, bf16[128,1024]{1,0:T(8,128)(2,1)}, u32[]{:S(2)}, u32[]{:S(2)}) collective-permute-start(bf16[128,1024]{1,0:T(8,128)(2,1)} %collective-permute-done.2.refs_2_), channel_id=1, source_target_pairs={{0,64},{64,0},{1,65},{65,1},{2,66},{66,2},{3,67},{67,3},{4,68},{68... | collective-permute-start | bytes 786440 | tf_op jit(solution)/shard_map/ppermute | solution.py:639
  49.4 11.6 %copy-start.13 = (bf16[144,1024]{1,0:T(8,128)(2,1)}, bf16[144,1024]{1,0:T(8,128)(2,1)S(1)}, u32[]{:S(2)}) copy-start(bf16[144,1024]{1,0:T(8,128)(2,1)S(1)} %collective-permute-done.10.refs_10_.refs_2_) | copy-start | bytes 884740
  49.4 10.7 %collective-permute-start.7 = (bf16[128,1024]{1,0:T(8,128)(2,1)S(1)}, bf16[128,1024]{1,0:T(8,128)(2,1)}, u32[]{:S(2)}, u32[]{:S(2)}) collective-permute-start(bf16[128,1024]{1,0:T(8,128)(2,1)S(1)} %collective-permute-done.3.refs_3_), channel_id=1, source_target_pairs={{0,64},{64,0},{1,65},{65,1},{2,66},{66,2},{3,67},{67,3},{4,68},{68... | collective-permute-start | bytes 786440 | tf_op jit(solution)/shard_map/ppermute | solution.py:639
  56.1 5.0 %copy-start.14 = (bf16[144,1024]{1,0:T(8,128)(2,1)}, bf16[144,1024]{1,0:T(8,128)(2,1)S(1)}, u32[]{:S(2)}) copy-start(bf16[144,1024]{1,0:T(8,128)(2,1)S(1)} %collective-permute-done.11.refs_11_.refs_3_) | copy-start | bytes 884740
  56.1 4.9 %collective-permute-start.12 = (bf16[144,1024]{1,0:T(8,128)(2,1)S(1)}, bf16[144,1024]{1,0:T(8,128)(2,1)S(1)}, u32[]{:S(2)}, u32[]{:S(2)}) collective-permute-start(bf16[144,1024]{1,0:T(8,128)(2,1)S(1)} %collective-permute-done.8.refs_8_.refs_0_), channel_id=1, source_target_pairs={{0,64},{64,0},{1,65},{65,1},{2,66},{66,2},{3,67},{67,3},{4,68},{68... | collective-permute-start | bytes 884744 | tf_op jit(solution)/shard_map/ppermute | solution.py:640
  58.3 0.7 copy-start.25
  58.3 2.6 %collective-permute-start.13 = (bf16[144,1024]{1,0:T(8,128)(2,1)S(1)}, bf16[144,1024]{1,0:T(8,128)(2,1)S(1)}, u32[]{:S(2)}, u32[]{:S(2)}) collective-permute-start(bf16[144,1024]{1,0:T(8,128)(2,1)S(1)} %collective-permute-done.9.refs_9_.refs_1_), channel_id=1, source_target_pairs={{0,64},{64,0},{1,65},{65,1},{2,66},{66,2},{3,67},{67,3},{4,68},{68... | collective-permute-start | bytes 884744 | tf_op jit(solution)/shard_map/ppermute | solution.py:640
  58.4 2.5 %collective-permute-start.14 = (bf16[144,1024]{1,0:T(8,128)(2,1)S(1)}, bf16[144,1024]{1,0:T(8,128)(2,1)S(1)}, u32[]{:S(2)}, u32[]{:S(2)}) collective-permute-start(bf16[144,1024]{1,0:T(8,128)(2,1)S(1)} %collective-permute-done.10.refs_10_.refs_2_), channel_id=1, source_target_pairs={{0,64},{64,0},{1,65},{65,1},{2,66},{66,2},{3,67},{67,3},{4,68},{68... | collective-permute-start | bytes 884744 | tf_op jit(solution)/shard_map/ppermute | solution.py:640
  59.0 2.0 %collective-permute-start.15 = (bf16[144,1024]{1,0:T(8,128)(2,1)S(1)}, bf16[144,1024]{1,0:T(8,128)(2,1)S(1)}, u32[]{:S(2)}, u32[]{:S(2)}) collective-permute-start(bf16[144,1024]{1,0:T(8,128)(2,1)S(1)} %collective-permute-done.11.refs_11_.refs_3_), channel_id=1, source_target_pairs={{0,64},{64,0},{1,65},{65,1},{2,66},{66,2},{3,67},{67,3},{4,68},{68... | collective-permute-start | bytes 884744 | tf_op jit(solution)/shard_map/ppermute | solution.py:640
  60.1 13.2 %collective-permute-start.16 = (bf16[4,32,1024]{2,1,0:T(8,128)(2,1)S(1)}, bf16[4,32,1024]{2,1,0:T(8,128)(2,1)S(1)}, u32[]{:S(2)}, u32[]{:S(2)}) collective-permute-start(bf16[4,32,1024]{2,1,0:T(8,128)(2,1)S(1)} %slice_select_fusion), channel_id=1, source_target_pairs={{0,64},{64,0},{1,65},{65,1},{2,66},{66,2},{3,67},{67,3},{4,68},{68... | collective-permute-start | bytes 786440 | tf_op jit(solution)/shard_map/ppermute | solution.py:642
  60.9 0.7 copy-start.15
  60.9 0.8 copy-start.16
  61.0 0.9 copy-start.17
  61.9 0.7 copy-start.18
  73.4 0.7 copy-start.20
  79.4 2.2 %collective-permute-start.17 = (f32[1024,128]{1,0:T(8,128)}, f32[1024,128]{1,0:T(8,128)S(1)}, u32[]{:S(2)}, u32[]{:S(2)}) collective-permute-start(f32[1024,128]{1,0:T(8,128)} %get-tuple-element.55.own.stats), channel_id=1, source_target_pairs={{0,64},{64,0},{1,65},{65,1},{2,66},{66,2},{3,67},{67,3},{4,68},{68... | collective-permute-start | bytes 1572872 | tf_op jit(solution)/shard_map/ppermute | solution.py:646
  81.6 0.8 copy-start.19
  89.4 2.1 %collective-permute-start.18 = (bf16[4,32,1024]{2,1,0:T(8,128)(2,1)}, bf16[4,32,1024]{2,1,0:T(8,128)(2,1)S(1)}, u32[]{:S(2)}, u32[]{:S(2)}) collective-permute-start(bf16[4,32,1024]{2,1,0:T(8,128)(2,1)} %get-tuple-element.60), channel_id=1, source_target_pairs={{0,64},{64,0},{1,65},{65,1},{2,66},{66,2},{3,67},{67,3},{4,68},{68... | collective-permute-start | bytes 786440 | tf_op jit(solution)/shard_map/ppermute | solution.py:648
  91.5 0.7 copy-start.21
  104.4 1.0 copy-start
  104.4 1.8 copy-start.1
  104.4 1.8 copy-start.7
  113.4 2.7 %collective-permute-start.19 = (bf16[512,1024]{1,0:T(8,128)(2,1)S(1)}, bf16[512,1024]{1,0:T(8,128)(2,1)S(1)}, u32[]{:S(2)}, u32[]{:S(2)}) collective-permute-start(bf16[512,1024]{1,0:T(8,128)(2,1)S(1)} %get-tuple-element.64), channel_id=1, source_target_pairs={{0,64},{64,0},{1,65},{65,1},{2,66},{66,2},{3,67},{67,3},{4,68},{68... | collective-permute-start | bytes 3145736 | tf_op jit(solution)/shard_map/ppermute | solution.py:652
  117.0 14.8 %collective-permute-start.20 = (bf16[128,1024]{1,0:T(8,128)(2,1)S(1)}, bf16[128,1024]{1,0:T(8,128)(2,1)S(1)}, u32[]{:S(2)}, u32[]{:S(2)}) collective-permute-start(bf16[128,1024]{1,0:T(8,128)(2,1)S(1)} %get-tuple-element.65), channel_id=1, source_target_pairs={{0,0},{16,8},{32,16},{48,24},{64,32},{80,40},{96,48},{112,56},{8,6... | collective-permute-start | bytes 786440 | tf_op jit(solution)/shard_map/ppermute | solution.py:653
  120.1 16.6 %collective-permute-start.21 = (bf16[128,1024]{1,0:T(8,128)(2,1)S(1)}, bf16[128,1024]{1,0:T(8,128)(2,1)S(1)}, u32[]{:S(2)}, u32[]{:S(2)}) collective-permute-start(bf16[128,1024]{1,0:T(8,128)(2,1)S(1)} %get-tuple-element.66), channel_id=1, source_target_pairs={{16,0},{0,8},{48,16},{32,24},{80,32},{64,40},{112,48},{96,56},{24,... | collective-permute-start | bytes 786440 | tf_op jit(solution)/shard_map/ppermute | solution.py:653
  124.4 13.9 %collective-permute-start.22 = (bf16[128,1024]{1,0:T(8,128)(2,1)S(1)}, bf16[128,1024]{1,0:T(8,128)(2,1)S(1)}, u32[]{:S(2)}, u32[]{:S(2)}) collective-permute-start(bf16[128,1024]{1,0:T(8,128)(2,1)S(1)} %get-tuple-element.67), channel_id=1, source_target_pairs={{32,0},{48,8},{0,16},{16,24},{96,32},{112,40},{64,48},{80,56},{40,... | collective-permute-start | bytes 786440 | tf_op jit(solution)/shard_map/ppermute | solution.py:653
  127.5 17.0 %collective-permute-start.23 = (bf16[128,1024]{1,0:T(8,128)(2,1)S(1)}, bf16[128,1024]{1,0:T(8,128)(2,1)S(1)}, u32[]{:S(2)}, u32[]{:S(2)}) collective-permute-start(bf16[128,1024]{1,0:T(8,128)(2,1)S(1)} %get-tuple-element.68), channel_id=1, source_target_pairs={{48,0},{32,8},{16,16},{0,24},{112,32},{96,40},{80,48},{64,56},{56,... | collective-permute-start | bytes 786440 | tf_op jit(solution)/shard_map/ppermute | solution.py:653
  170.8 8.4 %collective-permute-start.24 = (bf16[1408,128]{1,0:T(8,128)(2,1)S(1)}, bf16[1408,128]{1,0:T(8,128)(2,1)S(1)}, u32[]{:S(2)}, u32[]{:S(2)}) collective-permute-start(bf16[1408,128]{1,0:T(8,128)(2,1)S(1)} %bitcast.7), channel_id=1, source_target_pairs={{0,64},{64,0},{1,65},{65,1},{2,66},{66,2},{3,67},{67,3},{4,68},{68... | collective-permute-start | bytes 1081352 | tf_op jit(solution)/shard_map/ppermute | solution.py:663
Sparse Core Ops, SparseCore 0:
  12.8 43.1 all-gather.1
  104.5 40.7 reduce-scatter.1

commit v4 on v3

--- a/solution.py
+++ b/solution.py
@@ -55,61 +55,62 @@
         c.wait()
 
 
-def unit_of(raw):
-    yh, core, yl, x = raw[0], raw[1], raw[2], raw[3]
+def unit_of():
+    yh, core, yl, x = (lax.axis_index(n) for n in PLANE)
     e = 2 * yh + jnp.bitwise_and(x, 1)
     p = 2 * yl + jnp.bitwise_xor(lax.shift_right_logical(x, 1), yh)
     return e, p, core
 
 
-def prepare_kernel(raw, plan, lay, w_in, w_out, *refs):
+def prepare_kernel(plan, lay, w_in, w_out, *refs):
     outs, wsel, sem = refs[:4], refs[4], refs[5]
-    copies = [
+    h = lax.axis_index("core")
+    weights = [
         pltpu.make_async_copy(
-            lay.at[plan[jnp.bitwise_xor(raw[3], k)]], outs[k], sem.at[k]
+            w_in.at[:, rows(512 * c + 256 * h, 256)],
+            wsel.at[pl.ds(0, 128), pl.ds(256 * c, 256)],
+            sem.at[4 + c],
+        )
+        for c in range(4)
+    ] + [
+        pltpu.make_async_copy(
+            w_out.at[pl.ds(32 * r, 32), rows(512 * h, 512)],
+            wsel.at[pl.ds(128, 32), pl.ds(512 * r, 512)],
+            sem.at[8 + r],
+        )
+        for r in range(2)
+    ]
+    copies = weights + [
+        pltpu.make_async_copy(
+            lay.at[plan[jnp.bitwise_xor(lax.axis_index("x"), k)]], outs[k], sem.at[k]
         )
         for k in range(4)
     ]
-    for c in copies:
-        c.start()
-    for head in range(2):
-
-        @pl.when(raw[1] == head)
-        def _(head=head):
-            for c in range(4):
-                wsel[0:128, 256 * c : 256 * c + 256] = w_in[
-                    :, 512 * c + 256 * head : 512 * c + 256 * head + 256
-                ]
-            cols = slice(512 * head, 512 * head + 512)
-            wsel[128:160, 0:512] = w_out[0:32, cols]
-            wsel[128:160, 512:1024] = w_out[32:64, cols]
-
-    for c in copies:
-        c.wait()
-
-
-def prepare(raw, plan, lay, w_in, w_out):
+    run_copies(copies)
+
+
+def prepare(plan, lay, w_in, w_out):
     return pl.pallas_call(
         prepare_kernel,
         out_shape=[shape((128, D), BF)] * 4 + [shape((160, D), BF)],
-        in_specs=[SM, SM, ANY, VM, VM],
+        in_specs=[SM, ANY, ANY, ANY],
         out_specs=[VM] * 5,
-        scratch_shapes=[pltpu.SemaphoreType.DMA((4,))],
-        compiler_params=params(48),
+        scratch_shapes=[pltpu.SemaphoreType.DMA((10,))],
+        compiler_params=params(60),
         name="prepare",
-    )(raw, plan, lay, w_in, w_out)
-
-
-def pick_kernel(raw, lengths, grad, stamps, *refs):
+    )(plan, lay, w_in, w_out)
+
+
+def pick_kernel(lengths, grad, stamps, *refs):
     outs, sem = refs[:4], refs[4]
-    slots = [jnp.bitwise_xor(raw[3], k) for k in range(4)]
+    slots = [jnp.bitwise_xor(lax.axis_index("x"), k) for k in range(4)]
     copies = [
         pltpu.make_async_copy(grad.at[slots[k]], outs[k].at[pl.ds(0, 128)], sem.at[k])
         for k in range(4)
     ]
     for c in copies:
         c.start()
-    here = (raw[2] * 4 + raw[3]) * 128 + lax.broadcasted_iota(jnp.int32, (16, 128), 1)
+    here = (lax.axis_index("yl") * 4 + lax.axis_index("x")) * 128 + lax.broadcasted_iota(jnp.int32, (16, 128), 1)
     line = lax.broadcasted_iota(jnp.int32, (16, 128), 0)
     for k in range(4):
         time = jnp.broadcast_to(stamps[pl.ds(slots[k], 1), :].astype(F32), (16, 128))
@@ -121,16 +122,16 @@
         c.wait()
 
 
-def pick(raw, lengths, grad, stamps):
+def pick(lengths, grad, stamps):
     return pl.pallas_call(
         pick_kernel,
         out_shape=[shape((144, D), BF)] * 4,
-        in_specs=[SM, SM, ANY, VM],
+        in_specs=[SM, ANY, VM],
         out_specs=[VM] * 4,
         scratch_shapes=[pltpu.SemaphoreType.DMA((4,))],
-        compiler_params=params(48),
+        compiler_params=params(60),
         name="pick",
-    )(raw, lengths, grad, stamps)
+    )(lengths, grad, stamps)
 
 
 def block_of(h, other, k):
@@ -158,11 +159,11 @@
     ]
 
 
-def forward_kernel(raw, tb, *refs):
-    xs, gs, wag = refs[:8], refs[8:16], refs[16]
-    normed, act, slope, probs, pslope, mixed, stats = refs[17:24]
-    x, w, nv, av, sv, pv, qv, small, scol, srow, sem, out_sem = refs[24:]
-    e, p, h = unit_of(raw)
+def forward_kernel(tb, *refs):
+    xs, gs, wag, wrecv = refs[:8], refs[8:16], refs[16], refs[17]
+    normed, act, slope, probs, pslope, mixed, dz, stats = refs[18:26]
+    x, w, nv, av, sv, pv, qv, grad, wo, small, scol, srow, sem, out_sem = refs[26:]
+    e, p, h = unit_of()
     copies = load_weights(wag, w, sem, 0)
     for k in range(8):
         copies.append(
@@ -177,7 +178,25 @@
                 sem.at[16 + k],
             )
         )
-    run_copies(copies)
+    late = load_grad(gs, grad, p, h, sem, 24)
+    for q in range(4):
+        for r in range(2):
+            own = wag.at[
+                pl.ds(pl.multiple_of((4 * h + q) * 160 + 128, 32), 32), pl.ds(512 * r, 512)
+            ]
+            other = wrecv.at[q, :, pl.ds(512 * r, 512)]
+            to = pl.ds(64 * q + 32 * r, 32)
+            n = 32 + 4 * q + 2 * r
+            late.append(
+                pltpu.make_async_copy(own, wo.at[to, rows(h * 512, 512)], sem.at[n])
+            )
+            late.append(
+                pltpu.make_async_copy(other, wo.at[to, rows((1 - h) * 512, 512)], sem.at[n + 1])
+            )
+    for c in copies + late:
+        c.start()
+    for c in copies:
+        c.wait()
     leaving = []
 
     def leave(source, target):
@@ -241,103 +260,67 @@
             leave(source.at[at, pl.ds(0, upto)], target.at[at, pl.ds(0, upto)])
         mixed[at, :] = nn(pv[at, 0:upto], av[0:upto, 256:512])
         stats[at, :] = jnp.where(lane == 5, si, stats[at, :])
-    for c in leaving:
+    for c in late:
         c.wait()
-
-
-def forward(raw, tb, xs, gs, wag):
-    return pl.pallas_call(
-        forward_kernel,
-        out_shape=[shape((L, D), BF)] * 3
-        + [shape((L, L), BF)] * 2
-        + [shape((L, DH), F32), shape((L, 128), F32)],
-        in_specs=[SM, VM] + [ANY] * 17,
-        out_specs=[ANY] * 5 + [VM] * 2,
-        scratch_shapes=[
-            pltpu.VMEM((L, D), BF),
-            pltpu.VMEM((D, D), BF),
-            pltpu.VMEM((L, D), BF),
-            pltpu.VMEM((L, D), BF),
-            pltpu.VMEM((L, D), BF),
-            pltpu.VMEM((L, L), BF),
-            pltpu.VMEM((L, L), BF),
-            pltpu.VMEM((8, 16, 128), BF),
-            pltpu.VMEM((L, 128), F32),
-            pltpu.VMEM((8, L), F32),
-            pltpu.SemaphoreType.DMA((24,)),
-            pltpu.SemaphoreType.DMA((20,)),
-        ],
-        compiler_params=params(56),
-        name="forward",
-    )(raw, tb, *xs, *gs, wag)
-
-
-def whole(*dims):
-    return pl.BlockSpec(dims, lambda i: (0,) * len(dims))
-
-
-FIRST = pl.BlockSpec((L, DH), lambda i: (0, 0))
-
-
-def statistics_kernel(raw, mixed, gate, base, *refs):
-    gs, wag, wrecv = refs[:8], refs[8], refs[9]
-    dz, stats, grad, wo, sem = refs[10:]
-    _, p, h = unit_of(raw)
-    copies = load_grad(gs, grad, p, h, sem, 0)
-    for q in range(4):
-        for r in range(2):
-            own = wag.at[
-                pl.ds(pl.multiple_of((4 * h + q) * 160 + 128, 32), 32), pl.ds(512 * r, 512)
-            ]
-            other = wrecv.at[q, :, pl.ds(512 * r, 512)]
-            to = pl.ds(64 * q + 32 * r, 32)
-            copies.append(
-                pltpu.make_async_copy(own, wo.at[to, rows(h * 512, 512)], sem.at[8 + 4 * q + r])
-            )
-            copies.append(
-                pltpu.make_async_copy(
-                    other, wo.at[to, rows((1 - h) * 512, 512)], sem.at[10 + 4 * q + r]
-                )
-            )
-    run_copies(copies)
-    lane = lax.broadcasted_iota(jnp.int32, (BQ, 128), 1)
     for i in range(NQ):
         at = pl.ds(i * BQ, BQ)
         d = nt(grad[at, :], wo[...])
         dz[at, :] = d
-        gated = mixed[at, :] * gate[at, :].astype(F32)
+        gated = mixed[at, :] * av[at, 0:256].astype(F32)
         m = jnp.mean(gated, axis=-1, keepdims=True)
         centred = gated - m
         m2 = jnp.sum(centred * centred, axis=-1, keepdims=True)
         s3 = jnp.sum(d, axis=-1, keepdims=True)
         s4 = jnp.sum(d * centred, axis=-1, keepdims=True)
-        row = base[at, :]
+        row = stats[at, :]
         for n, value in enumerate((m, m2, s3, s4)):
             row = jnp.where(lane == n, value, row)
         stats[at, :] = row
-
-
-def statistics(raw, mixed, act, base, gs, wag, wrecv):
-    return pl.pallas_call(
-        statistics_kernel,
-        grid=(1,),
-        out_shape=[shape((L, DH), F32), shape((L, 128), F32)],
-        in_specs=[SM, whole(L, DH), FIRST, whole(L, 128)] + [ANY] * 10,
-        out_specs=[whole(L, DH), whole(L, 128)],
+    for c in leaving:
+        c.wait()
+
+
+def forward(tb, xs, gs, wag, wrecv):
+    return pl.pallas_call(
+        forward_kernel,
+        out_shape=[shape((L, D), BF)] * 3
+        + [shape((L, L), BF)] * 2
+        + [shape((L, DH), F32)] * 2
+        + [shape((L, 128), F32)],
+        in_specs=[VM] + [ANY] * 18,
+        out_specs=[ANY] * 5 + [VM] * 3,
         scratch_shapes=[
             pltpu.VMEM((L, D), BF),
+            pltpu.VMEM((D, D), BF),
+            pltpu.VMEM((L, D), BF),
+            pltpu.VMEM((L, D), BF),
+            pltpu.VMEM((L, D), BF),
+            pltpu.VMEM((L, L), BF),
+            pltpu.VMEM((L, L), BF),
+            pltpu.VMEM((L, D), BF),
             pltpu.VMEM((DH, D), BF),
-            pltpu.SemaphoreType.DMA((24,)),
+            pltpu.VMEM((8, 16, 128), BF),
+            pltpu.VMEM((L, 128), F32),
+            pltpu.VMEM((8, L), F32),
+            pltpu.SemaphoreType.DMA((48,)),
+            pltpu.SemaphoreType.DMA((20,)),
         ],
-        compiler_params=params(56),
-        name="statistics",
-    )(raw, mixed, act, base, *gs, wag, wrecv)
-
-
-def middle_kernel(raw, own, peer, mixed, dz, gate, gslope, *refs):
+        compiler_params=params(34),
+        name="forward",
+    )(tb, *xs, *gs, wag, wrecv)
+
+
+def whole(*dims):
+    return pl.BlockSpec(dims, lambda i: (0,) * len(dims))
+
+
+FIRST = pl.BlockSpec((L, DH), lambda i: (0, 0))
+
+
+def middle_kernel(own, peer, mixed, dz, gate, gslope, *refs):
     gs = refs[:8]
     datt, dhu, keep, send, zl, grad, sem = refs[8:]
-    _, p, h = unit_of(raw)
+    _, p, h = unit_of()
     copies = load_grad(gs, grad, p, h, sem, 0)
     for c in copies:
         c.start()
@@ -360,11 +343,15 @@
         dhu[at, :] = (dgated * mix * gslope[at, :].astype(F32)).astype(BF)
     for c in copies:
         c.wait()
+    out = tn(zl[...], grad[...]).astype(BF)
     for half in range(2):
-        po = tn(zl[...], grad[:, 512 * half : 512 * half + 512]).astype(BF)
         for q in range(4):
             block = jnp.concatenate(
-                [po[64 * q : 64 * q + 32], po[64 * q + 32 : 64 * q + 64]], axis=1
+                [
+                    out[64 * q + r : 64 * q + r + 32, 512 * half : 512 * half + 512]
+                    for r in (0, 32)
+                ],
+                axis=1,
             )
 
             @pl.when(h == half)
@@ -376,12 +363,12 @@
                 send[q] = block
 
 
-def middle(raw, own, peer, mixed, dz, act, slope, gs):
+def middle(own, peer, mixed, dz, act, slope, gs):
     return pl.pallas_call(
         middle_kernel,
         grid=(1,),
         out_shape=[shape((L, DH), BF)] * 2 + [shape((4, 32, D), BF)] * 2,
-        in_specs=[SM, whole(L, 128), whole(L, 128), whole(L, DH), whole(L, DH), FIRST, FIRST]
+        in_specs=[whole(L, 128), whole(L, 128), whole(L, DH), whole(L, DH), FIRST, FIRST]
         + [ANY] * 8,
         out_specs=[whole(L, DH), whole(L, DH), whole(4, 32, D), whole(4, 32, D)],
         scratch_shapes=[
@@ -389,16 +376,16 @@
             pltpu.VMEM((L, D), BF),
             pltpu.SemaphoreType.DMA((8,)),
         ],
-        compiler_params=params(56),
+        compiler_params=params(20),
         name="middle",
-    )(raw, own, peer, mixed, dz, act, slope, *gs)
+    )(own, peer, mixed, dz, act, slope, *gs)
 
 
 def backward_kernel(
-    raw, act_in, slope_in, probs_in, pslope_in, normed_in, datt, dhu, stats, keep, recv, *refs
+    act_in, slope_in, probs_in, pslope_in, normed_in, datt, dhu, stats, keep, recv, *refs
 ):
     part, dhid_out, act, slope, probs, pslope, normed, dhid, dlow, hot, sem = refs
-    h = raw[1]
+    h = lax.axis_index("core")
     sources = (act_in, pslope_in, slope_in, probs_in, normed_in)
     targets = (act, pslope, slope, probs, normed)
     copies = [
@@ -446,14 +433,12 @@
     leaving.start()
     copies[4].wait()
     for b in range(4):
-        for c in range(4):
-            pin = tn(normed[:, 256 * b : 256 * b + 256], dhid[:, pl.ds(256 * c, 256)]).astype(BF)
-            for z in range(2):
-                for t in range(2):
-                    start = (2 * b + z) * SHARD + 128 * (2 * c + t)
-                    part[pl.ds(start, 128), :] = pin[
-                        128 * z : 128 * z + 128, 128 * t : 128 * t + 128
-                    ]
+        pin = tn(normed[:, 256 * b : 256 * b + 256], dhid[...]).astype(BF)
+        for z in range(2):
+            for t in range(8):
+                part[pl.ds((2 * b + z) * SHARD + 128 * t, 128), :] = pin[
+                    128 * z : 128 * z + 128, 128 * t : 128 * t + 128
+                ]
     bias = jnp.sum(total, axis=0, keepdims=True)
     high = bias.astype(BF).astype(F32)
     line = lax.broadcasted_iota(jnp.int32, (128, 128), 0)
@@ -469,11 +454,11 @@
     leaving.wait()
 
 
-def backward(raw, act, slope, probs, pslope, normed, datt, dhu, stats, keep, recv):
+def backward(act, slope, probs, pslope, normed, datt, dhu, stats, keep, recv):
     return pl.pallas_call(
         backward_kernel,
         out_shape=[shape((8 * SHARD, 128), BF), shape((L, D), BF)],
-        in_specs=[SM] + [ANY] * 5 + [VM] * 5,
+        in_specs=[ANY] * 5 + [VM] * 5,
         out_specs=[VM, ANY],
         scratch_shapes=[
             pltpu.VMEM((L, D), BF),
@@ -486,13 +471,13 @@
             pltpu.VMEM((L, 256), BF),
             pltpu.SemaphoreType.DMA((6,)),
         ],
-        compiler_params=params(56),
+        compiler_params=params(34),
         name="backward",
-    )(raw, act, slope, probs, pslope, normed, datt, dhu, stats, keep, recv)
-
-
-def input_kernel(raw, dhid, normed, stats, wag, own, other, w, sem):
-    h = raw[1]
+    )(act, slope, probs, pslope, normed, datt, dhu, stats, keep, recv)
+
+
+def input_kernel(dhid, normed, stats, wag, own, other, w, sem):
+    h = lax.axis_index("core")
     run_copies(load_weights(wag, w, sem, 0))
     for i in range(NQ):
         at = pl.ds(i * BQ, BQ)
@@ -513,62 +498,62 @@
             other[to, :] = res
 
 
-def input_grad(raw, dhid, normed, stats, wag):
+def input_grad(dhid, normed, stats, wag):
     return pl.pallas_call(
         input_kernel,
         out_shape=[shape((512, D), BF)] * 2,
-        in_specs=[SM] + [VM] * 3 + [ANY],
+        in_specs=[VM] * 3 + [ANY],
         out_specs=[VM, VM],
         scratch_shapes=[pltpu.VMEM((D, D), BF), pltpu.SemaphoreType.DMA((8,))],
-        compiler_params=params(48),
+        compiler_params=params(20),
         name="input_grad",
-    )(raw, dhid, normed, stats, wag)
-
-
-def add_kernel(raw, a, b, *outs):
-    _, p, _ = unit_of(raw)
+    )(dhid, normed, stats, wag)
+
+
+def add_kernel(a, b, *outs):
+    _, p, _ = unit_of()
     for k in range(4):
         at = rows(jnp.bitwise_xor(p, k) * 128, 128)
         outs[k][...] = (a[at, :].astype(F32) + b[at, :].astype(F32)).astype(BF)
 
 
-def add_halves(raw, a, b):
+def add_halves(a, b):
     return pl.pallas_call(
         add_kernel,
         out_shape=[shape((128, D), BF)] * 4,
-        in_specs=[SM, VM, VM],
+        in_specs=[VM, VM],
         out_specs=[VM] * 4,
-        compiler_params=params(48),
+        compiler_params=params(16),
         name="add_halves",
-    )(raw, a, b)
-
-
-def place_kernel(raw, *refs):
+    )(a, b)
+
+
+def place_kernel(*refs):
     chunks, out, sem = refs[:4], refs[4], refs[5]
     run_copies(
         [
-            pltpu.make_async_copy(chunks[k], out.at[jnp.bitwise_xor(raw[3], k)], sem.at[k])
+            pltpu.make_async_copy(chunks[k], out.at[jnp.bitwise_xor(lax.axis_index("x"), k)], sem.at[k])
             for k in range(4)
         ]
     )
 
 
-def place(raw, chunks):
+def place(chunks):
     return pl.pallas_call(
         place_kernel,
         out_shape=shape((4, 128, D), BF),
-        in_specs=[SM] + [ANY] * 4,
+        in_specs=[ANY] * 4,
         out_specs=VM,
         scratch_shapes=[pltpu.SemaphoreType.DMA((4,))],
-        compiler_params=params(48),
+        compiler_params=params(16),
         name="place",
-    )(raw, *chunks)
-
-
-def finish_kernel(raw, mine, theirs, w_in, w_out, bias):
+    )(*chunks)
+
+
+def finish_kernel(mine, theirs, w_in, w_out, bias):
     for core in range(2):
 
-        @pl.when(raw[1] == core)
+        @pl.when(lax.axis_index("core") == core)
         def _(core=core):
             for side, src in ((core, mine), (1 - core, theirs)):
                 for t in range(8):
@@ -583,15 +568,15 @@
                 bias[side : side + 1, :] = (tail[0:1] + tail[1:2]) / 128.0
 
 
-def finish(raw, mine, theirs):
+def finish(mine, theirs):
     return pl.pallas_call(
         finish_kernel,
         out_shape=[shape((128, 2 * D), F32), shape((64, D), F32), shape((2, 128), F32)],
-        in_specs=[SM, VM, VM],
+        in_specs=[VM, VM],
         out_specs=[VM] * 3,
-        compiler_params=params(48),
+        compiler_params=params(16),
         name="finish",
-    )(raw, mine, theirs)
+    )(mine, theirs)
 
 
 def device(yh, core, yl, x):
@@ -627,31 +612,29 @@
 
 
 def local(layer_in, repack_plan, lengths, stamps, w_in, w_out, time_bias, grad_out):
-    raw = jnp.stack([lax.axis_index(n).astype(jnp.int32) for n in PLANE])
     first = lax.axis_index("core") == 0
     swap = functools.partial(lax.ppermute, axis_name="core", perm=[(0, 1), (1, 0)])
 
-    *chunks, wsel = prepare(raw, repack_plan, layer_in, w_in, w_out)
+    *chunks, wsel = prepare(repack_plan, layer_in, w_in, w_out)
     wag = lax.all_gather(wsel, "z", axis=0, tiled=True)
     xs = [lax.ppermute(c, PLANE, input_pairs(k)) for k, c in enumerate(chunks)]
-    picked = pick(raw, lengths, grad_out, stamps)
+    picked = pick(lengths, grad_out, stamps)
     gs = [lax.ppermute(c, PLANE, grad_pairs(k)) for k, c in enumerate(picked)]
     xs = xs + [swap(c) for c in xs]
     gs = gs + [swap(c) for c in gs]
     w3 = wag.reshape(8, 160, D)
     wrecv = swap(jnp.where(first, w3[4:, 128:], w3[:4, 128:]))
 
-    normed, act, slope, probs, pslope, mixed, base = forward(raw, time_bias, xs, gs, wag)
-    dz, stats = statistics(raw, mixed, act, base, gs, wag, wrecv)
-    datt, dhu, keep, send = middle(raw, stats, swap(stats), mixed, dz, act, slope, gs)
+    normed, act, slope, probs, pslope, mixed, dz, stats = forward(time_bias, xs, gs, wag, wrecv)
+    datt, dhu, keep, send = middle(stats, swap(stats), mixed, dz, act, slope, gs)
     part, dhid = backward(
-        raw, act, slope, probs, pslope, normed, datt, dhu, stats, keep, swap(send)
+        act, slope, probs, pslope, normed, datt, dhu, stats, keep, swap(send)
     )
     mine = lax.psum_scatter(part, "z", scatter_dimension=0, tiled=True)
-    own, other = input_grad(raw, dhid, normed, stats, wag)
-    pieces = add_halves(raw, own, swap(other))
+    own, other = input_grad(dhid, normed, stats, wag)
+    pieces = add_halves(own, swap(other))
     back = [lax.ppermute(pieces[k], PLANE, back_pairs(k)) for k in range(4)]
-    input_gradient = place(raw, back)
+    input_gradient = place(back)
     mine, input_gradient = lax.optimization_barrier((mine, input_gradient))
 
     def exchange(v):
@@ -660,7 +643,7 @@
     spread = exchange(mine.reshape(16, SHARD // 16, 128))
     summed = jnp.sum(spread.astype(F32), axis=0, keepdims=True).astype(BF)
     mine = exchange(jnp.broadcast_to(summed, spread.shape)).reshape(SHARD, 128)
-    grad_w_in, grad_w_out, grad_bias = finish(raw, mine, swap(mine))
+    grad_w_in, grad_w_out, grad_bias = finish(mine, swap(mine))
     return input_gradient, grad_w_in, grad_w_out, grad_bias
 
 

time: 189 us -> 179 us (0.947)
  Pallas kernels: 48.8 us -> 34.8 us
  local copies, waits for them, and re-layouts: 11 us -> 15.5 us
  starting transfers between devices: 66.3 us -> 64 us
    pallas_call x1 -> x0, Pallas kernels: 5.3 us -> none  [statistics(): pl.pallas_call(statistics_kernel, grid=(1,), out_shape=[shape((L, DH), F3...]
    pallas_call x1, Pallas kernels: 12.2 us -> 7.34 us  [backward(): pl.pallas_call(backward_kernel, out_shape=[shape((8 * SHARD, 128), BF), s...]
    unnamed x52 -> x32, local copies, waits for them, and re-layouts: 10.9 us -> 15.5 us
    pallas_call x1, Pallas kernels: 6.96 us -> 3.08 us  [middle(): pl.pallas_call(middle_kernel, grid=(1,), out_shape=[shape((L, DH), BF)] *...]
    pallas_call x1, Pallas kernels: 7.3 us -> 4.37 us  [input_grad(): pl.pallas_call(input_kernel, out_shape=[shape((512, D), BF)] * 2, in_spec...]
    pallas_call x1, Pallas kernels: 0.67 us -> 2.92 us  [pick(): pl.pallas_call(pick_kernel, out_shape=[shape((144, D), BF)] * 4, in_specs...]
    ppermute x4, starting transfers between devices: 15.7 us -> 13.6 us  [local(): gs = [lax.ppermute(c, PLANE, grad_pairs(k)) for k, c in enumerate(picked)]]
  transfers between devices with their start and end apart: 27 -> 27, of which waited for: 8 -> 10; matrix products, arithmetic and copies ran while one was open for 1% -> 1% of each run, Pallas kernels for 11% -> 5%
where the time goes in v4:
time: 179 us; the launch traced here: 178 us
  starting transfers between devices  64 us (36%)
  Pallas kernels  34.8 us (19%)
  blocking collectives  25.7 us (14%)
  waiting for transfers between devices  22.2 us (12%)
  local copies, waits for them, and re-layouts  15.5 us (9%)
  between operations  14.3 us (8%)
    all_to_all x2, blocking collectives, exchange(): return lax.all_to_all(v, CHIPS, split_axis=0, concat_axis=0, tiled=True)  25.7 us
    unnamed x32, local copies, waits for them, and re-layouts  15.5 us
    ppermute x4, starting transfers between devices, local(): xs = [lax.ppermute(c, PLANE, input_pairs(k)) for k, c in enumerate(chunks)]  14.6 us
    ppermute x4, starting transfers between devices, local(): back = [lax.ppermute(pieces[k], PLANE, back_pairs(k)) for k in range(4)]  13.9 us
    ppermute x4, starting transfers between devices, local(): gs = [lax.ppermute(c, PLANE, grad_pairs(k)) for k, c in enumerate(picked)]  13.6 us
    ppermute x4, waiting for transfers between devices, local(): back = [lax.ppermute(pieces[k], PLANE, back_pairs(k)) for k in range(4)]  12.8 us
    pallas_call x1, Pallas kernels, forward(): pl.pallas_call(forward_kernel, out_shape=[shape((L, D), BF)] * 3 + [shape...  11.4 us
    ppermute x4, starting transfers between devices, local(): xs = xs + [swap(c) for c in xs]  10.5 us
  transfers between devices with their start and end apart: 27, of which 10 were waited for; matrix products, arithmetic and copies ran while one was open for 1% of the time, Pallas kernels for 5%

profile of v4, /device:TPU:1, one launch (start us, length us, event | category | flops | bytes accessed | tf_op | source)
XLA Modules:
  0.0 177.7 jit_solution(5463793182171256989)
XLA Ops:
  7.2 0.0 all-gather.2.cloned.1.call-start
  7.2 3.2 %prepare.1 = (bf16[128,1024]{1,0:T(8,128)(2,1)}, bf16[128,1024]{1,0:T(8,128)(2,1)}, bf16[128,1024]{1,0:T(8,128)(2,1)}, bf16[128,1024]{1,0:T(8,128)(2,1)}, bf16[160,1024]{1,0:T(8,128)(2,1)}) custom-call(s32[4]{0:T(128)} %plan.1, bf16[4,128,1024]{2,1,0:T(8,128)(2,1)} %lay.1, bf16[128,2048]{1,0:T(8,128)(2,1)} %w_in.1, bf16[64,1024]{1,0:T(8,128)(2,1)} %w_out.1), custom_call_target="tpu_custom_call" | custom-call | tf_op jit(solution)/shard_map/prepare/pallas_call | solution.py:93
  10.4 0.0 all-gather.2.cloned.1.call-update
  10.5 0.0 reduce-scatter.2.cloned.1.call-start
  10.5 6.0 %collective-permute-start = (bf16[128,1024]{1,0:T(8,128)(2,1)}, bf16[128,1024]{1,0:T(8,128)(2,1)S(1)}, u32[]{:S(2)}, u32[]{:S(2)}) collective-permute-start(bf16[128,1024]{1,0:T(8,128)(2,1)} %get-tuple-element.38), channel_id=1, source_target_pairs={{0,0},{8,8},{16,144},{24,152},{32,64},{40,72},{48,208},{56,216},{6... | collective-permute-start | bytes 786440 | tf_op jit(solution)/shard_map/ppermute | solution.py:620
  16.6 3.0 %collective-permute-start.1 = (bf16[128,1024]{1,0:T(8,128)(2,1)}, bf16[128,1024]{1,0:T(8,128)(2,1)S(1)}, u32[]{:S(2)}, u32[]{:S(2)}) collective-permute-start(bf16[128,1024]{1,0:T(8,128)(2,1)} %get-tuple-element.39), channel_id=1, source_target_pairs={{0,8},{8,0},{16,152},{24,144},{32,72},{40,64},{48,216},{56,208},{6... | collective-permute-start | bytes 786440 | tf_op jit(solution)/shard_map/ppermute | solution.py:620
  19.6 1.9 %collective-permute-start.2 = (bf16[128,1024]{1,0:T(8,128)(2,1)}, bf16[128,1024]{1,0:T(8,128)(2,1)S(1)}, u32[]{:S(2)}, u32[]{:S(2)}) collective-permute-start(bf16[128,1024]{1,0:T(8,128)(2,1)} %get-tuple-element.40), channel_id=1, source_target_pairs={{0,144},{8,152},{16,0},{24,8},{32,208},{40,216},{48,64},{56,72},{6... | collective-permute-start | bytes 786440 | tf_op jit(solution)/shard_map/ppermute | solution.py:620
  21.5 2.9 %pick.1 = (bf16[144,1024]{1,0:T(8,128)(2,1)}, bf16[144,1024]{1,0:T(8,128)(2,1)}, bf16[144,1024]{1,0:T(8,128)(2,1)}, bf16[144,1024]{1,0:T(8,128)(2,1)}) custom-call(s32[4]{0:T(128)} %lengths.1, bf16[4,128,1024]{2,1,0:T(8,128)(2,1)} %grad.1, s32[4,128]{1,0:T(4,128)} %stamps.1), custom_call_target="tpu_custom_call" | custom-call | tf_op jit(solution)/shard_map/pick/pallas_call | solution.py:126
  24.4 3.8 %collective-permute-start.8 = (bf16[144,1024]{1,0:T(8,128)(2,1)}, bf16[144,1024]{1,0:T(8,128)(2,1)S(1)}, u32[]{:S(2)}, u32[]{:S(2)}) collective-permute-start(bf16[144,1024]{1,0:T(8,128)(2,1)} %get-tuple-element.42), channel_id=1, source_target_pairs={{0,0},{8,16},{16,32},{24,48},{32,64},{40,80},{48,96},{56,112},{64,... | collective-permute-start | bytes 884744 | tf_op jit(solution)/shard_map/ppermute | solution.py:622
  28.2 4.8 %collective-permute-start.9 = (bf16[144,1024]{1,0:T(8,128)(2,1)}, bf16[144,1024]{1,0:T(8,128)(2,1)S(1)}, u32[]{:S(2)}, u32[]{:S(2)}) collective-permute-start(bf16[144,1024]{1,0:T(8,128)(2,1)} %get-tuple-element.43), channel_id=1, source_target_pairs={{0,16},{8,0},{16,48},{24,32},{32,80},{40,64},{48,112},{56,96},{64,... | collective-permute-start | bytes 884744 | tf_op jit(solution)/shard_map/ppermute | solution.py:622
  33.0 3.6 %collective-permute-start.3 = (bf16[128,1024]{1,0:T(8,128)(2,1)}, bf16[128,1024]{1,0:T(8,128)(2,1)S(1)}, u32[]{:S(2)}, u32[]{:S(2)}) collective-permute-start(bf16[128,1024]{1,0:T(8,128)(2,1)} %get-tuple-element.41), channel_id=1, source_target_pairs={{0,152},{8,144},{16,8},{24,0},{32,216},{40,208},{48,72},{56,64},{6... | collective-permute-start | bytes 786440 | tf_op jit(solution)/shard_map/ppermute | solution.py:620
  36.6 3.1 %collective-permute-start.10 = (bf16[144,1024]{1,0:T(8,128)(2,1)}, bf16[144,1024]{1,0:T(8,128)(2,1)S(1)}, u32[]{:S(2)}, u32[]{:S(2)}) collective-permute-start(bf16[144,1024]{1,0:T(8,128)(2,1)} %get-tuple-element.44), channel_id=1, source_target_pairs={{0,32},{8,48},{16,0},{24,16},{32,96},{40,112},{48,64},{56,80},{64,... | collective-permute-start | bytes 884744 | tf_op jit(solution)/shard_map/ppermute | solution.py:622
  39.7 1.4 collective-permute-done.2.refs_2_
  41.1 1.9 %collective-permute-start.11 = (bf16[144,1024]{1,0:T(8,128)(2,1)}, bf16[144,1024]{1,0:T(8,128)(2,1)S(1)}, u32[]{:S(2)}, u32[]{:S(2)}) collective-permute-start(bf16[144,1024]{1,0:T(8,128)(2,1)} %get-tuple-element.45), channel_id=1, source_target_pairs={{0,48},{8,32},{16,16},{24,0},{32,112},{40,96},{48,80},{56,64},{64,... | collective-permute-start | bytes 884744 | tf_op jit(solution)/shard_map/ppermute | solution.py:622
  43.0 6.7 %collective-permute-start.4 = (bf16[128,1024]{1,0:T(8,128)(2,1)S(1)}, bf16[128,1024]{1,0:T(8,128)(2,1)S(1)}, u32[]{:S(2)}, u32[]{:S(2)}) collective-permute-start(bf16[128,1024]{1,0:T(8,128)(2,1)S(1)} %collective-permute-done.refs_0_), channel_id=1, source_target_pairs={{0,64},{64,0},{1,65},{65,1},{2,66},{66,2},{3,67},{67,3},{4,68},{68... | collective-permute-start | bytes 786440 | tf_op jit(solution)/shard_map/ppermute | solution.py:623
  49.7 0.5 collective-permute-start.6
  50.2 0.7 copy-done.7
  50.9 3.4 %collective-permute-start.7 = (bf16[128,1024]{1,0:T(8,128)(2,1)S(1)}, bf16[128,1024]{1,0:T(8,128)(2,1)}, u32[]{:S(2)}, u32[]{:S(2)}) collective-permute-start(bf16[128,1024]{1,0:T(8,128)(2,1)S(1)} %collective-permute-done.3.refs_3_), channel_id=1, source_target_pairs={{0,64},{64,0},{1,65},{65,1},{2,66},{66,2},{3,67},{67,3},{4,68},{68... | collective-permute-start | bytes 786440 | tf_op jit(solution)/shard_map/ppermute | solution.py:623
  54.3 0.7 copy-done.9
  55.0 1.5 collective-permute-start.12
  56.5 0.1 collective-permute-start.13
  56.6 0.7 copy-done.13
  57.3 0.4 collective-permute-start.14
  57.7 0.1 collective-permute-start.15
  57.8 1.1 slice_select_fusion
  58.9 0.7 collective-permute-start.16
  59.6 1.1 collective-permute-done.16.refs_17_
  60.8 1.7 copy-done
  62.5 0.9 copy-done.8
  63.5 0.9 copy-done.10
  64.4 0.9 copy-done.12
  65.4 0.9 copy-done.14
  66.3 11.4 %forward.1 = (bf16[1024,1024]{1,0:T(8,128)(2,1)S(1)}, bf16[1024,1024]{1,0:T(8,128)(2,1)S(1)}, bf16[1024,1024]{1,0:T(8,128)(2,1)S(1)}, bf16[1024,1024]{1,0:T(8,12...) custom-call(bf16[2,128]{1,0:T(2,128)(2,1)S(1)} %copy-done.15, ...), custom_call_target="tpu_custom_call" | custom-call | tf_op jit(solution)/shard_map/forward/pallas_call | solution.py:284
  77.7 0.5 collective-permute-start.17
  78.2 1.5 collective-permute-done.17.peer
  79.7 3.1 %middle.1 = (bf16[1024,256]{1,0:T(8,128)(2,1)S(1)}, bf16[1024,256]{1,0:T(8,128)(2,1)S(1)}, bf16[4,32,1024]{2,1,0:T(8,128)(2,1)S(1)}, bf16[4,32,1024]{2,1,0:T(8,128)(2,1)S(1)}) custom-call(f32[1024,128]{1,0:T(8,128)S(1)} %get-tuple-element.52.own.stats, f32[1024,128]{1,0:T(8,128)S(1)} %collective-permute-done.17.peer, ...), custom_call_target="tpu_custom_call" | custom-call | tf_op jit(solution)/shard_map/middle/pallas_call | solution.py:367
  82.8 0.5 collective-permute-start.18
  83.3 1.2 collective-permute-done.18.recv
  84.5 7.3 %backward.1 = (bf16[11264,128]{1,0:T(8,128)(2,1)S(1)}, bf16[1024,1024]{1,0:T(8,128)(2,1)S(1)}) custom-call(bf16[1024,1024]{1,0:T(8,128)(2,1)S(1)} %get-tuple-element.47.gate.act_in, bf16[1024,1024]{1,0:T(8,128)(2,1)S(1)} %get-tuple-element.48.gslope.slope_in, bf16[1024,1024]{1,0:T(8,128)(2,1)S(1)} %get-tuple-element.49.probs_in, ...), custom_call_target="tpu_custom_call" | custom-call | tf_op jit(solution)/shard_map/backward/pallas_call | solution.py:458
  91.8 1.5 copy-done.4
  93.4 1.4 copy-done.5
  94.7 0.0 reduce-scatter.2.cloned.1.call-update
  94.8 1.7 copy-done.1
  96.5 1.6 copy-done.3
  98.1 1.6 copy-done.6
  99.7 4.4 %input_grad.1 = (bf16[512,1024]{1,0:T(8,128)(2,1)S(1)}, bf16[512,1024]{1,0:T(8,128)(2,1)S(1)}) custom-call(bf16[1024,1024]{1,0:T(8,128)(2,1)S(1)} %copy-done.6, bf16[1024,1024]{1,0:T(8,128)(2,1)S(1)} %copy-done.3, f32[1024,128]{1,0:T(8,128)S(1)} %get-tuple-element.52.own.stats, bf16[1280,1024]{1,0:T(8,128)(2,1)S(1)} %copy-done.1), custom_call_target="tpu_custom_call" | custom-call | tf_op jit(solution)/shard_map/input_grad/pallas_call | solution.py:502
  104.0 0.5 collective-permute-start.19
  104.5 2.3 %collective-permute-done.19.b = bf16[512,1024]{1,0:T(8,128)(2,1)S(1)} collective-permute-done((bf16[512,1024]{1,0:T(8,128)(2,1)S(1)}, bf16[512,1024]{1,0:T(8,128)(2,1)S(1)}, u32[]{:S(2)}, u32[]{:S(2)}) %collective-permute-start.19) | collective-permute-done | bytes 1048608 | tf_op jit(solution)/shard_map/ppermute | solution.py:635
  106.8 0.2 add_halves.1
  107.0 2.5 %collective-permute-start.20 = (bf16[128,1024]{1,0:T(8,128)(2,1)S(1)}, bf16[128,1024]{1,0:T(8,128)(2,1)S(1)}, u32[]{:S(2)}, u32[]{:S(2)}) collective-permute-start(bf16[128,1024]{1,0:T(8,128)(2,1)S(1)} %get-tuple-element.63), channel_id=1, source_target_pairs={{0,0},{16,8},{32,16},{48,24},{64,32},{80,40},{96,48},{112,56},{8,6... | collective-permute-start | bytes 786440 | tf_op jit(solution)/shard_map/ppermute | solution.py:636
  109.5 4.0 %collective-permute-start.21 = (bf16[128,1024]{1,0:T(8,128)(2,1)S(1)}, bf16[128,1024]{1,0:T(8,128)(2,1)S(1)}, u32[]{:S(2)}, u32[]{:S(2)}) collective-permute-start(bf16[128,1024]{1,0:T(8,128)(2,1)S(1)} %get-tuple-element.64), channel_id=1, source_target_pairs={{16,0},{0,8},{48,16},{32,24},{80,32},{64,40},{112,48},{96,56},{24,... | collective-permute-start | bytes 786440 | tf_op jit(solution)/shard_map/ppermute | solution.py:636
  113.5 3.4 %collective-permute-start.22 = (bf16[128,1024]{1,0:T(8,128)(2,1)S(1)}, bf16[128,1024]{1,0:T(8,128)(2,1)S(1)}, u32[]{:S(2)}, u32[]{:S(2)}) collective-permute-start(bf16[128,1024]{1,0:T(8,128)(2,1)S(1)} %get-tuple-element.65), channel_id=1, source_target_pairs={{32,0},{48,8},{0,16},{16,24},{96,32},{112,40},{64,48},{80,56},{40,... | collective-permute-start | bytes 786440 | tf_op jit(solution)/shard_map/ppermute | solution.py:636
  117.0 4.0 %collective-permute-start.23 = (bf16[128,1024]{1,0:T(8,128)(2,1)S(1)}, bf16[128,1024]{1,0:T(8,128)(2,1)S(1)}, u32[]{:S(2)}, u32[]{:S(2)}) collective-permute-start(bf16[128,1024]{1,0:T(8,128)(2,1)S(1)} %get-tuple-element.66), channel_id=1, source_target_pairs={{48,0},{32,8},{16,16},{0,24},{112,32},{96,40},{80,48},{64,56},{56,... | collective-permute-start | bytes 786440 | tf_op jit(solution)/shard_map/ppermute | solution.py:636
  121.0 5.3 %collective-permute-done.21.refs_1_ = bf16[128,1024]{1,0:T(8,128)(2,1)S(1)} collective-permute-done((bf16[128,1024]{1,0:T(8,128)(2,1)S(1)}, bf16[128,1024]{1,0:T(8,128)(2,1)S(1)}, u32[]{:S(2)}, u32[]{:S(2)}) %collective-permute-start.21) | collective-permute-done | bytes 262176 | tf_op jit(solution)/shard_map/ppermute | solution.py:636
  126.3 0.9 collective-permute-done.22.refs_2_
  127.2 6.6 %collective-permute-done.23.refs_3_ = bf16[128,1024]{1,0:T(8,128)(2,1)S(1)} collective-permute-done((bf16[128,1024]{1,0:T(8,128)(2,1)S(1)}, bf16[128,1024]{1,0:T(8,128)(2,1)S(1)}, u32[]{:S(2)}, u32[]{:S(2)}) %collective-permute-start.23) | collective-permute-done | bytes 262176 | tf_op jit(solution)/shard_map/ppermute | solution.py:636
  133.8 1.1 place.1
  134.9 0.5 reduce-scatter.2.cloned.1.call-done
  135.4 15.0 %all_to_all.10 = bf16[16,88,128]{2,1,0:T(8,128)(2,1)S(1)} all-to-all(bf16[16,88,128]{2,1,0:T(8,128)(2,1)} %bitcast.6), channel_id=1, replica_groups=mesh['yh'=2,'core'=2,'yl'=2,'x'=4,'z'=8] {'yh','yl','x'}, dimensions={0} | all-to-all | bytes 720896 | tf_op jit(solution)/shard_map/all_to_all | solution.py:641
  150.4 0.1 reduce_sum.12
  150.5 10.7 %all_to_all.11 = bf16[16,88,128]{2,1,0:T(8,128)(2,1)S(1)} all-to-all(bf16[16,88,128]{2,1,0:T(8,128)(2,1)S(1)} %broadcast_in_dim.2), channel_id=1, replica_groups=mesh['yh'=2,'core'=2,'yl'=2,'x'=4,'z'=8] {'yh','yl','x'}, dimensions={0} | all-to-all | bytes 720896 | tf_op jit(solution)/shard_map/all_to_all | solution.py:641
  161.2 7.1 %collective-permute-start.24 = (bf16[1408,128]{1,0:T(8,128)(2,1)S(1)}, bf16[1408,128]{1,0:T(8,128)(2,1)S(1)}, u32[]{:S(2)}, u32[]{:S(2)}) collective-permute-start(bf16[1408,128]{1,0:T(8,128)(2,1)S(1)} %bitcast.4), channel_id=1, source_target_pairs={{0,64},{64,0},{1,65},{65,1},{2,66},{66,2},{3,67},{67,3},{4,68},{68... | collective-permute-start | bytes 1081352 | tf_op jit(solution)/shard_map/ppermute | solution.py:646
  168.3 1.3 collective-permute-done.24.theirs
  169.6 1.2 finish.1
  (38 shorter events, 0.1 us)
Async XLA Ops:
  7.2 53.6 %copy-start.15 = (bf16[2,128]{1,0:T(2,128)(2,1)S(1)}, bf16[2,128]{1,0:T(2,128)(2,1)}, u32[]{:S(2)}) copy-start(bf16[2,128]{1,0:T(2,128)(2,1)} %tb.1) | copy-start | bytes 1540
  7.2 50.7 %all-gather.2.cloned.1.call-start = ((), (), s32[]{:S(2)}) async-start(), calls=%async_computation.3 | async-start | bytes 2949120 | tf_op jit(solution)/shard_map/all_gather | solution.py:619
  10.5 124.9 %reduce-scatter.2.cloned.1.call-start = ((), (), s32[]{:S(2)}) async-start(), calls=%async_computation.4 | async-start | bytes 3244032 | tf_op jit(solution)/shard_map/reduce_scatter | solution.py:633
  10.5 22.4 %collective-permute-start = (bf16[128,1024]{1,0:T(8,128)(2,1)}, bf16[128,1024]{1,0:T(8,128)(2,1)S(1)}, u32[]{:S(2)}, u32[]{:S(2)}) collective-permute-start(bf16[128,1024]{1,0:T(8,128)(2,1)} %get-tuple-element.38), channel_id=1, source_target_pairs={{0,0},{8,8},{16,144},{24,152},{32,64},{40,72},{48,208},{56,216},{6... | collective-permute-start | bytes 786440 | tf_op jit(solution)/shard_map/ppermute | solution.py:620
  16.6 20.0 %collective-permute-start.1 = (bf16[128,1024]{1,0:T(8,128)(2,1)}, bf16[128,1024]{1,0:T(8,128)(2,1)S(1)}, u32[]{:S(2)}, u32[]{:S(2)}) collective-permute-start(bf16[128,1024]{1,0:T(8,128)(2,1)} %get-tuple-element.39), channel_id=1, source_target_pairs={{0,8},{8,0},{16,152},{24,144},{32,72},{40,64},{48,216},{56,208},{6... | collective-permute-start | bytes 786440 | tf_op jit(solution)/shard_map/ppermute | solution.py:620
  19.6 21.5 %collective-permute-start.2 = (bf16[128,1024]{1,0:T(8,128)(2,1)}, bf16[128,1024]{1,0:T(8,128)(2,1)S(1)}, u32[]{:S(2)}, u32[]{:S(2)}) collective-permute-start(bf16[128,1024]{1,0:T(8,128)(2,1)} %get-tuple-element.40), channel_id=1, source_target_pairs={{0,144},{8,152},{16,0},{24,8},{32,208},{40,216},{48,64},{56,72},{6... | collective-permute-start | bytes 786440 | tf_op jit(solution)/shard_map/ppermute | solution.py:620
  24.4 25.3 %collective-permute-start.8 = (bf16[144,1024]{1,0:T(8,128)(2,1)}, bf16[144,1024]{1,0:T(8,128)(2,1)S(1)}, u32[]{:S(2)}, u32[]{:S(2)}) collective-permute-start(bf16[144,1024]{1,0:T(8,128)(2,1)} %get-tuple-element.42), channel_id=1, source_target_pairs={{0,0},{8,16},{16,32},{24,48},{32,64},{40,80},{48,96},{56,112},{64,... | collective-permute-start | bytes 884744 | tf_op jit(solution)/shard_map/ppermute | solution.py:622
  28.2 21.5 %collective-permute-start.9 = (bf16[144,1024]{1,0:T(8,128)(2,1)}, bf16[144,1024]{1,0:T(8,128)(2,1)S(1)}, u32[]{:S(2)}, u32[]{:S(2)}) collective-permute-start(bf16[144,1024]{1,0:T(8,128)(2,1)} %get-tuple-element.43), channel_id=1, source_target_pairs={{0,16},{8,0},{16,48},{24,32},{32,80},{40,64},{48,112},{56,96},{64,... | collective-permute-start | bytes 884744 | tf_op jit(solution)/shard_map/ppermute | solution.py:622
  33.0 10.1 %collective-permute-start.3 = (bf16[128,1024]{1,0:T(8,128)(2,1)}, bf16[128,1024]{1,0:T(8,128)(2,1)S(1)}, u32[]{:S(2)}, u32[]{:S(2)}) collective-permute-start(bf16[128,1024]{1,0:T(8,128)(2,1)} %get-tuple-element.41), channel_id=1, source_target_pairs={{0,152},{8,144},{16,8},{24,0},{32,216},{40,208},{48,72},{56,64},{6... | collective-permute-start | bytes 786440 | tf_op jit(solution)/shard_map/ppermute | solution.py:620
  36.6 14.3 %collective-permute-start.10 = (bf16[144,1024]{1,0:T(8,128)(2,1)}, bf16[144,1024]{1,0:T(8,128)(2,1)S(1)}, u32[]{:S(2)}, u32[]{:S(2)}) collective-permute-start(bf16[144,1024]{1,0:T(8,128)(2,1)} %get-tuple-element.44), channel_id=1, source_target_pairs={{0,32},{8,48},{16,0},{24,16},{32,96},{40,112},{48,64},{56,80},{64,... | collective-permute-start | bytes 884744 | tf_op jit(solution)/shard_map/ppermute | solution.py:622
  41.1 13.9 %collective-permute-start.11 = (bf16[144,1024]{1,0:T(8,128)(2,1)}, bf16[144,1024]{1,0:T(8,128)(2,1)S(1)}, u32[]{:S(2)}, u32[]{:S(2)}) collective-permute-start(bf16[144,1024]{1,0:T(8,128)(2,1)} %get-tuple-element.45), channel_id=1, source_target_pairs={{0,48},{8,32},{16,16},{24,0},{32,112},{40,96},{48,80},{56,64},{64,... | collective-permute-start | bytes 884744 | tf_op jit(solution)/shard_map/ppermute | solution.py:622
  43.0 13.5 %collective-permute-start.4 = (bf16[128,1024]{1,0:T(8,128)(2,1)S(1)}, bf16[128,1024]{1,0:T(8,128)(2,1)S(1)}, u32[]{:S(2)}, u32[]{:S(2)}) collective-permute-start(bf16[128,1024]{1,0:T(8,128)(2,1)S(1)} %collective-permute-done.refs_0_), channel_id=1, source_target_pairs={{0,64},{64,0},{1,65},{65,1},{2,66},{66,2},{3,67},{67,3},{4,68},{68... | collective-permute-start | bytes 786440 | tf_op jit(solution)/shard_map/ppermute | solution.py:623
  49.7 6.9 %collective-permute-start.5 = (bf16[128,1024]{1,0:T(8,128)(2,1)S(1)}, bf16[128,1024]{1,0:T(8,128)(2,1)S(1)}, u32[]{:S(2)}, u32[]{:S(2)}) collective-permute-start(bf16[128,1024]{1,0:T(8,128)(2,1)S(1)} %collective-permute-done.1.refs_1_), channel_id=1, source_target_pairs={{0,64},{64,0},{1,65},{65,1},{2,66},{66,2},{3,67},{67,3},{4,68},{68... | collective-permute-start | bytes 786440 | tf_op jit(solution)/shard_map/ppermute | solution.py:623
  49.7 8.0 %collective-permute-start.6 = (bf16[128,1024]{1,0:T(8,128)(2,1)S(1)}, bf16[128,1024]{1,0:T(8,128)(2,1)}, u32[]{:S(2)}, u32[]{:S(2)}) collective-permute-start(bf16[128,1024]{1,0:T(8,128)(2,1)S(1)} %collective-permute-done.2.refs_2_), channel_id=1, source_target_pairs={{0,64},{64,0},{1,65},{65,1},{2,66},{66,2},{3,67},{67,3},{4,68},{68... | collective-permute-start | bytes 786440 | tf_op jit(solution)/shard_map/ppermute | solution.py:623
  50.2 0.7 copy-start.7
  50.9 8.0 %collective-permute-start.7 = (bf16[128,1024]{1,0:T(8,128)(2,1)S(1)}, bf16[128,1024]{1,0:T(8,128)(2,1)}, u32[]{:S(2)}, u32[]{:S(2)}) collective-permute-start(bf16[128,1024]{1,0:T(8,128)(2,1)S(1)} %collective-permute-done.3.refs_3_), channel_id=1, source_target_pairs={{0,64},{64,0},{1,65},{65,1},{2,66},{66,2},{3,67},{67,3},{4,68},{68... | collective-permute-start | bytes 786440 | tf_op jit(solution)/shard_map/ppermute | solution.py:623
  54.3 0.7 copy-start.9
  55.0 4.6 %collective-permute-start.12 = (bf16[144,1024]{1,0:T(8,128)(2,1)S(1)}, bf16[144,1024]{1,0:T(8,128)(2,1)S(1)}, u32[]{:S(2)}, u32[]{:S(2)}) collective-permute-start(bf16[144,1024]{1,0:T(8,128)(2,1)S(1)} %collective-permute-done.8.refs_8_.refs_0_), channel_id=1, source_target_pairs={{0,64},{64,0},{1,65},{65,1},{2,66},{66,2},{3,67},{67,3},{4,68},{68... | collective-permute-start | bytes 884744 | tf_op jit(solution)/shard_map/ppermute | solution.py:624
  56.5 3.1 %copy-start.11 = (bf16[128,1024]{1,0:T(8,128)(2,1)}, bf16[128,1024]{1,0:T(8,128)(2,1)S(1)}, u32[]{:S(2)}) copy-start(bf16[128,1024]{1,0:T(8,128)(2,1)S(1)} %collective-permute-done.4.refs_4_) | copy-start | bytes 786436
  56.5 3.1 %collective-permute-start.13 = (bf16[144,1024]{1,0:T(8,128)(2,1)S(1)}, bf16[144,1024]{1,0:T(8,128)(2,1)S(1)}, u32[]{:S(2)}, u32[]{:S(2)}) collective-permute-start(bf16[144,1024]{1,0:T(8,128)(2,1)S(1)} %collective-permute-done.9.refs_9_.refs_1_), channel_id=1, source_target_pairs={{0,64},{64,0},{1,65},{65,1},{2,66},{66,2},{3,67},{67,3},{4,68},{68... | collective-permute-start | bytes 884744 | tf_op jit(solution)/shard_map/ppermute | solution.py:624
  56.6 0.7 copy-start.13
  57.3 2.3 %collective-permute-start.14 = (bf16[144,1024]{1,0:T(8,128)(2,1)S(1)}, bf16[144,1024]{1,0:T(8,128)(2,1)S(1)}, u32[]{:S(2)}, u32[]{:S(2)}) collective-permute-start(bf16[144,1024]{1,0:T(8,128)(2,1)S(1)} %collective-permute-done.10.refs_10_.refs_2_), channel_id=1, source_target_pairs={{0,64},{64,0},{1,65},{65,1},{2,66},{66,2},{3,67},{67,3},{4,68},{68... | collective-permute-start | bytes 884744 | tf_op jit(solution)/shard_map/ppermute | solution.py:624
  57.7 1.9 %collective-permute-start.15 = (bf16[144,1024]{1,0:T(8,128)(2,1)S(1)}, bf16[144,1024]{1,0:T(8,128)(2,1)S(1)}, u32[]{:S(2)}, u32[]{:S(2)}) collective-permute-start(bf16[144,1024]{1,0:T(8,128)(2,1)S(1)} %collective-permute-done.11.refs_11_.refs_3_), channel_id=1, source_target_pairs={{0,64},{64,0},{1,65},{65,1},{2,66},{66,2},{3,67},{67,3},{4,68},{68... | collective-permute-start | bytes 884744 | tf_op jit(solution)/shard_map/ppermute | solution.py:624
  58.9 1.8 %collective-permute-start.16 = (bf16[4,32,1024]{2,1,0:T(8,128)(2,1)S(1)}, bf16[4,32,1024]{2,1,0:T(8,128)(2,1)S(1)}, u32[]{:S(2)}, u32[]{:S(2)}) collective-permute-start(bf16[4,32,1024]{2,1,0:T(8,128)(2,1)S(1)} %slice_select_fusion), channel_id=1, source_target_pairs={{0,64},{64,0},{1,65},{65,1},{2,66},{66,2},{3,67},{67,3},{4,68},{68... | collective-permute-start | bytes 786440 | tf_op jit(solution)/shard_map/ppermute | solution.py:626
  60.8 1.7 copy-start
  62.5 0.9 copy-start.8
  63.5 0.9 copy-start.10
  64.4 0.9 copy-start.12
  65.4 0.9 copy-start.14
  77.7 6.8 %copy-start.2 = (bf16[1024,1024]{1,0:T(8,128)(2,1)}, bf16[1024,1024]{1,0:T(8,128)(2,1)S(1)}, u32[]{:S(2)}) copy-start(bf16[1024,1024]{1,0:T(8,128)(2,1)S(1)} %get-tuple-element.51.normed_in.normed) | copy-start | bytes 6291460
  77.7 2.0 %collective-permute-start.17 = (f32[1024,128]{1,0:T(8,128)S(1)}, f32[1024,128]{1,0:T(8,128)S(1)}, u32[]{:S(2)}, u32[]{:S(2)}) collective-permute-start(f32[1024,128]{1,0:T(8,128)S(1)} %get-tuple-element.52.own.stats), channel_id=1, source_target_pairs={{0,64},{64,0},{1,65},{65,1},{2,66},{66,2},{3,67},{67,3},{4,68},{68... | collective-permute-start | bytes 1572872 | tf_op jit(solution)/shard_map/ppermute | solution.py:629
  82.8 1.6 collective-permute-start.18
  91.8 1.6 copy-start.4
  93.4 1.4 copy-start.5
  94.7 1.7 copy-start.1
  96.5 1.6 copy-start.3
  98.1 1.6 copy-start.6
  104.0 2.7 %collective-permute-start.19 = (bf16[512,1024]{1,0:T(8,128)(2,1)S(1)}, bf16[512,1024]{1,0:T(8,128)(2,1)S(1)}, u32[]{:S(2)}, u32[]{:S(2)}) collective-permute-start(bf16[512,1024]{1,0:T(8,128)(2,1)S(1)} %get-tuple-element.62), channel_id=1, source_target_pairs={{0,64},{64,0},{1,65},{65,1},{2,66},{66,2},{3,67},{67,3},{4,68},{68... | collective-permute-start | bytes 3145736 | tf_op jit(solution)/shard_map/ppermute | solution.py:635
  107.0 13.9 %collective-permute-start.20 = (bf16[128,1024]{1,0:T(8,128)(2,1)S(1)}, bf16[128,1024]{1,0:T(8,128)(2,1)S(1)}, u32[]{:S(2)}, u32[]{:S(2)}) collective-permute-start(bf16[128,1024]{1,0:T(8,128)(2,1)S(1)} %get-tuple-element.63), channel_id=1, source_target_pairs={{0,0},{16,8},{32,16},{48,24},{64,32},{80,40},{96,48},{112,56},{8,6... | collective-permute-start | bytes 786440 | tf_op jit(solution)/shard_map/ppermute | solution.py:636
  109.5 16.7 %collective-permute-start.21 = (bf16[128,1024]{1,0:T(8,128)(2,1)S(1)}, bf16[128,1024]{1,0:T(8,128)(2,1)S(1)}, u32[]{:S(2)}, u32[]{:S(2)}) collective-permute-start(bf16[128,1024]{1,0:T(8,128)(2,1)S(1)} %get-tuple-element.64), channel_id=1, source_target_pairs={{16,0},{0,8},{48,16},{32,24},{80,32},{64,40},{112,48},{96,56},{24,... | collective-permute-start | bytes 786440 | tf_op jit(solution)/shard_map/ppermute | solution.py:636
  113.5 13.7 %collective-permute-start.22 = (bf16[128,1024]{1,0:T(8,128)(2,1)S(1)}, bf16[128,1024]{1,0:T(8,128)(2,1)S(1)}, u32[]{:S(2)}, u32[]{:S(2)}) collective-permute-start(bf16[128,1024]{1,0:T(8,128)(2,1)S(1)} %get-tuple-element.65), channel_id=1, source_target_pairs={{32,0},{48,8},{0,16},{16,24},{96,32},{112,40},{64,48},{80,56},{40,... | collective-permute-start | bytes 786440 | tf_op jit(solution)/shard_map/ppermute | solution.py:636
  117.0 16.8 %collective-permute-start.23 = (bf16[128,1024]{1,0:T(8,128)(2,1)S(1)}, bf16[128,1024]{1,0:T(8,128)(2,1)S(1)}, u32[]{:S(2)}, u32[]{:S(2)}) collective-permute-start(bf16[128,1024]{1,0:T(8,128)(2,1)S(1)} %get-tuple-element.66), channel_id=1, source_target_pairs={{48,0},{32,8},{16,16},{0,24},{112,32},{96,40},{80,48},{64,56},{56,... | collective-permute-start | bytes 786440 | tf_op jit(solution)/shard_map/ppermute | solution.py:636
  161.2 8.4 %collective-permute-start.24 = (bf16[1408,128]{1,0:T(8,128)(2,1)S(1)}, bf16[1408,128]{1,0:T(8,128)(2,1)S(1)}, u32[]{:S(2)}, u32[]{:S(2)}) collective-permute-start(bf16[1408,128]{1,0:T(8,128)(2,1)S(1)} %bitcast.4), channel_id=1, source_target_pairs={{0,64},{64,0},{1,65},{65,1},{2,66},{66,2},{3,67},{67,3},{4,68},{68... | collective-permute-start | bytes 1081352 | tf_op jit(solution)/shard_map/ppermute | solution.py:646
Sparse Core Ops, SparseCore 0:
  10.6 43.1 all-gather.1
  94.9 40.4 reduce-scatter.1

commit v5 on v4

--- a/solution.py
+++ b/solution.py
@@ -22,6 +22,7 @@
 ANY = pl.BlockSpec(memory_space=pl.ANY)
 VM = pl.BlockSpec(memory_space=pltpu.VMEM)
 SM = pl.BlockSpec(memory_space=pltpu.SMEM)
+HB = pl.BlockSpec(memory_space=pltpu.HBM)
 
 
 def params(mib):
@@ -62,43 +63,59 @@
     return e, p, core
 
 
-def prepare_kernel(plan, lay, w_in, w_out, *refs):
-    outs, wsel, sem = refs[:4], refs[4], refs[5]
+def weights_kernel(w_in, w_out, wsel, sem):
     h = lax.axis_index("core")
-    weights = [
+    copies = [
         pltpu.make_async_copy(
             w_in.at[:, rows(512 * c + 256 * h, 256)],
             wsel.at[pl.ds(0, 128), pl.ds(256 * c, 256)],
-            sem.at[4 + c],
+            sem.at[c],
         )
         for c in range(4)
     ] + [
         pltpu.make_async_copy(
             w_out.at[pl.ds(32 * r, 32), rows(512 * h, 512)],
             wsel.at[pl.ds(128, 32), pl.ds(512 * r, 512)],
-            sem.at[8 + r],
+            sem.at[4 + r],
         )
         for r in range(2)
     ]
-    copies = weights + [
-        pltpu.make_async_copy(
-            lay.at[plan[jnp.bitwise_xor(lax.axis_index("x"), k)]], outs[k], sem.at[k]
-        )
-        for k in range(4)
-    ]
     run_copies(copies)
 
 
-def prepare(plan, lay, w_in, w_out):
-    return pl.pallas_call(
-        prepare_kernel,
-        out_shape=[shape((128, D), BF)] * 4 + [shape((160, D), BF)],
-        in_specs=[SM, ANY, ANY, ANY],
-        out_specs=[VM] * 5,
-        scratch_shapes=[pltpu.SemaphoreType.DMA((10,))],
+def own_weights(w_in, w_out):
+    return pl.pallas_call(
+        weights_kernel,
+        out_shape=shape((160, D), BF),
+        in_specs=[HB, HB],
+        out_specs=VM,
+        scratch_shapes=[pltpu.SemaphoreType.DMA((6,))],
         compiler_params=params(60),
-        name="prepare",
-    )(plan, lay, w_in, w_out)
+        name="own_weights",
+    )(w_in, w_out)
+
+
+def deal_kernel(plan, lay, *refs):
+    outs, sem = refs[:4], refs[4]
+    x = lax.axis_index("x")
+    run_copies(
+        [
+            pltpu.make_async_copy(lay.at[plan[jnp.bitwise_xor(x, k)]], outs[k], sem.at[k])
+            for k in range(4)
+        ]
+    )
+
+
+def deal(plan, lay):
+    return pl.pallas_call(
+        deal_kernel,
+        out_shape=[shape((128, D), BF)] * 4,
+        in_specs=[SM, HB],
+        out_specs=[VM] * 4,
+        scratch_shapes=[pltpu.SemaphoreType.DMA((4,))],
+        compiler_params=params(60),
+        name="deal",
+    )(plan, lay)
 
 
 def pick_kernel(lengths, grad, stamps, *refs):
@@ -126,10 +143,10 @@
     return pl.pallas_call(
         pick_kernel,
         out_shape=[shape((144, D), BF)] * 4,
-        in_specs=[SM, ANY, VM],
+        in_specs=[SM, HB, VM],
         out_specs=[VM] * 4,
         scratch_shapes=[pltpu.SemaphoreType.DMA((4,))],
-        compiler_params=params(60),
+        compiler_params=params(24),
         name="pick",
     )(lengths, grad, stamps)
 
@@ -160,9 +177,9 @@
 
 
 def forward_kernel(tb, *refs):
-    xs, gs, wag, wrecv = refs[:8], refs[8:16], refs[16], refs[17]
-    normed, act, slope, probs, pslope, mixed, dz, stats = refs[18:26]
-    x, w, nv, av, sv, pv, qv, grad, wo, small, scol, srow, sem, out_sem = refs[26:]
+    xs, gs, wag = refs[:8], refs[8:16], refs[16]
+    nv, av, sv, pv, qv, mixed, stats = refs[17:24]
+    x, w, small, scol, srow, sem = refs[24:]
     e, p, h = unit_of()
     copies = load_weights(wag, w, sem, 0)
     for k in range(8):
@@ -178,31 +195,7 @@
                 sem.at[16 + k],
             )
         )
-    late = load_grad(gs, grad, p, h, sem, 24)
-    for q in range(4):
-        for r in range(2):
-            own = wag.at[
-                pl.ds(pl.multiple_of((4 * h + q) * 160 + 128, 32), 32), pl.ds(512 * r, 512)
-            ]
-            other = wrecv.at[q, :, pl.ds(512 * r, 512)]
-            to = pl.ds(64 * q + 32 * r, 32)
-            n = 32 + 4 * q + 2 * r
-            late.append(
-                pltpu.make_async_copy(own, wo.at[to, rows(h * 512, 512)], sem.at[n])
-            )
-            late.append(
-                pltpu.make_async_copy(other, wo.at[to, rows((1 - h) * 512, 512)], sem.at[n + 1])
-            )
-    for c in copies + late:
-        c.start()
-    for c in copies:
-        c.wait()
-    leaving = []
-
-    def leave(source, target):
-        c = pltpu.make_async_copy(source, target, out_sem.at[len(leaving)])
-        c.start()
-        leaving.append(c)
+    run_copies(copies)
 
     for i in range(NQ):
         at = pl.ds(i * BQ, BQ)
@@ -218,8 +211,6 @@
             sg = jax.nn.sigmoid(hidden)
             av[at, cols] = (hidden * sg).astype(BF)
             sv[at, cols] = (sg * (1.0 + hidden * (1.0 - sg))).astype(BF)
-        for source, target in ((nv, normed), (av, act), (sv, slope)):
-            leave(source.at[at], target.at[at])
 
     for b in range(8):
         tile = small[b].astype(F32)
@@ -256,65 +247,80 @@
             pv[at, cols] = (s * sg * live).astype(BF)
             qv[at, cols] = (sg * (1.0 + s * (1.0 - sg)) * live).astype(BF)
         upto = (i + 1) * BQ
-        for source, target in ((pv, probs), (qv, pslope)):
-            leave(source.at[at, pl.ds(0, upto)], target.at[at, pl.ds(0, upto)])
         mixed[at, :] = nn(pv[at, 0:upto], av[0:upto, 256:512])
         stats[at, :] = jnp.where(lane == 5, si, stats[at, :])
-    for c in late:
-        c.wait()
+
+
+def forward(tb, xs, gs, wag):
+    return pl.pallas_call(
+        forward_kernel,
+        out_shape=[shape((L, D), BF)] * 3
+        + [shape((L, L), BF)] * 2
+        + [shape((L, DH), F32), shape((L, 128), F32)],
+        in_specs=[VM] + [HB] * 17,
+        out_specs=[VM] * 7,
+        scratch_shapes=[
+            pltpu.VMEM((L, D), BF),
+            pltpu.VMEM((D, D), BF),
+            pltpu.VMEM((8, 16, 128), BF),
+            pltpu.VMEM((L, 128), F32),
+            pltpu.VMEM((8, L), F32),
+            pltpu.SemaphoreType.DMA((24,)),
+        ],
+        compiler_params=params(28),
+        name="forward",
+    )(tb, *xs, *gs, wag)
+
+
+def statistics_kernel(mixed, gate, base, *refs):
+    gs, wag, wrecv = refs[:8], refs[8], refs[9]
+    dz, stats, grad, wo, sem = refs[10:]
+    _, p, h = unit_of()
+    copies = load_grad(gs, grad, p, h, sem, 0)
+    for q in range(4):
+        for r in range(2):
+            own = wag.at[
+                pl.ds(pl.multiple_of((4 * h + q) * 160 + 128, 32), 32), pl.ds(512 * r, 512)
+            ]
+            other = wrecv.at[q, :, pl.ds(512 * r, 512)]
+            to = pl.ds(64 * q + 32 * r, 32)
+            n = 8 + 4 * q + 2 * r
+            copies.append(pltpu.make_async_copy(own, wo.at[to, rows(h * 512, 512)], sem.at[n]))
+            copies.append(
+                pltpu.make_async_copy(other, wo.at[to, rows((1 - h) * 512, 512)], sem.at[n + 1])
+            )
+    run_copies(copies)
+    lane = lax.broadcasted_iota(jnp.int32, (BQ, 128), 1)
     for i in range(NQ):
         at = pl.ds(i * BQ, BQ)
         d = nt(grad[at, :], wo[...])
         dz[at, :] = d
-        gated = mixed[at, :] * av[at, 0:256].astype(F32)
+        gated = mixed[at, :] * gate[at, 0:256].astype(F32)
         m = jnp.mean(gated, axis=-1, keepdims=True)
         centred = gated - m
         m2 = jnp.sum(centred * centred, axis=-1, keepdims=True)
         s3 = jnp.sum(d, axis=-1, keepdims=True)
         s4 = jnp.sum(d * centred, axis=-1, keepdims=True)
-        row = stats[at, :]
+        row = base[at, :]
         for n, value in enumerate((m, m2, s3, s4)):
             row = jnp.where(lane == n, value, row)
         stats[at, :] = row
-    for c in leaving:
-        c.wait()
-
-
-def forward(tb, xs, gs, wag, wrecv):
-    return pl.pallas_call(
-        forward_kernel,
-        out_shape=[shape((L, D), BF)] * 3
-        + [shape((L, L), BF)] * 2
-        + [shape((L, DH), F32)] * 2
-        + [shape((L, 128), F32)],
-        in_specs=[VM] + [ANY] * 18,
-        out_specs=[ANY] * 5 + [VM] * 3,
+
+
+def statistics(mixed, act, base, gs, wag, wrecv):
+    return pl.pallas_call(
+        statistics_kernel,
+        out_shape=[shape((L, DH), F32), shape((L, 128), F32)],
+        in_specs=[VM, VM, VM] + [HB] * 10,
+        out_specs=[VM, VM],
         scratch_shapes=[
             pltpu.VMEM((L, D), BF),
-            pltpu.VMEM((D, D), BF),
-            pltpu.VMEM((L, D), BF),
-            pltpu.VMEM((L, D), BF),
-            pltpu.VMEM((L, D), BF),
-            pltpu.VMEM((L, L), BF),
-            pltpu.VMEM((L, L), BF),
-            pltpu.VMEM((L, D), BF),
             pltpu.VMEM((DH, D), BF),
-            pltpu.VMEM((8, 16, 128), BF),
-            pltpu.VMEM((L, 128), F32),
-            pltpu.VMEM((8, L), F32),
-            pltpu.SemaphoreType.DMA((48,)),
-            pltpu.SemaphoreType.DMA((20,)),
+            pltpu.SemaphoreType.DMA((24,)),
         ],
-        compiler_params=params(34),
-        name="forward",
-    )(tb, *xs, *gs, wag, wrecv)
-
-
-def whole(*dims):
-    return pl.BlockSpec(dims, lambda i: (0,) * len(dims))
-
-
-FIRST = pl.BlockSpec((L, DH), lambda i: (0, 0))
+        compiler_params=params(16),
+        name="statistics",
+    )(mixed, act, base, *gs, wag, wrecv)
 
 
 def middle_kernel(own, peer, mixed, dz, gate, gslope, *refs):
@@ -335,12 +341,12 @@
         cross = a[:, 3:4] + b[:, 3:4] + gap * (a[:, 2:3] - b[:, 2:3])
         cross = cross * r * (1.0 / 512.0)
         mix = mixed[at, :]
-        u = gate[at, :].astype(F32)
+        u = gate[at, 0:256].astype(F32)
         zhat = (mix * u - mean) * r
         zl[at, :] = zhat.astype(BF)
         dgated = r * (dz[at, :] - dmean - zhat * cross)
         datt[at, :] = (dgated * u).astype(BF)
-        dhu[at, :] = (dgated * mix * gslope[at, :].astype(F32)).astype(BF)
+        dhu[at, :] = (dgated * mix * gslope[at, 0:256].astype(F32)).astype(BF)
     for c in copies:
         c.wait()
     out = tn(zl[...], grad[...]).astype(BF)
@@ -366,11 +372,9 @@
 def middle(own, peer, mixed, dz, act, slope, gs):
     return pl.pallas_call(
         middle_kernel,
-        grid=(1,),
         out_shape=[shape((L, DH), BF)] * 2 + [shape((4, 32, D), BF)] * 2,
-        in_specs=[whole(L, 128), whole(L, 128), whole(L, DH), whole(L, DH), FIRST, FIRST]
-        + [ANY] * 8,
-        out_specs=[whole(L, DH), whole(L, DH), whole(4, 32, D), whole(4, 32, D)],
+        in_specs=[VM] * 6 + [HB] * 8,
+        out_specs=[VM] * 4,
         scratch_shapes=[
             pltpu.VMEM((L, DH), BF),
             pltpu.VMEM((L, D), BF),
@@ -382,25 +386,16 @@
 
 
 def backward_kernel(
-    act_in, slope_in, probs_in, pslope_in, normed_in, datt, dhu, stats, keep, recv, *refs
+    act, slope, probs, pslope, normed, datt, dhu, stats, keep, recv, *refs
 ):
-    part, dhid_out, act, slope, probs, pslope, normed, dhid, dlow, hot, sem = refs
+    part_out, dhid_out, part, dhid, dlow, hot, sem = refs
     h = lax.axis_index("core")
-    sources = (act_in, pslope_in, slope_in, probs_in, normed_in)
-    targets = (act, pslope, slope, probs, normed)
-    copies = [
-        pltpu.make_async_copy(a, b, sem.at[n]) for n, (a, b) in enumerate(zip(sources, targets))
-    ]
-    for c in copies:
-        c.start()
     stamp_lane = lax.broadcasted_iota(jnp.int32, (L, 256), 1).astype(F32)
     hot[...] = jnp.where(stats[:, 5:6] == stamp_lane, 1.0, 0.0).astype(BF)
     dhid[:, 0:256] = dhu[...]
     bucket = lax.broadcasted_iota(jnp.int32, (BQ, 128), 1)
     time = lax.broadcasted_iota(jnp.int32, (BQ, 256), 1)
     total = jnp.zeros((BQ, 128), F32)
-    for c in copies[:3]:
-        c.wait()
     for i in range(NQ):
         at = pl.ds(i * BQ, BQ)
         upto = (i + 1) * BQ
@@ -421,7 +416,6 @@
         picked = jnp.where(when >= 128, late, jnp.where(when >= 0, early, 0.0))
         far = jnp.sum(jnp.where(time <= si - 127, by_time, 0.0), axis=-1, keepdims=True)
         total = total + jnp.where(bucket == 127, far, picked)
-    copies[3].wait()
     for j in range(NQ):
         cols = pl.ds(j * BQ, BQ)
         frm = j * BQ
@@ -429,16 +423,8 @@
         dhid[cols, 256:512] = (dv * slope[cols, 256:512].astype(F32)).astype(BF)
         dk = tn(dlow[frm:, cols], act[frm:, 512:768]) * (DH**-0.5)
         dhid[cols, 768:1024] = (dk * slope[cols, 768:1024].astype(F32)).astype(BF)
-    leaving = pltpu.make_async_copy(dhid, dhid_out, sem.at[5])
-    leaving.start()
-    copies[4].wait()
-    for b in range(4):
-        pin = tn(normed[:, 256 * b : 256 * b + 256], dhid[...]).astype(BF)
-        for z in range(2):
-            for t in range(8):
-                part[pl.ds((2 * b + z) * SHARD + 128 * t, 128), :] = pin[
-                    128 * z : 128 * z + 128, 128 * t : 128 * t + 128
-                ]
+    leaving = [pltpu.make_async_copy(dhid, dhid_out, sem.at[4])]
+    leaving[0].start()
     bias = jnp.sum(total, axis=0, keepdims=True)
     high = bias.astype(BF).astype(F32)
     line = lax.broadcasted_iota(jnp.int32, (128, 128), 0)
@@ -451,36 +437,58 @@
             theirs = pl.multiple_of((4 * (1 - h) + q) * SHARD + 1024 + 32 * t, 32)
             part[pl.ds(mine, 32), :] = keep[q, :, 128 * t : 128 * t + 128]
             part[pl.ds(theirs, 32), :] = recv[q, :, 128 * t : 128 * t + 128]
-    leaving.wait()
+    for b in range(4):
+        pin = tn(normed[:, 256 * b : 256 * b + 256], dhid[...]).astype(BF)
+        for z in range(2):
+            for t in range(8):
+                part[pl.ds((2 * b + z) * SHARD + 128 * t, 128), :] = pin[
+                    128 * z : 128 * z + 128, 128 * t : 128 * t + 128
+                ]
+        two = pl.ds(2 * b * SHARD, 2 * SHARD)
+        leaving.append(pltpu.make_async_copy(part.at[two], part_out.at[two], sem.at[b]))
+        leaving[-1].start()
+    for c in leaving:
+        c.wait()
 
 
 def backward(act, slope, probs, pslope, normed, datt, dhu, stats, keep, recv):
     return pl.pallas_call(
         backward_kernel,
         out_shape=[shape((8 * SHARD, 128), BF), shape((L, D), BF)],
-        in_specs=[ANY] * 5 + [VM] * 5,
-        out_specs=[VM, ANY],
+        in_specs=[VM] * 10,
+        out_specs=[HB, HB],
         scratch_shapes=[
-            pltpu.VMEM((L, D), BF),
-            pltpu.VMEM((L, D), BF),
-            pltpu.VMEM((L, L), BF),
-            pltpu.VMEM((L, L), BF),
-            pltpu.VMEM((L, D), BF),
+            pltpu.VMEM((8 * SHARD, 128), BF),
             pltpu.VMEM((L, D), BF),
             pltpu.VMEM((L, L), BF),
             pltpu.VMEM((L, 256), BF),
-            pltpu.SemaphoreType.DMA((6,)),
+            pltpu.SemaphoreType.DMA((5,)),
         ],
-        compiler_params=params(34),
+        compiler_params=params(28),
         name="backward",
     )(act, slope, probs, pslope, normed, datt, dhu, stats, keep, recv)
 
 
-def input_kernel(dhid, normed, stats, wag, own, other, w, sem):
+def input_kernel(dhid_in, normed_in, stats, wag, own, other, dhid, normed, w, sem):
     h = lax.axis_index("core")
-    run_copies(load_weights(wag, w, sem, 0))
+    copies = load_weights(wag, w, sem, 0)
+    blocks = []
     for i in range(NQ):
         at = pl.ds(i * BQ, BQ)
+        blocks.append(
+            [
+                pltpu.make_async_copy(dhid_in.at[at], dhid.at[at], sem.at[8 + 2 * i]),
+                pltpu.make_async_copy(normed_in.at[at], normed.at[at], sem.at[9 + 2 * i]),
+            ]
+        )
+    for c in copies + sum(blocks, []):
+        c.start()
+    for c in copies:
+        c.wait()
+    for i in range(NQ):
+        at = pl.ds(i * BQ, BQ)
+        for c in blocks[i]:
+            c.wait()
         dn = nt(dhid[at, :], w[...])
         n = normed[at, :].astype(F32)
         r = stats[at, 4:5]
@@ -502,9 +510,14 @@
     return pl.pallas_call(
         input_kernel,
         out_shape=[shape((512, D), BF)] * 2,
-        in_specs=[VM] * 3 + [ANY],
+        in_specs=[HB, ANY, VM, HB],
         out_specs=[VM, VM],
-        scratch_shapes=[pltpu.VMEM((D, D), BF), pltpu.SemaphoreType.DMA((8,))],
+        scratch_shapes=[
+            pltpu.VMEM((L, D), BF),
+            pltpu.VMEM((L, D), BF),
+            pltpu.VMEM((D, D), BF),
+            pltpu.SemaphoreType.DMA((16,)),
+        ],
         compiler_params=params(20),
         name="input_grad",
     )(dhid, normed, stats, wag)
@@ -615,8 +628,8 @@
     first = lax.axis_index("core") == 0
     swap = functools.partial(lax.ppermute, axis_name="core", perm=[(0, 1), (1, 0)])
 
-    *chunks, wsel = prepare(repack_plan, layer_in, w_in, w_out)
-    wag = lax.all_gather(wsel, "z", axis=0, tiled=True)
+    wag = lax.all_gather(own_weights(w_in, w_out), "z", axis=0, tiled=True)
+    chunks = deal(repack_plan, layer_in)
     xs = [lax.ppermute(c, PLANE, input_pairs(k)) for k, c in enumerate(chunks)]
     picked = pick(lengths, grad_out, stamps)
     gs = [lax.ppermute(c, PLANE, grad_pairs(k)) for k, c in enumerate(picked)]
@@ -625,7 +638,8 @@
     w3 = wag.reshape(8, 160, D)
     wrecv = swap(jnp.where(first, w3[4:, 128:], w3[:4, 128:]))
 
-    normed, act, slope, probs, pslope, mixed, dz, stats = forward(time_bias, xs, gs, wag, wrecv)
+    normed, act, slope, probs, pslope, mixed, base = forward(time_bias, xs, gs, wag)
+    dz, stats = statistics(mixed, act, base, gs, wag, wrecv)
     datt, dhu, keep, send = middle(stats, swap(stats), mixed, dz, act, slope, gs)
     part, dhid = backward(
         act, slope, probs, pslope, normed, datt, dhu, stats, keep, swap(send)

time: 179 us -> 175 us (0.978)
  Pallas kernels: 34.8 us -> 32 us
  local copies, waits for them, and re-layouts: 15.5 us -> 12.9 us
    pallas_call x1, Pallas kernels: 11.4 us -> 7.04 us  [forward(): pl.pallas_call(forward_kernel, out_shape=[shape((L, D), BF)] * 3 + [shape...]
    pallas_call x2 -> x4, Pallas kernels: 6.28 us -> 9.02 us  [the longest x1 2.88 us: deal(): pl.pallas_call(deal_kernel, out_shape=[shape((128, D), BF)] * 4, in_specs...]
    unnamed x32 -> x30, local copies, waits for them, and re-layouts: 15.5 us -> 12.9 us
    pallas_call x1, Pallas kernels: 2.92 us -> 0.68 us  [pick(): pl.pallas_call(pick_kernel, out_shape=[shape((144, D), BF)] * 4, in_specs...]
    ppermute x4, starting transfers between devices: 14.6 us -> 16.7 us  [local(): xs = [lax.ppermute(c, PLANE, input_pairs(k)) for k, c in enumerate(chunks)]]
  transfers between devices with their start and end apart: 27 -> 27, of which waited for: 10 -> 8; matrix products, arithmetic and copies ran while one was open for 1% -> 1% of each run, Pallas kernels for 5% -> 10%
where the time goes in v5:
time: 175 us; the launch traced here: 174 us
  starting transfers between devices  64.8 us (37%)
  Pallas kernels  32 us (18%)
  blocking collectives  25.4 us (15%)
  waiting for transfers between devices  23.3 us (13%)
  between operations  14.4 us (8%)
  local copies, waits for them, and re-layouts  12.9 us (7%)
    all_to_all x2, blocking collectives, exchange(): return lax.all_to_all(v, CHIPS, split_axis=0, concat_axis=0, tiled=True)  25.4 us
    ppermute x4, starting transfers between devices, local(): xs = [lax.ppermute(c, PLANE, input_pairs(k)) for k, c in enumerate(chunks)]  16.7 us
    ppermute x4, waiting for transfers between devices, local(): back = [lax.ppermute(pieces[k], PLANE, back_pairs(k)) for k in range(4)]  13.9 us
    ppermute x4, starting transfers between devices, local(): gs = [lax.ppermute(c, PLANE, grad_pairs(k)) for k, c in enumerate(picked)]  13.8 us
    ppermute x4, starting transfers between devices, local(): back = [lax.ppermute(pieces[k], PLANE, back_pairs(k)) for k in range(4)]  13.1 us
    unnamed x30, local copies, waits for them, and re-layouts  12.9 us
    ppermute x4, starting transfers between devices, local(): xs = xs + [swap(c) for c in xs]  10.3 us
    pallas_call x1, Pallas kernels, backward(): pl.pallas_call(backward_kernel, out_shape=[shape((8 * SHARD, 128), BF), s...  8.09 us
  transfers between devices with their start and end apart: 27, of which 8 were waited for; matrix products, arithmetic and copies ran while one was open for 1% of the time, Pallas kernels for 10%

profile of v5, /device:TPU:1, one launch (start us, length us, event | category | flops | bytes accessed | tf_op | source)
XLA Modules:
  0.0 173.9 jit_solution(417918435254673433)
XLA Ops:
  7.2 0.0 all-gather.2.cloned.1.call-start
  7.3 1.8 %own_weights.1 = bf16[160,1024]{1,0:T(8,128)(2,1)} custom-call(bf16[128,2048]{1,0:T(8,128)(2,1)} %w_in.1, bf16[64,1024]{1,0:T(8,128)(2,1)} %w_out.1), custom_call_target="tpu_custom_call" | custom-call | tf_op jit(solution)/shard_map/own_weights/pallas_call | solution.py:87
  9.1 0.0 all-gather.2.cloned.1.call-update
  9.1 0.0 reduce-scatter.2.cloned.1.call-start
  9.1 2.9 %deal.1 = (bf16[128,1024]{1,0:T(8,128)(2,1)}, bf16[128,1024]{1,0:T(8,128)(2,1)}, bf16[128,1024]{1,0:T(8,128)(2,1)}, bf16[128,1024]{1,0:T(8,128)(2,1)}) custom-call(s32[4]{0:T(128)} %plan.1, bf16[4,128,1024]{2,1,0:T(8,128)(2,1)} %lay.1), custom_call_target="tpu_custom_call" | custom-call | tf_op jit(solution)/shard_map/deal/pallas_call | solution.py:110
  12.0 6.0 %collective-permute-start = (bf16[128,1024]{1,0:T(8,128)(2,1)}, bf16[128,1024]{1,0:T(8,128)(2,1)S(1)}, u32[]{:S(2)}, u32[]{:S(2)}) collective-permute-start(bf16[128,1024]{1,0:T(8,128)(2,1)} %get-tuple-element.38), channel_id=1, source_target_pairs={{0,0},{8,8},{16,144},{24,152},{32,64},{40,72},{48,208},{56,216},{6... | collective-permute-start | bytes 786440 | tf_op jit(solution)/shard_map/ppermute | solution.py:633
  18.1 3.0 %collective-permute-start.1 = (bf16[128,1024]{1,0:T(8,128)(2,1)}, bf16[128,1024]{1,0:T(8,128)(2,1)S(1)}, u32[]{:S(2)}, u32[]{:S(2)}) collective-permute-start(bf16[128,1024]{1,0:T(8,128)(2,1)} %get-tuple-element.39), channel_id=1, source_target_pairs={{0,8},{8,0},{16,152},{24,144},{32,72},{40,64},{48,216},{56,208},{6... | collective-permute-start | bytes 786440 | tf_op jit(solution)/shard_map/ppermute | solution.py:633
  21.1 1.9 %collective-permute-start.2 = (bf16[128,1024]{1,0:T(8,128)(2,1)}, bf16[128,1024]{1,0:T(8,128)(2,1)S(1)}, u32[]{:S(2)}, u32[]{:S(2)}) collective-permute-start(bf16[128,1024]{1,0:T(8,128)(2,1)} %get-tuple-element.40), channel_id=1, source_target_pairs={{0,144},{8,152},{16,0},{24,8},{32,208},{40,216},{48,64},{56,72},{6... | collective-permute-start | bytes 786440 | tf_op jit(solution)/shard_map/ppermute | solution.py:633
  23.0 0.7 pick.1
  23.7 3.8 %collective-permute-start.8 = (bf16[144,1024]{1,0:T(8,128)(2,1)S(1)}, bf16[144,1024]{1,0:T(8,128)(2,1)S(1)}, u32[]{:S(2)}, u32[]{:S(2)}) collective-permute-start(bf16[144,1024]{1,0:T(8,128)(2,1)S(1)} %get-tuple-element.42), channel_id=1, source_target_pairs={{0,0},{8,16},{16,32},{24,48},{32,64},{40,80},{48,96},{56,112},{64,... | collective-permute-start | bytes 884744 | tf_op jit(solution)/shard_map/ppermute | solution.py:635
  27.5 4.8 %collective-permute-start.9 = (bf16[144,1024]{1,0:T(8,128)(2,1)S(1)}, bf16[144,1024]{1,0:T(8,128)(2,1)S(1)}, u32[]{:S(2)}, u32[]{:S(2)}) collective-permute-start(bf16[144,1024]{1,0:T(8,128)(2,1)S(1)} %get-tuple-element.43), channel_id=1, source_target_pairs={{0,16},{8,0},{16,48},{24,32},{32,80},{40,64},{48,112},{56,96},{64,... | collective-permute-start | bytes 884744 | tf_op jit(solution)/shard_map/ppermute | solution.py:635
  32.2 0.0 collective-permute-done.refs_0_
  32.3 5.7 %collective-permute-start.3 = (bf16[128,1024]{1,0:T(8,128)(2,1)}, bf16[128,1024]{1,0:T(8,128)(2,1)S(1)}, u32[]{:S(2)}, u32[]{:S(2)}) collective-permute-start(bf16[128,1024]{1,0:T(8,128)(2,1)} %get-tuple-element.41), channel_id=1, source_target_pairs={{0,152},{8,144},{16,8},{24,0},{32,216},{40,208},{48,72},{56,64},{6... | collective-permute-start | bytes 786440 | tf_op jit(solution)/shard_map/ppermute | solution.py:633
  38.0 3.3 %collective-permute-start.10 = (bf16[144,1024]{1,0:T(8,128)(2,1)S(1)}, bf16[144,1024]{1,0:T(8,128)(2,1)S(1)}, u32[]{:S(2)}, u32[]{:S(2)}) collective-permute-start(bf16[144,1024]{1,0:T(8,128)(2,1)S(1)} %get-tuple-element.44), channel_id=1, source_target_pairs={{0,32},{8,48},{16,0},{24,16},{32,96},{40,112},{48,64},{56,80},{64,... | collective-permute-start | bytes 884744 | tf_op jit(solution)/shard_map/ppermute | solution.py:635
  41.2 1.4 collective-permute-done.2.refs_2_
  42.6 2.0 %collective-permute-start.11 = (bf16[144,1024]{1,0:T(8,128)(2,1)S(1)}, bf16[144,1024]{1,0:T(8,128)(2,1)S(1)}, u32[]{:S(2)}, u32[]{:S(2)}) collective-permute-start(bf16[144,1024]{1,0:T(8,128)(2,1)S(1)} %get-tuple-element.45), channel_id=1, source_target_pairs={{0,48},{8,32},{16,16},{24,0},{32,112},{40,96},{48,80},{56,64},{64,... | collective-permute-start | bytes 884744 | tf_op jit(solution)/shard_map/ppermute | solution.py:635
  44.6 5.4 %collective-permute-start.4 = (bf16[128,1024]{1,0:T(8,128)(2,1)S(1)}, bf16[128,1024]{1,0:T(8,128)(2,1)S(1)}, u32[]{:S(2)}, u32[]{:S(2)}) collective-permute-start(bf16[128,1024]{1,0:T(8,128)(2,1)S(1)} %collective-permute-done.refs_0_), channel_id=1, source_target_pairs={{0,64},{64,0},{1,65},{65,1},{2,66},{66,2},{3,67},{67,3},{4,68},{68... | collective-permute-start | bytes 786440 | tf_op jit(solution)/shard_map/ppermute | solution.py:636
  50.0 0.0 collective-permute-done.9.refs_9_.refs_1_
  50.0 0.5 collective-permute-start.6
  50.6 0.7 copy-done.8
  51.3 4.4 %collective-permute-start.7 = (bf16[128,1024]{1,0:T(8,128)(2,1)S(1)}, bf16[128,1024]{1,0:T(8,128)(2,1)}, u32[]{:S(2)}, u32[]{:S(2)}) collective-permute-start(bf16[128,1024]{1,0:T(8,128)(2,1)S(1)} %collective-permute-done.3.refs_3_), channel_id=1, source_target_pairs={{0,64},{64,0},{1,65},{65,1},{2,66},{66,2},{3,67},{67,3},{4,68},{68... | collective-permute-start | bytes 786440 | tf_op jit(solution)/shard_map/ppermute | solution.py:636
  55.6 1.5 collective-permute-start.12
  57.1 0.0 collective-permute-done.4.refs_4_
  57.2 0.0 copy-start.10
  57.2 0.7 copy-done.10
  57.9 0.5 collective-permute-start.14
  58.4 0.0 collective-permute-start.15
  58.4 1.1 slice_select_fusion
  59.5 0.8 collective-permute-start.16
  60.3 1.7 copy-done
  62.0 0.9 copy-done.9
  62.9 0.9 copy-done.11
  63.9 7.0 %forward.1 = (bf16[1024,1024]{1,0:T(8,128)(2,1)S(1)}, bf16[1024,1024]{1,0:T(8,128)(2,1)S(1)}, bf16[1024,1024]{1,0:T(8,128)(2,1)S(1)}, bf16[1024,1024]{1,0:T(8,12...) custom-call(bf16[2,128]{1,0:T(2,128)(2,1)S(1)} %copy-done.14, ...), custom_call_target="tpu_custom_call" | custom-call | tf_op jit(solution)/shard_map/forward/pallas_call | solution.py:255
  71.0 1.6 statistics.1
  72.6 0.2 collective-permute-start.17
  72.8 1.8 %collective-permute-done.17.peer = f32[1024,128]{1,0:T(8,128)S(1)} collective-permute-done((f32[1024,128]{1,0:T(8,128)S(1)}, f32[1024,128]{1,0:T(8,128)S(1)}, u32[]{:S(2)}, u32[]{:S(2)}) %collective-permute-start.17) | collective-permute-done | bytes 524320 | tf_op jit(solution)/shard_map/ppermute | solution.py:643
  74.6 2.7 %middle.1 = (bf16[1024,256]{1,0:T(8,128)(2,1)S(1)}, bf16[1024,256]{1,0:T(8,128)(2,1)S(1)}, bf16[4,32,1024]{2,1,0:T(8,128)(2,1)S(1)}, bf16[4,32,1024]{2,1,0:T(8,128)(2,1)S(1)}) custom-call(f32[1024,128]{1,0:T(8,128)S(1)} %get-tuple-element.53.own.stats, f32[1024,128]{1,0:T(8,128)S(1)} %collective-permute-done.17.peer, ...), custom_call_target="tpu_custom_call" | custom-call | tf_op jit(solution)/shard_map/middle/pallas_call | solution.py:373
  77.3 0.4 collective-permute-start.18
  77.8 1.4 collective-permute-done.18.recv
  79.2 8.1 %backward.1 = (bf16[11264,128]{1,0:T(8,128)(2,1)S(1)}, bf16[1024,1024]{1,0:T(8,128)(2,1)S(1)}) custom-call(bf16[1024,1024]{1,0:T(8,128)(2,1)S(1)} %get-tuple-element.46.gate.act, bf16[1024,1024]{1,0:T(8,128)(2,1)S(1)} %get-tuple-element.47.gslope.slope, bf16[1024,1024]{1,0:T(8,128)(2,1)S(1)} %get-tuple-element.48.probs, ...), custom_call_target="tpu_custom_call" | custom-call | tf_op jit(solution)/shard_map/backward/pallas_call | solution.py:455
  87.3 1.5 copy-done.4
  88.8 1.4 copy-done.5
  90.2 0.0 reduce-scatter.2.cloned.1.call-update
  90.2 1.7 copy-done.1
  91.9 1.6 copy-done.3
  93.5 1.6 copy-done.6
  95.1 4.7 %input_grad.1 = (bf16[512,1024]{1,0:T(8,128)(2,1)S(1)}, bf16[512,1024]{1,0:T(8,128)(2,1)S(1)}) custom-call(bf16[1024,1024]{1,0:T(8,128)(2,1)S(1)} %copy-done.6, bf16[1024,1024]{1,0:T(8,128)(2,1)S(1)} %copy-done.3, f32[1024,128]{1,0:T(8,128)S(1)} %get-tuple-element.53.own.stats, bf16[1280,1024]{1,0:T(8,128)(2,1)S(1)} %copy-done.1), custom_call_target="tpu_custom_call" | custom-call | tf_op jit(solution)/shard_map/input_grad/pallas_call | solution.py:510
  99.8 0.2 collective-permute-start.19
  100.0 2.5 %collective-permute-done.19.b = bf16[512,1024]{1,0:T(8,128)(2,1)S(1)} collective-permute-done((bf16[512,1024]{1,0:T(8,128)(2,1)S(1)}, bf16[512,1024]{1,0:T(8,128)(2,1)S(1)}, u32[]{:S(2)}, u32[]{:S(2)}) %collective-permute-start.19) | collective-permute-done | bytes 1048608 | tf_op jit(solution)/shard_map/ppermute | solution.py:649
  102.5 0.2 add_halves.1
  102.8 2.0 %collective-permute-start.20 = (bf16[128,1024]{1,0:T(8,128)(2,1)S(1)}, bf16[128,1024]{1,0:T(8,128)(2,1)S(1)}, u32[]{:S(2)}, u32[]{:S(2)}) collective-permute-start(bf16[128,1024]{1,0:T(8,128)(2,1)S(1)} %get-tuple-element.63), channel_id=1, source_target_pairs={{0,0},{16,8},{32,16},{48,24},{64,32},{80,40},{96,48},{112,56},{8,6... | collective-permute-start | bytes 786440 | tf_op jit(solution)/shard_map/ppermute | solution.py:650
  104.8 3.7 %collective-permute-start.21 = (bf16[128,1024]{1,0:T(8,128)(2,1)S(1)}, bf16[128,1024]{1,0:T(8,128)(2,1)S(1)}, u32[]{:S(2)}, u32[]{:S(2)}) collective-permute-start(bf16[128,1024]{1,0:T(8,128)(2,1)S(1)} %get-tuple-element.64), channel_id=1, source_target_pairs={{16,0},{0,8},{48,16},{32,24},{80,32},{64,40},{112,48},{96,56},{24,... | collective-permute-start | bytes 786440 | tf_op jit(solution)/shard_map/ppermute | solution.py:650
  108.5 4.4 %collective-permute-start.22 = (bf16[128,1024]{1,0:T(8,128)(2,1)S(1)}, bf16[128,1024]{1,0:T(8,128)(2,1)S(1)}, u32[]{:S(2)}, u32[]{:S(2)}) collective-permute-start(bf16[128,1024]{1,0:T(8,128)(2,1)S(1)} %get-tuple-element.65), channel_id=1, source_target_pairs={{32,0},{48,8},{0,16},{16,24},{96,32},{112,40},{64,48},{80,56},{40,... | collective-permute-start | bytes 786440 | tf_op jit(solution)/shard_map/ppermute | solution.py:650
  112.9 3.0 %collective-permute-start.23 = (bf16[128,1024]{1,0:T(8,128)(2,1)S(1)}, bf16[128,1024]{1,0:T(8,128)(2,1)S(1)}, u32[]{:S(2)}, u32[]{:S(2)}) collective-permute-start(bf16[128,1024]{1,0:T(8,128)(2,1)S(1)} %get-tuple-element.66), channel_id=1, source_target_pairs={{48,0},{32,8},{16,16},{0,24},{112,32},{96,40},{80,48},{64,56},{56,... | collective-permute-start | bytes 786440 | tf_op jit(solution)/shard_map/ppermute | solution.py:650
  115.9 6.3 %collective-permute-done.21.refs_1_ = bf16[128,1024]{1,0:T(8,128)(2,1)S(1)} collective-permute-done((bf16[128,1024]{1,0:T(8,128)(2,1)S(1)}, bf16[128,1024]{1,0:T(8,128)(2,1)S(1)}, u32[]{:S(2)}, u32[]{:S(2)}) %collective-permute-start.21) | collective-permute-done | bytes 262176 | tf_op jit(solution)/shard_map/ppermute | solution.py:650
  122.3 7.5 %collective-permute-done.23.refs_3_ = bf16[128,1024]{1,0:T(8,128)(2,1)S(1)} collective-permute-done((bf16[128,1024]{1,0:T(8,128)(2,1)S(1)}, bf16[128,1024]{1,0:T(8,128)(2,1)S(1)}, u32[]{:S(2)}, u32[]{:S(2)}) %collective-permute-start.23) | collective-permute-done | bytes 262176 | tf_op jit(solution)/shard_map/ppermute | solution.py:650
  129.8 1.1 place.1
  130.9 0.9 reduce-scatter.2.cloned.1.call-done
  131.8 14.8 %all_to_all.10 = bf16[16,88,128]{2,1,0:T(8,128)(2,1)S(1)} all-to-all(bf16[16,88,128]{2,1,0:T(8,128)(2,1)} %bitcast.6), channel_id=1, replica_groups=mesh['yh'=2,'core'=2,'yl'=2,'x'=4,'z'=8] {'yh','yl','x'}, dimensions={0} | all-to-all | bytes 720896 | tf_op jit(solution)/shard_map/all_to_all | solution.py:655
  146.6 0.1 reduce_sum.12
  146.7 10.7 %all_to_all.11 = bf16[16,88,128]{2,1,0:T(8,128)(2,1)S(1)} all-to-all(bf16[16,88,128]{2,1,0:T(8,128)(2,1)S(1)} %broadcast_in_dim.2), channel_id=1, replica_groups=mesh['yh'=2,'core'=2,'yl'=2,'x'=4,'z'=8] {'yh','yl','x'}, dimensions={0} | all-to-all | bytes 720896 | tf_op jit(solution)/shard_map/all_to_all | solution.py:655
  157.4 7.2 %collective-permute-start.24 = (bf16[1408,128]{1,0:T(8,128)(2,1)S(1)}, bf16[1408,128]{1,0:T(8,128)(2,1)S(1)}, u32[]{:S(2)}, u32[]{:S(2)}) collective-permute-start(bf16[1408,128]{1,0:T(8,128)(2,1)S(1)} %bitcast.4), channel_id=1, source_target_pairs={{0,64},{64,0},{1,65},{65,1},{2,66},{66,2},{3,67},{67,3},{4,68},{68... | collective-permute-start | bytes 1081352 | tf_op jit(solution)/shard_map/ppermute | solution.py:660
  164.6 1.3 collective-permute-done.24.theirs
  165.9 1.2 finish.1
  (38 shorter events, 0.1 us)
Async XLA Ops:
  7.2 15.8 %copy-start.7 = (bf16[4,128,1024]{2,1,0:T(8,128)(2,1)S(1)}, bf16[4,128,1024]{2,1,0:T(8,128)(2,1)}, u32[]{:S(2)}) copy-start(bf16[4,128,1024]{2,1,0:T(8,128)(2,1)} %grad.1) | copy-start | bytes 3145732
  7.2 15.8 %copy-start.12 = (s32[4,128]{1,0:T(4,128)S(1)}, s32[4,128]{1,0:T(4,128)}, u32[]{:S(2)}) copy-start(s32[4,128]{1,0:T(4,128)} %stamps.1) | copy-start | bytes 6148
  7.2 15.8 %copy-start.13 = (s32[4]{0:T(128)S(1)}, s32[4]{0:T(128)}, u32[]{:S(2)}) copy-start(s32[4]{0:T(128)} %lengths.1) | copy-start | bytes 52
  7.2 53.0 %copy-start.14 = (bf16[2,128]{1,0:T(2,128)(2,1)S(1)}, bf16[2,128]{1,0:T(2,128)(2,1)}, u32[]{:S(2)}) copy-start(bf16[2,128]{1,0:T(2,128)(2,1)} %tb.1) | copy-start | bytes 1540
  7.2 51.2 %all-gather.2.cloned.1.call-start = ((), (), s32[]{:S(2)}) async-start(), calls=%async_computation.3 | async-start | bytes 2949120 | tf_op jit(solution)/shard_map/all_gather | solution.py:631
  9.1 122.7 %reduce-scatter.2.cloned.1.call-start = ((), (), s32[]{:S(2)}) async-start(), calls=%async_computation.4 | async-start | bytes 3244032 | tf_op jit(solution)/shard_map/reduce_scatter | solution.py:647
  12.0 20.2 %collective-permute-start = (bf16[128,1024]{1,0:T(8,128)(2,1)}, bf16[128,1024]{1,0:T(8,128)(2,1)S(1)}, u32[]{:S(2)}, u32[]{:S(2)}) collective-permute-start(bf16[128,1024]{1,0:T(8,128)(2,1)} %get-tuple-element.38), channel_id=1, source_target_pairs={{0,0},{8,8},{16,144},{24,152},{32,64},{40,72},{48,208},{56,216},{6... | collective-permute-start | bytes 786440 | tf_op jit(solution)/shard_map/ppermute | solution.py:633
  18.1 19.9 %collective-permute-start.1 = (bf16[128,1024]{1,0:T(8,128)(2,1)}, bf16[128,1024]{1,0:T(8,128)(2,1)S(1)}, u32[]{:S(2)}, u32[]{:S(2)}) collective-permute-start(bf16[128,1024]{1,0:T(8,128)(2,1)} %get-tuple-element.39), channel_id=1, source_target_pairs={{0,8},{8,0},{16,152},{24,144},{32,72},{40,64},{48,216},{56,208},{6... | collective-permute-start | bytes 786440 | tf_op jit(solution)/shard_map/ppermute | solution.py:633
  21.1 21.5 %collective-permute-start.2 = (bf16[128,1024]{1,0:T(8,128)(2,1)}, bf16[128,1024]{1,0:T(8,128)(2,1)S(1)}, u32[]{:S(2)}, u32[]{:S(2)}) collective-permute-start(bf16[128,1024]{1,0:T(8,128)(2,1)} %get-tuple-element.40), channel_id=1, source_target_pairs={{0,144},{8,152},{16,0},{24,8},{32,208},{40,216},{48,64},{56,72},{6... | collective-permute-start | bytes 786440 | tf_op jit(solution)/shard_map/ppermute | solution.py:633
  23.7 26.3 %collective-permute-start.8 = (bf16[144,1024]{1,0:T(8,128)(2,1)S(1)}, bf16[144,1024]{1,0:T(8,128)(2,1)S(1)}, u32[]{:S(2)}, u32[]{:S(2)}) collective-permute-start(bf16[144,1024]{1,0:T(8,128)(2,1)S(1)} %get-tuple-element.42), channel_id=1, source_target_pairs={{0,0},{8,16},{16,32},{24,48},{32,64},{40,80},{48,96},{56,112},{64,... | collective-permute-start | bytes 884744 | tf_op jit(solution)/shard_map/ppermute | solution.py:635
  27.5 22.6 %collective-permute-start.9 = (bf16[144,1024]{1,0:T(8,128)(2,1)S(1)}, bf16[144,1024]{1,0:T(8,128)(2,1)S(1)}, u32[]{:S(2)}, u32[]{:S(2)}) collective-permute-start(bf16[144,1024]{1,0:T(8,128)(2,1)S(1)} %get-tuple-element.43), channel_id=1, source_target_pairs={{0,16},{8,0},{16,48},{24,32},{32,80},{40,64},{48,112},{56,96},{64,... | collective-permute-start | bytes 884744 | tf_op jit(solution)/shard_map/ppermute | solution.py:635
  32.3 12.4 %collective-permute-start.3 = (bf16[128,1024]{1,0:T(8,128)(2,1)}, bf16[128,1024]{1,0:T(8,128)(2,1)S(1)}, u32[]{:S(2)}, u32[]{:S(2)}) collective-permute-start(bf16[128,1024]{1,0:T(8,128)(2,1)} %get-tuple-element.41), channel_id=1, source_target_pairs={{0,152},{8,144},{16,8},{24,0},{32,216},{40,208},{48,72},{56,64},{6... | collective-permute-start | bytes 786440 | tf_op jit(solution)/shard_map/ppermute | solution.py:633
  38.0 13.3 %collective-permute-start.10 = (bf16[144,1024]{1,0:T(8,128)(2,1)S(1)}, bf16[144,1024]{1,0:T(8,128)(2,1)S(1)}, u32[]{:S(2)}, u32[]{:S(2)}) collective-permute-start(bf16[144,1024]{1,0:T(8,128)(2,1)S(1)} %get-tuple-element.44), channel_id=1, source_target_pairs={{0,32},{8,48},{16,0},{24,16},{32,96},{40,112},{48,64},{56,80},{64,... | collective-permute-start | bytes 884744 | tf_op jit(solution)/shard_map/ppermute | solution.py:635
  42.6 13.0 %collective-permute-start.11 = (bf16[144,1024]{1,0:T(8,128)(2,1)S(1)}, bf16[144,1024]{1,0:T(8,128)(2,1)S(1)}, u32[]{:S(2)}, u32[]{:S(2)}) collective-permute-start(bf16[144,1024]{1,0:T(8,128)(2,1)S(1)} %get-tuple-element.45), channel_id=1, source_target_pairs={{0,48},{8,32},{16,16},{24,0},{32,112},{40,96},{48,80},{56,64},{64,... | collective-permute-start | bytes 884744 | tf_op jit(solution)/shard_map/ppermute | solution.py:635
  44.6 12.5 %collective-permute-start.4 = (bf16[128,1024]{1,0:T(8,128)(2,1)S(1)}, bf16[128,1024]{1,0:T(8,128)(2,1)S(1)}, u32[]{:S(2)}, u32[]{:S(2)}) collective-permute-start(bf16[128,1024]{1,0:T(8,128)(2,1)S(1)} %collective-permute-done.refs_0_), channel_id=1, source_target_pairs={{0,64},{64,0},{1,65},{65,1},{2,66},{66,2},{3,67},{67,3},{4,68},{68... | collective-permute-start | bytes 786440 | tf_op jit(solution)/shard_map/ppermute | solution.py:636
  50.0 7.1 %collective-permute-start.5 = (bf16[128,1024]{1,0:T(8,128)(2,1)S(1)}, bf16[128,1024]{1,0:T(8,128)(2,1)S(1)}, u32[]{:S(2)}, u32[]{:S(2)}) collective-permute-start(bf16[128,1024]{1,0:T(8,128)(2,1)S(1)} %collective-permute-done.1.refs_1_), channel_id=1, source_target_pairs={{0,64},{64,0},{1,65},{65,1},{2,66},{66,2},{3,67},{67,3},{4,68},{68... | collective-permute-start | bytes 786440 | tf_op jit(solution)/shard_map/ppermute | solution.py:636
  50.0 8.3 %collective-permute-start.6 = (bf16[128,1024]{1,0:T(8,128)(2,1)S(1)}, bf16[128,1024]{1,0:T(8,128)(2,1)}, u32[]{:S(2)}, u32[]{:S(2)}) collective-permute-start(bf16[128,1024]{1,0:T(8,128)(2,1)S(1)} %collective-permute-done.2.refs_2_), channel_id=1, source_target_pairs={{0,64},{64,0},{1,65},{65,1},{2,66},{66,2},{3,67},{67,3},{4,68},{68... | collective-permute-start | bytes 786440 | tf_op jit(solution)/shard_map/ppermute | solution.py:636
  50.6 0.7 copy-start.8
  51.3 8.2 %collective-permute-start.7 = (bf16[128,1024]{1,0:T(8,128)(2,1)S(1)}, bf16[128,1024]{1,0:T(8,128)(2,1)}, u32[]{:S(2)}, u32[]{:S(2)}) collective-permute-start(bf16[128,1024]{1,0:T(8,128)(2,1)S(1)} %collective-permute-done.3.refs_3_), channel_id=1, source_target_pairs={{0,64},{64,0},{1,65},{65,1},{2,66},{66,2},{3,67},{67,3},{4,68},{68... | collective-permute-start | bytes 786440 | tf_op jit(solution)/shard_map/ppermute | solution.py:636
  55.6 4.6 %collective-permute-start.12 = (bf16[144,1024]{1,0:T(8,128)(2,1)S(1)}, bf16[144,1024]{1,0:T(8,128)(2,1)S(1)}, u32[]{:S(2)}, u32[]{:S(2)}) collective-permute-start(bf16[144,1024]{1,0:T(8,128)(2,1)S(1)} %collective-permute-done.8.refs_8_.refs_0_), channel_id=1, source_target_pairs={{0,64},{64,0},{1,65},{65,1},{2,66},{66,2},{3,67},{67,3},{4,68},{68... | collective-permute-start | bytes 884744 | tf_op jit(solution)/shard_map/ppermute | solution.py:637
  57.1 3.1 %collective-permute-start.13 = (bf16[144,1024]{1,0:T(8,128)(2,1)S(1)}, bf16[144,1024]{1,0:T(8,128)(2,1)S(1)}, u32[]{:S(2)}, u32[]{:S(2)}) collective-permute-start(bf16[144,1024]{1,0:T(8,128)(2,1)S(1)} %collective-permute-done.9.refs_9_.refs_1_), channel_id=1, source_target_pairs={{0,64},{64,0},{1,65},{65,1},{2,66},{66,2},{3,67},{67,3},{4,68},{68... | collective-permute-start | bytes 884744 | tf_op jit(solution)/shard_map/ppermute | solution.py:637
  57.2 0.7 copy-start.10
  57.9 2.4 %collective-permute-start.14 = (bf16[144,1024]{1,0:T(8,128)(2,1)S(1)}, bf16[144,1024]{1,0:T(8,128)(2,1)S(1)}, u32[]{:S(2)}, u32[]{:S(2)}) collective-permute-start(bf16[144,1024]{1,0:T(8,128)(2,1)S(1)} %collective-permute-done.10.refs_10_.refs_2_), channel_id=1, source_target_pairs={{0,64},{64,0},{1,65},{65,1},{2,66},{66,2},{3,67},{67,3},{4,68},{68... | collective-permute-start | bytes 884744 | tf_op jit(solution)/shard_map/ppermute | solution.py:637
  58.4 1.9 %collective-permute-start.15 = (bf16[144,1024]{1,0:T(8,128)(2,1)S(1)}, bf16[144,1024]{1,0:T(8,128)(2,1)S(1)}, u32[]{:S(2)}, u32[]{:S(2)}) collective-permute-start(bf16[144,1024]{1,0:T(8,128)(2,1)S(1)} %collective-permute-done.11.refs_11_.refs_3_), channel_id=1, source_target_pairs={{0,64},{64,0},{1,65},{65,1},{2,66},{66,2},{3,67},{67,3},{4,68},{68... | collective-permute-start | bytes 884744 | tf_op jit(solution)/shard_map/ppermute | solution.py:637
  59.5 11.5 %collective-permute-start.16 = (bf16[4,32,1024]{2,1,0:T(8,128)(2,1)S(1)}, bf16[4,32,1024]{2,1,0:T(8,128)(2,1)S(1)}, u32[]{:S(2)}, u32[]{:S(2)}) collective-permute-start(bf16[4,32,1024]{2,1,0:T(8,128)(2,1)S(1)} %slice_select_fusion), channel_id=1, source_target_pairs={{0,64},{64,0},{1,65},{65,1},{2,66},{66,2},{3,67},{67,3},{4,68},{68... | collective-permute-start | bytes 786440 | tf_op jit(solution)/shard_map/ppermute | solution.py:639
  60.3 1.7 %copy-start = (bf16[1280,1024]{1,0:T(8,128)(2,1)S(1)}, bf16[1280,1024]{1,0:T(8,128)(2,1)}, u32[]{:S(2)}) copy-start(bf16[1280,1024]{1,0:T(8,128)(2,1)} %all-gather.2.cloned.1.call-done.refs_16_.refs_8_.wag) | copy-start | bytes 7864324
  62.0 0.9 copy-start.9
  62.9 0.9 copy-start.11
  70.9 8.2 %copy-start.2 = (bf16[1024,1024]{1,0:T(8,128)(2,1)}, bf16[1024,1024]{1,0:T(8,128)(2,1)S(1)}, u32[]{:S(2)}) copy-start(bf16[1024,1024]{1,0:T(8,128)(2,1)S(1)} %get-tuple-element.50.normed.normed_in) | copy-start | bytes 6291460
  72.6 2.0 %collective-permute-start.17 = (f32[1024,128]{1,0:T(8,128)S(1)}, f32[1024,128]{1,0:T(8,128)S(1)}, u32[]{:S(2)}, u32[]{:S(2)}) collective-permute-start(f32[1024,128]{1,0:T(8,128)S(1)} %get-tuple-element.53.own.stats), channel_id=1, source_target_pairs={{0,64},{64,0},{1,65},{65,1},{2,66},{66,2},{3,67},{67,3},{4,68},{68... | collective-permute-start | bytes 1572872 | tf_op jit(solution)/shard_map/ppermute | solution.py:643
  77.3 1.8 %collective-permute-start.18 = (bf16[4,32,1024]{2,1,0:T(8,128)(2,1)S(1)}, bf16[4,32,1024]{2,1,0:T(8,128)(2,1)S(1)}, u32[]{:S(2)}, u32[]{:S(2)}) collective-permute-start(bf16[4,32,1024]{2,1,0:T(8,128)(2,1)S(1)} %get-tuple-element.58), channel_id=1, source_target_pairs={{0,64},{64,0},{1,65},{65,1},{2,66},{66,2},{3,67},{67,3},{4,68},{68... | collective-permute-start | bytes 786440 | tf_op jit(solution)/shard_map/ppermute | solution.py:645
  87.3 1.6 copy-start.4
  88.8 1.4 copy-start.5
  90.2 1.7 %copy-start.1 = (bf16[1280,1024]{1,0:T(8,128)(2,1)S(1)}, bf16[1280,1024]{1,0:T(8,128)(2,1)}, u32[]{:S(2)}) copy-start(bf16[1280,1024]{1,0:T(8,128)(2,1)} %all-gather.2.cloned.1.call-done.refs_16_.refs_8_.wag) | copy-start | bytes 7864324
  91.9 1.6 copy-start.3
  93.5 1.6 copy-start.6
  99.8 2.7 %collective-permute-start.19 = (bf16[512,1024]{1,0:T(8,128)(2,1)S(1)}, bf16[512,1024]{1,0:T(8,128)(2,1)S(1)}, u32[]{:S(2)}, u32[]{:S(2)}) collective-permute-start(bf16[512,1024]{1,0:T(8,128)(2,1)S(1)} %get-tuple-element.62), channel_id=1, source_target_pairs={{0,64},{64,0},{1,65},{65,1},{2,66},{66,2},{3,67},{67,3},{4,68},{68... | collective-permute-start | bytes 3145736 | tf_op jit(solution)/shard_map/ppermute | solution.py:649
  102.8 13.1 %collective-permute-start.20 = (bf16[128,1024]{1,0:T(8,128)(2,1)S(1)}, bf16[128,1024]{1,0:T(8,128)(2,1)S(1)}, u32[]{:S(2)}, u32[]{:S(2)}) collective-permute-start(bf16[128,1024]{1,0:T(8,128)(2,1)S(1)} %get-tuple-element.63), channel_id=1, source_target_pairs={{0,0},{16,8},{32,16},{48,24},{64,32},{80,40},{96,48},{112,56},{8,6... | collective-permute-start | bytes 786440 | tf_op jit(solution)/shard_map/ppermute | solution.py:650
  104.8 17.5 %collective-permute-start.21 = (bf16[128,1024]{1,0:T(8,128)(2,1)S(1)}, bf16[128,1024]{1,0:T(8,128)(2,1)S(1)}, u32[]{:S(2)}, u32[]{:S(2)}) collective-permute-start(bf16[128,1024]{1,0:T(8,128)(2,1)S(1)} %get-tuple-element.64), channel_id=1, source_target_pairs={{16,0},{0,8},{48,16},{32,24},{80,32},{64,40},{112,48},{96,56},{24,... | collective-permute-start | bytes 786440 | tf_op jit(solution)/shard_map/ppermute | solution.py:650
  108.5 13.8 %collective-permute-start.22 = (bf16[128,1024]{1,0:T(8,128)(2,1)S(1)}, bf16[128,1024]{1,0:T(8,128)(2,1)S(1)}, u32[]{:S(2)}, u32[]{:S(2)}) collective-permute-start(bf16[128,1024]{1,0:T(8,128)(2,1)S(1)} %get-tuple-element.65), channel_id=1, source_target_pairs={{32,0},{48,8},{0,16},{16,24},{96,32},{112,40},{64,48},{80,56},{40,... | collective-permute-start | bytes 786440 | tf_op jit(solution)/shard_map/ppermute | solution.py:650
  112.9 16.9 %collective-permute-start.23 = (bf16[128,1024]{1,0:T(8,128)(2,1)S(1)}, bf16[128,1024]{1,0:T(8,128)(2,1)S(1)}, u32[]{:S(2)}, u32[]{:S(2)}) collective-permute-start(bf16[128,1024]{1,0:T(8,128)(2,1)S(1)} %get-tuple-element.66), channel_id=1, source_target_pairs={{48,0},{32,8},{16,16},{0,24},{112,32},{96,40},{80,48},{64,56},{56,... | collective-permute-start | bytes 786440 | tf_op jit(solution)/shard_map/ppermute | solution.py:650
  157.4 8.5 %collective-permute-start.24 = (bf16[1408,128]{1,0:T(8,128)(2,1)S(1)}, bf16[1408,128]{1,0:T(8,128)(2,1)S(1)}, u32[]{:S(2)}, u32[]{:S(2)}) collective-permute-start(bf16[1408,128]{1,0:T(8,128)(2,1)S(1)} %bitcast.4), channel_id=1, source_target_pairs={{0,64},{64,0},{1,65},{65,1},{2,66},{66,2},{3,67},{67,3},{4,68},{68... | collective-permute-start | bytes 1081352 | tf_op jit(solution)/shard_map/ppermute | solution.py:660
Sparse Core Ops, SparseCore 0:
  10.4 43.1 all-gather.1
  90.3 41.4 reduce-scatter.1

commit v6 on v5

--- a/solution.py
+++ b/solution.py
@@ -16,6 +16,7 @@
 F32 = jnp.float32
 BQ = 256
 NQ = L // BQ
+SENT = 1296
 SHARD = 1408
 PLANE = ("yh", "core", "yl", "x")
 CHIPS = ("yh", "yl", "x")
@@ -427,24 +428,24 @@
     leaving[0].start()
     bias = jnp.sum(total, axis=0, keepdims=True)
     high = bias.astype(BF).astype(F32)
-    line = lax.broadcasted_iota(jnp.int32, (128, 128), 0)
+    line = lax.broadcasted_iota(jnp.int32, (16, 128), 0)
     tile = jnp.where(line == 0, high, jnp.where(line == 1, bias - high, 0.0)).astype(BF)
     for z in range(8):
-        part[pl.ds(z * SHARD + 1280, 128), :] = tile
+        part[pl.ds(z * SENT + 1280, 16), :] = tile
     for q in range(4):
         for t in range(8):
-            mine = pl.multiple_of((4 * h + q) * SHARD + 1024 + 32 * t, 32)
-            theirs = pl.multiple_of((4 * (1 - h) + q) * SHARD + 1024 + 32 * t, 32)
+            mine = pl.multiple_of((4 * h + q) * SENT + 1024 + 32 * t, 16)
+            theirs = pl.multiple_of((4 * (1 - h) + q) * SENT + 1024 + 32 * t, 16)
             part[pl.ds(mine, 32), :] = keep[q, :, 128 * t : 128 * t + 128]
             part[pl.ds(theirs, 32), :] = recv[q, :, 128 * t : 128 * t + 128]
     for b in range(4):
         pin = tn(normed[:, 256 * b : 256 * b + 256], dhid[...]).astype(BF)
         for z in range(2):
             for t in range(8):
-                part[pl.ds((2 * b + z) * SHARD + 128 * t, 128), :] = pin[
+                part[pl.ds((2 * b + z) * SENT + 128 * t, 128), :] = pin[
                     128 * z : 128 * z + 128, 128 * t : 128 * t + 128
                 ]
-        two = pl.ds(2 * b * SHARD, 2 * SHARD)
+        two = pl.ds(2 * b * SENT, 2 * SENT)
         leaving.append(pltpu.make_async_copy(part.at[two], part_out.at[two], sem.at[b]))
         leaving[-1].start()
     for c in leaving:
@@ -454,11 +455,11 @@
 def backward(act, slope, probs, pslope, normed, datt, dhu, stats, keep, recv):
     return pl.pallas_call(
         backward_kernel,
-        out_shape=[shape((8 * SHARD, 128), BF), shape((L, D), BF)],
+        out_shape=[shape((8 * SENT, 128), BF), shape((L, D), BF)],
         in_specs=[VM] * 10,
         out_specs=[HB, HB],
         scratch_shapes=[
-            pltpu.VMEM((8 * SHARD, 128), BF),
+            pltpu.VMEM((8 * SENT, 128), BF),
             pltpu.VMEM((L, D), BF),
             pltpu.VMEM((L, L), BF),
             pltpu.VMEM((L, 256), BF),
@@ -654,6 +655,7 @@
     def exchange(v):
         return lax.all_to_all(v, CHIPS, split_axis=0, concat_axis=0, tiled=True)
 
+    mine = jnp.pad(mine, ((0, SHARD - SENT), (0, 0)))
     spread = exchange(mine.reshape(16, SHARD // 16, 128))
     summed = jnp.sum(spread.astype(F32), axis=0, keepdims=True).astype(BF)
     mine = exchange(jnp.broadcast_to(summed, spread.shape)).reshape(SHARD, 128)

time: 175 us -> 177 us (1.011)
  local copies, waits for them, and re-layouts: 12.9 us -> 15.5 us
    unnamed x30 -> x34, local copies, waits for them, and re-layouts: 12.9 us -> 14.5 us
  transfers between devices with their start and end apart: 27 -> 27, of which waited for: 8 -> 8; matrix products, arithmetic and copies ran while one was open for 1% -> 1% of each run, Pallas kernels for 10% -> 9%
where the time goes in v6:
time: 177 us; the launch traced here: 176 us
  starting transfers between devices  64.5 us (36%)
  Pallas kernels  31.9 us (18%)
  blocking collectives  24.9 us (14%)
  waiting for transfers between devices  23.5 us (13%)
  local copies, waits for them, and re-layouts  15.5 us (9%)
  between operations  14.4 us (8%)
    all_to_all x2, blocking collectives, exchange(): return lax.all_to_all(v, CHIPS, split_axis=0, concat_axis=0, tiled=True)  24.9 us
    ppermute x4, starting transfers between devices, local(): xs = [lax.ppermute(c, PLANE, input_pairs(k)) for k, c in enumerate(chunks)]  16.7 us
    ppermute x4, waiting for transfers between devices, local(): back = [lax.ppermute(pieces[k], PLANE, back_pairs(k)) for k in range(4)]  14.6 us
    unnamed x34, local copies, waits for them, and re-layouts  14.5 us
    ppermute x4, starting transfers between devices, local(): gs = [lax.ppermute(c, PLANE, grad_pairs(k)) for k, c in enumerate(picked)]  13.8 us
    ppermute x4, starting transfers between devices, local(): back = [lax.ppermute(pieces[k], PLANE, back_pairs(k)) for k in range(4)]  12.4 us
    ppermute x4, starting transfers between devices, local(): xs = xs + [swap(c) for c in xs]  11 us
    pallas_call x1, Pallas kernels, backward(): pl.pallas_call(backward_kernel, out_shape=[shape((8 * SENT, 128), BF), sh...  7.85 us
  transfers between devices with their start and end apart: 27, of which 8 were waited for; matrix products, arithmetic and copies ran while one was open for 1% of the time, Pallas kernels for 9%

profile of v6, /device:TPU:1, one launch (start us, length us, event | category | flops | bytes accessed | tf_op | source)
XLA Modules:
  0.0 175.9 jit_solution(16014778248943172)
XLA Ops:
  7.2 0.0 all-gather.2.cloned.1.call-start
  7.3 1.8 %own_weights.1 = bf16[160,1024]{1,0:T(8,128)(2,1)} custom-call(bf16[128,2048]{1,0:T(8,128)(2,1)} %w_in.1, bf16[64,1024]{1,0:T(8,128)(2,1)} %w_out.1), custom_call_target="tpu_custom_call" | custom-call | tf_op jit(solution)/shard_map/own_weights/pallas_call | solution.py:88
  9.1 0.0 all-gather.2.cloned.1.call-update
  9.1 0.0 reduce-scatter.2.cloned.1.call-start
  9.1 2.9 %deal.1 = (bf16[128,1024]{1,0:T(8,128)(2,1)}, bf16[128,1024]{1,0:T(8,128)(2,1)}, bf16[128,1024]{1,0:T(8,128)(2,1)}, bf16[128,1024]{1,0:T(8,128)(2,1)}) custom-call(s32[4]{0:T(128)} %plan.1, bf16[4,128,1024]{2,1,0:T(8,128)(2,1)} %lay.1), custom_call_target="tpu_custom_call" | custom-call | tf_op jit(solution)/shard_map/deal/pallas_call | solution.py:111
  12.0 6.0 %collective-permute-start = (bf16[128,1024]{1,0:T(8,128)(2,1)}, bf16[128,1024]{1,0:T(8,128)(2,1)S(1)}, u32[]{:S(2)}, u32[]{:S(2)}) collective-permute-start(bf16[128,1024]{1,0:T(8,128)(2,1)} %get-tuple-element.38), channel_id=1, source_target_pairs={{0,0},{8,8},{16,144},{24,152},{32,64},{40,72},{48,208},{56,216},{6... | collective-permute-start | bytes 786440 | tf_op jit(solution)/shard_map/ppermute | solution.py:634
  18.0 3.0 %collective-permute-start.1 = (bf16[128,1024]{1,0:T(8,128)(2,1)}, bf16[128,1024]{1,0:T(8,128)(2,1)S(1)}, u32[]{:S(2)}, u32[]{:S(2)}) collective-permute-start(bf16[128,1024]{1,0:T(8,128)(2,1)} %get-tuple-element.39), channel_id=1, source_target_pairs={{0,8},{8,0},{16,152},{24,144},{32,72},{40,64},{48,216},{56,208},{6... | collective-permute-start | bytes 786440 | tf_op jit(solution)/shard_map/ppermute | solution.py:634
  21.1 1.9 %collective-permute-start.2 = (bf16[128,1024]{1,0:T(8,128)(2,1)}, bf16[128,1024]{1,0:T(8,128)(2,1)S(1)}, u32[]{:S(2)}, u32[]{:S(2)}) collective-permute-start(bf16[128,1024]{1,0:T(8,128)(2,1)} %get-tuple-element.40), channel_id=1, source_target_pairs={{0,144},{8,152},{16,0},{24,8},{32,208},{40,216},{48,64},{56,72},{6... | collective-permute-start | bytes 786440 | tf_op jit(solution)/shard_map/ppermute | solution.py:634
  23.0 0.7 pick.1
  23.7 3.8 %collective-permute-start.8 = (bf16[144,1024]{1,0:T(8,128)(2,1)S(1)}, bf16[144,1024]{1,0:T(8,128)(2,1)S(1)}, u32[]{:S(2)}, u32[]{:S(2)}) collective-permute-start(bf16[144,1024]{1,0:T(8,128)(2,1)S(1)} %get-tuple-element.42), channel_id=1, source_target_pairs={{0,0},{8,16},{16,32},{24,48},{32,64},{40,80},{48,96},{56,112},{64,... | collective-permute-start | bytes 884744 | tf_op jit(solution)/shard_map/ppermute | solution.py:636
  27.5 4.8 %collective-permute-start.9 = (bf16[144,1024]{1,0:T(8,128)(2,1)S(1)}, bf16[144,1024]{1,0:T(8,128)(2,1)S(1)}, u32[]{:S(2)}, u32[]{:S(2)}) collective-permute-start(bf16[144,1024]{1,0:T(8,128)(2,1)S(1)} %get-tuple-element.43), channel_id=1, source_target_pairs={{0,16},{8,0},{16,48},{24,32},{32,80},{40,64},{48,112},{56,96},{64,... | collective-permute-start | bytes 884744 | tf_op jit(solution)/shard_map/ppermute | solution.py:636
  32.2 5.7 %collective-permute-start.3 = (bf16[128,1024]{1,0:T(8,128)(2,1)}, bf16[128,1024]{1,0:T(8,128)(2,1)S(1)}, u32[]{:S(2)}, u32[]{:S(2)}) collective-permute-start(bf16[128,1024]{1,0:T(8,128)(2,1)} %get-tuple-element.41), channel_id=1, source_target_pairs={{0,152},{8,144},{16,8},{24,0},{32,216},{40,208},{48,72},{56,64},{6... | collective-permute-start | bytes 786440 | tf_op jit(solution)/shard_map/ppermute | solution.py:634
  37.9 3.3 %collective-permute-start.10 = (bf16[144,1024]{1,0:T(8,128)(2,1)S(1)}, bf16[144,1024]{1,0:T(8,128)(2,1)S(1)}, u32[]{:S(2)}, u32[]{:S(2)}) collective-permute-start(bf16[144,1024]{1,0:T(8,128)(2,1)S(1)} %get-tuple-element.44), channel_id=1, source_target_pairs={{0,32},{8,48},{16,0},{24,16},{32,96},{40,112},{48,64},{56,80},{64,... | collective-permute-start | bytes 884744 | tf_op jit(solution)/shard_map/ppermute | solution.py:636
  41.2 1.4 collective-permute-done.2.refs_2_
  42.6 2.0 %collective-permute-start.11 = (bf16[144,1024]{1,0:T(8,128)(2,1)S(1)}, bf16[144,1024]{1,0:T(8,128)(2,1)S(1)}, u32[]{:S(2)}, u32[]{:S(2)}) collective-permute-start(bf16[144,1024]{1,0:T(8,128)(2,1)S(1)} %get-tuple-element.45), channel_id=1, source_target_pairs={{0,48},{8,32},{16,16},{24,0},{32,112},{40,96},{48,80},{56,64},{64,... | collective-permute-start | bytes 884744 | tf_op jit(solution)/shard_map/ppermute | solution.py:636
  44.6 5.4 %collective-permute-start.4 = (bf16[128,1024]{1,0:T(8,128)(2,1)S(1)}, bf16[128,1024]{1,0:T(8,128)(2,1)S(1)}, u32[]{:S(2)}, u32[]{:S(2)}) collective-permute-start(bf16[128,1024]{1,0:T(8,128)(2,1)S(1)} %collective-permute-done.refs_0_), channel_id=1, source_target_pairs={{0,64},{64,0},{1,65},{65,1},{2,66},{66,2},{3,67},{67,3},{4,68},{68... | collective-permute-start | bytes 786440 | tf_op jit(solution)/shard_map/ppermute | solution.py:637
  50.0 0.5 collective-permute-start.6
  50.5 5.1 %collective-permute-start.7 = (bf16[128,1024]{1,0:T(8,128)(2,1)S(1)}, bf16[128,1024]{1,0:T(8,128)(2,1)}, u32[]{:S(2)}, u32[]{:S(2)}) collective-permute-start(bf16[128,1024]{1,0:T(8,128)(2,1)S(1)} %collective-permute-done.3.refs_3_), channel_id=1, source_target_pairs={{0,64},{64,0},{1,65},{65,1},{2,66},{66,2},{3,67},{67,3},{4,68},{68... | collective-permute-start | bytes 786440 | tf_op jit(solution)/shard_map/ppermute | solution.py:637
  55.6 1.5 collective-permute-start.12
  57.1 0.7 copy-done.8
  57.8 0.0 collective-permute-start.13
  57.8 0.7 copy-done.10
  58.5 0.5 collective-permute-start.14
  59.0 0.7 copy-done.12
  59.7 0.0 collective-permute-start.15
  59.8 1.1 slice_select_fusion
  60.8 0.8 collective-permute-start.16
  61.6 1.7 copy-done
  63.4 0.9 copy-done.9
  64.3 0.9 copy-done.11
  65.3 0.9 copy-done.13
  66.2 7.1 %forward.1 = (bf16[1024,1024]{1,0:T(8,128)(2,1)S(1)}, bf16[1024,1024]{1,0:T(8,128)(2,1)S(1)}, bf16[1024,1024]{1,0:T(8,128)(2,1)S(1)}, bf16[1024,1024]{1,0:T(8,12...) custom-call(bf16[2,128]{1,0:T(2,128)(2,1)S(1)} %copy-done.16, ...), custom_call_target="tpu_custom_call" | custom-call | tf_op jit(solution)/shard_map/forward/pallas_call | solution.py:256
  73.4 1.6 statistics.1
  75.0 0.1 collective-permute-start.17
  75.1 1.9 %collective-permute-done.17.peer = f32[1024,128]{1,0:T(8,128)S(1)} collective-permute-done((f32[1024,128]{1,0:T(8,128)S(1)}, f32[1024,128]{1,0:T(8,128)S(1)}, u32[]{:S(2)}, u32[]{:S(2)}) %collective-permute-start.17) | collective-permute-done | bytes 524320 | tf_op jit(solution)/shard_map/ppermute | solution.py:644
  77.0 2.8 %middle.1 = (bf16[1024,256]{1,0:T(8,128)(2,1)S(1)}, bf16[1024,256]{1,0:T(8,128)(2,1)S(1)}, bf16[4,32,1024]{2,1,0:T(8,128)(2,1)S(1)}, bf16[4,32,1024]{2,1,0:T(8,128)(2,1)S(1)}) custom-call(f32[1024,128]{1,0:T(8,128)S(1)} %get-tuple-element.53.own.stats, f32[1024,128]{1,0:T(8,128)S(1)} %collective-permute-done.17.peer, ...), custom_call_target="tpu_custom_call" | custom-call | tf_op jit(solution)/shard_map/middle/pallas_call | solution.py:374
  79.8 0.4 collective-permute-start.18
  80.3 1.4 collective-permute-done.18.recv
  81.7 7.8 %backward.1 = (bf16[10368,128]{1,0:T(8,128)(2,1)S(1)}, bf16[1024,1024]{1,0:T(8,128)(2,1)S(1)}) custom-call(bf16[1024,1024]{1,0:T(8,128)(2,1)S(1)} %get-tuple-element.46.gate.act, bf16[1024,1024]{1,0:T(8,128)(2,1)S(1)} %get-tuple-element.47.gslope.slope, bf16[1024,1024]{1,0:T(8,128)(2,1)S(1)} %get-tuple-element.48.probs, ...), custom_call_target="tpu_custom_call" | custom-call | tf_op jit(solution)/shard_map/backward/pallas_call | solution.py:456
  89.5 1.5 copy-done.4
  91.0 1.4 copy-done.5
  92.4 0.0 reduce-scatter.2.cloned.1.call-update
  92.5 1.7 copy-done.1
  94.2 1.6 copy-done.3
  95.8 1.6 copy-done.6
  97.4 4.7 %input_grad.1 = (bf16[512,1024]{1,0:T(8,128)(2,1)S(1)}, bf16[512,1024]{1,0:T(8,128)(2,1)S(1)}) custom-call(bf16[1024,1024]{1,0:T(8,128)(2,1)S(1)} %copy-done.6, bf16[1024,1024]{1,0:T(8,128)(2,1)S(1)} %copy-done.3, f32[1024,128]{1,0:T(8,128)S(1)} %get-tuple-element.53.own.stats, bf16[1280,1024]{1,0:T(8,128)(2,1)S(1)} %copy-done.1), custom_call_target="tpu_custom_call" | custom-call | tf_op jit(solution)/shard_map/input_grad/pallas_call | solution.py:511
  102.0 0.2 collective-permute-start.19
  102.3 2.5 %collective-permute-done.19.b = bf16[512,1024]{1,0:T(8,128)(2,1)S(1)} collective-permute-done((bf16[512,1024]{1,0:T(8,128)(2,1)S(1)}, bf16[512,1024]{1,0:T(8,128)(2,1)S(1)}, u32[]{:S(2)}, u32[]{:S(2)}) %collective-permute-start.19) | collective-permute-done | bytes 1048608 | tf_op jit(solution)/shard_map/ppermute | solution.py:650
  104.8 0.2 add_halves.1
  105.0 2.0 %collective-permute-start.20 = (bf16[128,1024]{1,0:T(8,128)(2,1)S(1)}, bf16[128,1024]{1,0:T(8,128)(2,1)S(1)}, u32[]{:S(2)}, u32[]{:S(2)}) collective-permute-start(bf16[128,1024]{1,0:T(8,128)(2,1)S(1)} %get-tuple-element.63), channel_id=1, source_target_pairs={{0,0},{16,8},{32,16},{48,24},{64,32},{80,40},{96,48},{112,56},{8,6... | collective-permute-start | bytes 786440 | tf_op jit(solution)/shard_map/ppermute | solution.py:651
  107.0 2.3 %collective-permute-start.21 = (bf16[128,1024]{1,0:T(8,128)(2,1)S(1)}, bf16[128,1024]{1,0:T(8,128)(2,1)S(1)}, u32[]{:S(2)}, u32[]{:S(2)}) collective-permute-start(bf16[128,1024]{1,0:T(8,128)(2,1)S(1)} %get-tuple-element.64), channel_id=1, source_target_pairs={{16,0},{0,8},{48,16},{32,24},{80,32},{64,40},{112,48},{96,56},{24,... | collective-permute-start | bytes 786440 | tf_op jit(solution)/shard_map/ppermute | solution.py:651
  109.4 5.8 %collective-permute-start.22 = (bf16[128,1024]{1,0:T(8,128)(2,1)S(1)}, bf16[128,1024]{1,0:T(8,128)(2,1)S(1)}, u32[]{:S(2)}, u32[]{:S(2)}) collective-permute-start(bf16[128,1024]{1,0:T(8,128)(2,1)S(1)} %get-tuple-element.65), channel_id=1, source_target_pairs={{32,0},{48,8},{0,16},{16,24},{96,32},{112,40},{64,48},{80,56},{40,... | collective-permute-start | bytes 786440 | tf_op jit(solution)/shard_map/ppermute | solution.py:651
  115.1 2.3 %collective-permute-start.23 = (bf16[128,1024]{1,0:T(8,128)(2,1)S(1)}, bf16[128,1024]{1,0:T(8,128)(2,1)S(1)}, u32[]{:S(2)}, u32[]{:S(2)}) collective-permute-start(bf16[128,1024]{1,0:T(8,128)(2,1)S(1)} %get-tuple-element.66), channel_id=1, source_target_pairs={{48,0},{32,8},{16,16},{0,24},{112,32},{96,40},{80,48},{64,56},{56,... | collective-permute-start | bytes 786440 | tf_op jit(solution)/shard_map/ppermute | solution.py:651
  117.5 7.1 %collective-permute-done.21.refs_1_ = bf16[128,1024]{1,0:T(8,128)(2,1)S(1)} collective-permute-done((bf16[128,1024]{1,0:T(8,128)(2,1)S(1)}, bf16[128,1024]{1,0:T(8,128)(2,1)S(1)}, u32[]{:S(2)}, u32[]{:S(2)}) %collective-permute-start.21) | collective-permute-done | bytes 262176 | tf_op jit(solution)/shard_map/ppermute | solution.py:651
  124.6 7.5 %collective-permute-done.23.refs_3_ = bf16[128,1024]{1,0:T(8,128)(2,1)S(1)} collective-permute-done((bf16[128,1024]{1,0:T(8,128)(2,1)S(1)}, bf16[128,1024]{1,0:T(8,128)(2,1)S(1)}, u32[]{:S(2)}, u32[]{:S(2)}) %collective-permute-start.23) | collective-permute-done | bytes 262176 | tf_op jit(solution)/shard_map/ppermute | solution.py:651
  132.1 1.1 place.1
  133.2 0.3 reduce-scatter.2.cloned.1.call-done
  133.5 1.0 pad.4
  134.5 14.3 %all_to_all.10 = bf16[16,88,128]{2,1,0:T(8,128)(2,1)S(1)} all-to-all(bf16[16,88,128]{2,1,0:T(8,128)(2,1)S(1)} %bitcast.6), channel_id=1, replica_groups=mesh['yh'=2,'core'=2,'yl'=2,'x'=4,'z'=8] {'yh','yl','x'}, dimensions={0} | all-to-all | bytes 720896 | tf_op jit(solution)/shard_map/all_to_all | solution.py:656
  148.8 0.1 reduce_sum.12
  148.9 10.7 %all_to_all.11 = bf16[16,88,128]{2,1,0:T(8,128)(2,1)S(1)} all-to-all(bf16[16,88,128]{2,1,0:T(8,128)(2,1)S(1)} %broadcast_in_dim.2), channel_id=1, replica_groups=mesh['yh'=2,'core'=2,'yl'=2,'x'=4,'z'=8] {'yh','yl','x'}, dimensions={0} | all-to-all | bytes 720896 | tf_op jit(solution)/shard_map/all_to_all | solution.py:656
  159.6 7.0 %collective-permute-start.24 = (bf16[1408,128]{1,0:T(8,128)(2,1)S(1)}, bf16[1408,128]{1,0:T(8,128)(2,1)S(1)}, u32[]{:S(2)}, u32[]{:S(2)}) collective-permute-start(bf16[1408,128]{1,0:T(8,128)(2,1)S(1)} %bitcast.4), channel_id=1, source_target_pairs={{0,64},{64,0},{1,65},{65,1},{2,66},{66,2},{3,67},{67,3},{4,68},{68... | collective-permute-start | bytes 1081352 | tf_op jit(solution)/shard_map/ppermute | solution.py:662
  166.5 1.3 collective-permute-done.24.theirs
  167.8 1.2 finish.1
  (43 shorter events, 0.1 us)
Async XLA Ops:
  7.2 15.8 %copy-start.7 = (bf16[4,128,1024]{2,1,0:T(8,128)(2,1)S(1)}, bf16[4,128,1024]{2,1,0:T(8,128)(2,1)}, u32[]{:S(2)}) copy-start(bf16[4,128,1024]{2,1,0:T(8,128)(2,1)} %grad.1) | copy-start | bytes 3145732
  7.2 15.8 %copy-start.14 = (s32[4,128]{1,0:T(4,128)S(1)}, s32[4,128]{1,0:T(4,128)}, u32[]{:S(2)}) copy-start(s32[4,128]{1,0:T(4,128)} %stamps.1) | copy-start | bytes 6148
  7.2 15.8 %copy-start.15 = (s32[4]{0:T(128)S(1)}, s32[4]{0:T(128)}, u32[]{:S(2)}) copy-start(s32[4]{0:T(128)} %lengths.1) | copy-start | bytes 52
  7.2 54.4 %copy-start.16 = (bf16[2,128]{1,0:T(2,128)(2,1)S(1)}, bf16[2,128]{1,0:T(2,128)(2,1)}, u32[]{:S(2)}) copy-start(bf16[2,128]{1,0:T(2,128)(2,1)} %tb.1) | copy-start | bytes 1540
  7.2 52.5 %all-gather.2.cloned.1.call-start = ((), (), s32[]{:S(2)}) async-start(), calls=%async_computation.3 | async-start | bytes 2949120 | tf_op jit(solution)/shard_map/all_gather | solution.py:632
  9.1 124.4 %reduce-scatter.2.cloned.1.call-start = ((), (), s32[]{:S(2)}) async-start(), calls=%async_computation.4 | async-start | bytes 2985984 | tf_op jit(solution)/shard_map/reduce_scatter | solution.py:648
  12.0 20.2 %collective-permute-start = (bf16[128,1024]{1,0:T(8,128)(2,1)}, bf16[128,1024]{1,0:T(8,128)(2,1)S(1)}, u32[]{:S(2)}, u32[]{:S(2)}) collective-permute-start(bf16[128,1024]{1,0:T(8,128)(2,1)} %get-tuple-element.38), channel_id=1, source_target_pairs={{0,0},{8,8},{16,144},{24,152},{32,64},{40,72},{48,208},{56,216},{6... | collective-permute-start | bytes 786440 | tf_op jit(solution)/shard_map/ppermute | solution.py:634
  18.0 19.9 %collective-permute-start.1 = (bf16[128,1024]{1,0:T(8,128)(2,1)}, bf16[128,1024]{1,0:T(8,128)(2,1)S(1)}, u32[]{:S(2)}, u32[]{:S(2)}) collective-permute-start(bf16[128,1024]{1,0:T(8,128)(2,1)} %get-tuple-element.39), channel_id=1, source_target_pairs={{0,8},{8,0},{16,152},{24,144},{32,72},{40,64},{48,216},{56,208},{6... | collective-permute-start | bytes 786440 | tf_op jit(solution)/shard_map/ppermute | solution.py:634
  21.1 21.5 %collective-permute-start.2 = (bf16[128,1024]{1,0:T(8,128)(2,1)}, bf16[128,1024]{1,0:T(8,128)(2,1)S(1)}, u32[]{:S(2)}, u32[]{:S(2)}) collective-permute-start(bf16[128,1024]{1,0:T(8,128)(2,1)} %get-tuple-element.40), channel_id=1, source_target_pairs={{0,144},{8,152},{16,0},{24,8},{32,208},{40,216},{48,64},{56,72},{6... | collective-permute-start | bytes 786440 | tf_op jit(solution)/shard_map/ppermute | solution.py:634
  23.7 26.3 %collective-permute-start.8 = (bf16[144,1024]{1,0:T(8,128)(2,1)S(1)}, bf16[144,1024]{1,0:T(8,128)(2,1)S(1)}, u32[]{:S(2)}, u32[]{:S(2)}) collective-permute-start(bf16[144,1024]{1,0:T(8,128)(2,1)S(1)} %get-tuple-element.42), channel_id=1, source_target_pairs={{0,0},{8,16},{16,32},{24,48},{32,64},{40,80},{48,96},{56,112},{64,... | collective-permute-start | bytes 884744 | tf_op jit(solution)/shard_map/ppermute | solution.py:636
  27.5 22.6 %collective-permute-start.9 = (bf16[144,1024]{1,0:T(8,128)(2,1)S(1)}, bf16[144,1024]{1,0:T(8,128)(2,1)S(1)}, u32[]{:S(2)}, u32[]{:S(2)}) collective-permute-start(bf16[144,1024]{1,0:T(8,128)(2,1)S(1)} %get-tuple-element.43), channel_id=1, source_target_pairs={{0,16},{8,0},{16,48},{24,32},{32,80},{40,64},{48,112},{56,96},{64,... | collective-permute-start | bytes 884744 | tf_op jit(solution)/shard_map/ppermute | solution.py:636
  32.2 12.4 %collective-permute-start.3 = (bf16[128,1024]{1,0:T(8,128)(2,1)}, bf16[128,1024]{1,0:T(8,128)(2,1)S(1)}, u32[]{:S(2)}, u32[]{:S(2)}) collective-permute-start(bf16[128,1024]{1,0:T(8,128)(2,1)} %get-tuple-element.41), channel_id=1, source_target_pairs={{0,152},{8,144},{16,8},{24,0},{32,216},{40,208},{48,72},{56,64},{6... | collective-permute-start | bytes 786440 | tf_op jit(solution)/shard_map/ppermute | solution.py:634
  37.9 12.6 %collective-permute-start.10 = (bf16[144,1024]{1,0:T(8,128)(2,1)S(1)}, bf16[144,1024]{1,0:T(8,128)(2,1)S(1)}, u32[]{:S(2)}, u32[]{:S(2)}) collective-permute-start(bf16[144,1024]{1,0:T(8,128)(2,1)S(1)} %get-tuple-element.44), channel_id=1, source_target_pairs={{0,32},{8,48},{16,0},{24,16},{32,96},{40,112},{48,64},{56,80},{64,... | collective-permute-start | bytes 884744 | tf_op jit(solution)/shard_map/ppermute | solution.py:636
  42.6 13.0 %collective-permute-start.11 = (bf16[144,1024]{1,0:T(8,128)(2,1)S(1)}, bf16[144,1024]{1,0:T(8,128)(2,1)S(1)}, u32[]{:S(2)}, u32[]{:S(2)}) collective-permute-start(bf16[144,1024]{1,0:T(8,128)(2,1)S(1)} %get-tuple-element.45), channel_id=1, source_target_pairs={{0,48},{8,32},{16,16},{24,0},{32,112},{40,96},{48,80},{56,64},{64,... | collective-permute-start | bytes 884744 | tf_op jit(solution)/shard_map/ppermute | solution.py:636
  44.6 12.5 %collective-permute-start.4 = (bf16[128,1024]{1,0:T(8,128)(2,1)S(1)}, bf16[128,1024]{1,0:T(8,128)(2,1)S(1)}, u32[]{:S(2)}, u32[]{:S(2)}) collective-permute-start(bf16[128,1024]{1,0:T(8,128)(2,1)S(1)} %collective-permute-done.refs_0_), channel_id=1, source_target_pairs={{0,64},{64,0},{1,65},{65,1},{2,66},{66,2},{3,67},{67,3},{4,68},{68... | collective-permute-start | bytes 786440 | tf_op jit(solution)/shard_map/ppermute | solution.py:637
  50.0 7.8 %collective-permute-start.5 = (bf16[128,1024]{1,0:T(8,128)(2,1)S(1)}, bf16[128,1024]{1,0:T(8,128)(2,1)S(1)}, u32[]{:S(2)}, u32[]{:S(2)}) collective-permute-start(bf16[128,1024]{1,0:T(8,128)(2,1)S(1)} %collective-permute-done.1.refs_1_), channel_id=1, source_target_pairs={{0,64},{64,0},{1,65},{65,1},{2,66},{66,2},{3,67},{67,3},{4,68},{68... | collective-permute-start | bytes 786440 | tf_op jit(solution)/shard_map/ppermute | solution.py:637
  50.0 9.0 %collective-permute-start.6 = (bf16[128,1024]{1,0:T(8,128)(2,1)S(1)}, bf16[128,1024]{1,0:T(8,128)(2,1)S(1)}, u32[]{:S(2)}, u32[]{:S(2)}) collective-permute-start(bf16[128,1024]{1,0:T(8,128)(2,1)S(1)} %collective-permute-done.2.refs_2_), channel_id=1, source_target_pairs={{0,64},{64,0},{1,65},{65,1},{2,66},{66,2},{3,67},{67,3},{4,68},{68... | collective-permute-start | bytes 786440 | tf_op jit(solution)/shard_map/ppermute | solution.py:637
  50.5 10.3 %collective-permute-start.7 = (bf16[128,1024]{1,0:T(8,128)(2,1)S(1)}, bf16[128,1024]{1,0:T(8,128)(2,1)}, u32[]{:S(2)}, u32[]{:S(2)}) collective-permute-start(bf16[128,1024]{1,0:T(8,128)(2,1)S(1)} %collective-permute-done.3.refs_3_), channel_id=1, source_target_pairs={{0,64},{64,0},{1,65},{65,1},{2,66},{66,2},{3,67},{67,3},{4,68},{68... | collective-permute-start | bytes 786440 | tf_op jit(solution)/shard_map/ppermute | solution.py:637
  55.6 6.0 %collective-permute-start.12 = (bf16[144,1024]{1,0:T(8,128)(2,1)S(1)}, bf16[144,1024]{1,0:T(8,128)(2,1)S(1)}, u32[]{:S(2)}, u32[]{:S(2)}) collective-permute-start(bf16[144,1024]{1,0:T(8,128)(2,1)S(1)} %collective-permute-done.8.refs_8_.refs_0_), channel_id=1, source_target_pairs={{0,64},{64,0},{1,65},{65,1},{2,66},{66,2},{3,67},{67,3},{4,68},{68... | collective-permute-start | bytes 884744 | tf_op jit(solution)/shard_map/ppermute | solution.py:638
  57.1 0.7 copy-start.8
  57.8 3.8 %collective-permute-start.13 = (bf16[144,1024]{1,0:T(8,128)(2,1)S(1)}, bf16[144,1024]{1,0:T(8,128)(2,1)S(1)}, u32[]{:S(2)}, u32[]{:S(2)}) collective-permute-start(bf16[144,1024]{1,0:T(8,128)(2,1)S(1)} %collective-permute-done.9.refs_9_.refs_1_), channel_id=1, source_target_pairs={{0,64},{64,0},{1,65},{65,1},{2,66},{66,2},{3,67},{67,3},{4,68},{68... | collective-permute-start | bytes 884744 | tf_op jit(solution)/shard_map/ppermute | solution.py:638
  57.8 0.7 copy-start.10
  58.5 3.1 %collective-permute-start.14 = (bf16[144,1024]{1,0:T(8,128)(2,1)S(1)}, bf16[144,1024]{1,0:T(8,128)(2,1)S(1)}, u32[]{:S(2)}, u32[]{:S(2)}) collective-permute-start(bf16[144,1024]{1,0:T(8,128)(2,1)S(1)} %collective-permute-done.10.refs_10_.refs_2_), channel_id=1, source_target_pairs={{0,64},{64,0},{1,65},{65,1},{2,66},{66,2},{3,67},{67,3},{4,68},{68... | collective-permute-start | bytes 884744 | tf_op jit(solution)/shard_map/ppermute | solution.py:638
  59.0 0.7 copy-start.12
  59.7 1.9 %collective-permute-start.15 = (bf16[144,1024]{1,0:T(8,128)(2,1)S(1)}, bf16[144,1024]{1,0:T(8,128)(2,1)S(1)}, u32[]{:S(2)}, u32[]{:S(2)}) collective-permute-start(bf16[144,1024]{1,0:T(8,128)(2,1)S(1)} %collective-permute-done.11.refs_11_.refs_3_), channel_id=1, source_target_pairs={{0,64},{64,0},{1,65},{65,1},{2,66},{66,2},{3,67},{67,3},{4,68},{68... | collective-permute-start | bytes 884744 | tf_op jit(solution)/shard_map/ppermute | solution.py:638
  60.8 12.5 %collective-permute-start.16 = (bf16[4,32,1024]{2,1,0:T(8,128)(2,1)S(1)}, bf16[4,32,1024]{2,1,0:T(8,128)(2,1)S(1)}, u32[]{:S(2)}, u32[]{:S(2)}) collective-permute-start(bf16[4,32,1024]{2,1,0:T(8,128)(2,1)S(1)} %slice_select_fusion), channel_id=1, source_target_pairs={{0,64},{64,0},{1,65},{65,1},{2,66},{66,2},{3,67},{67,3},{4,68},{68... | collective-permute-start | bytes 786440 | tf_op jit(solution)/shard_map/ppermute | solution.py:640
  61.6 1.7 copy-start
  63.4 0.9 copy-start.9
  64.3 0.9 copy-start.11
  65.3 0.9 copy-start.13
  73.3 8.3 %copy-start.2 = (bf16[1024,1024]{1,0:T(8,128)(2,1)}, bf16[1024,1024]{1,0:T(8,128)(2,1)S(1)}, u32[]{:S(2)}) copy-start(bf16[1024,1024]{1,0:T(8,128)(2,1)S(1)} %get-tuple-element.50.normed.normed_in) | copy-start | bytes 6291460
  75.0 2.0 %collective-permute-start.17 = (f32[1024,128]{1,0:T(8,128)S(1)}, f32[1024,128]{1,0:T(8,128)S(1)}, u32[]{:S(2)}, u32[]{:S(2)}) collective-permute-start(f32[1024,128]{1,0:T(8,128)S(1)} %get-tuple-element.53.own.stats), channel_id=1, source_target_pairs={{0,64},{64,0},{1,65},{65,1},{2,66},{66,2},{3,67},{67,3},{4,68},{68... | collective-permute-start | bytes 1572872 | tf_op jit(solution)/shard_map/ppermute | solution.py:644
  79.8 1.8 %collective-permute-start.18 = (bf16[4,32,1024]{2,1,0:T(8,128)(2,1)S(1)}, bf16[4,32,1024]{2,1,0:T(8,128)(2,1)S(1)}, u32[]{:S(2)}, u32[]{:S(2)}) collective-permute-start(bf16[4,32,1024]{2,1,0:T(8,128)(2,1)S(1)} %get-tuple-element.58), channel_id=1, source_target_pairs={{0,64},{64,0},{1,65},{65,1},{2,66},{66,2},{3,67},{67,3},{4,68},{68... | collective-permute-start | bytes 786440 | tf_op jit(solution)/shard_map/ppermute | solution.py:646
  89.5 1.5 copy-start.4
  91.0 1.4 copy-start.5
  92.4 1.7 copy-start.1
  94.2 1.6 copy-start.3
  95.8 1.6 copy-start.6
  102.0 2.7 %collective-permute-start.19 = (bf16[512,1024]{1,0:T(8,128)(2,1)S(1)}, bf16[512,1024]{1,0:T(8,128)(2,1)S(1)}, u32[]{:S(2)}, u32[]{:S(2)}) collective-permute-start(bf16[512,1024]{1,0:T(8,128)(2,1)S(1)} %get-tuple-element.62), channel_id=1, source_target_pairs={{0,64},{64,0},{1,65},{65,1},{2,66},{66,2},{3,67},{67,3},{4,68},{68... | collective-permute-start | bytes 3145736 | tf_op jit(solution)/shard_map/ppermute | solution.py:650
  105.0 12.4 %collective-permute-start.20 = (bf16[128,1024]{1,0:T(8,128)(2,1)S(1)}, bf16[128,1024]{1,0:T(8,128)(2,1)S(1)}, u32[]{:S(2)}, u32[]{:S(2)}) collective-permute-start(bf16[128,1024]{1,0:T(8,128)(2,1)S(1)} %get-tuple-element.63), channel_id=1, source_target_pairs={{0,0},{16,8},{32,16},{48,24},{64,32},{80,40},{96,48},{112,56},{8,6... | collective-permute-start | bytes 786440 | tf_op jit(solution)/shard_map/ppermute | solution.py:651
  107.0 17.5 %collective-permute-start.21 = (bf16[128,1024]{1,0:T(8,128)(2,1)S(1)}, bf16[128,1024]{1,0:T(8,128)(2,1)S(1)}, u32[]{:S(2)}, u32[]{:S(2)}) collective-permute-start(bf16[128,1024]{1,0:T(8,128)(2,1)S(1)} %get-tuple-element.64), channel_id=1, source_target_pairs={{16,0},{0,8},{48,16},{32,24},{80,32},{64,40},{112,48},{96,56},{24,... | collective-permute-start | bytes 786440 | tf_op jit(solution)/shard_map/ppermute | solution.py:651
  109.4 15.2 %collective-permute-start.22 = (bf16[128,1024]{1,0:T(8,128)(2,1)S(1)}, bf16[128,1024]{1,0:T(8,128)(2,1)S(1)}, u32[]{:S(2)}, u32[]{:S(2)}) collective-permute-start(bf16[128,1024]{1,0:T(8,128)(2,1)S(1)} %get-tuple-element.65), channel_id=1, source_target_pairs={{32,0},{48,8},{0,16},{16,24},{96,32},{112,40},{64,48},{80,56},{40,... | collective-permute-start | bytes 786440 | tf_op jit(solution)/shard_map/ppermute | solution.py:651
  115.1 16.9 %collective-permute-start.23 = (bf16[128,1024]{1,0:T(8,128)(2,1)S(1)}, bf16[128,1024]{1,0:T(8,128)(2,1)S(1)}, u32[]{:S(2)}, u32[]{:S(2)}) collective-permute-start(bf16[128,1024]{1,0:T(8,128)(2,1)S(1)} %get-tuple-element.66), channel_id=1, source_target_pairs={{48,0},{32,8},{16,16},{0,24},{112,32},{96,40},{80,48},{64,56},{56,... | collective-permute-start | bytes 786440 | tf_op jit(solution)/shard_map/ppermute | solution.py:651
  159.6 8.3 %collective-permute-start.24 = (bf16[1408,128]{1,0:T(8,128)(2,1)S(1)}, bf16[1408,128]{1,0:T(8,128)(2,1)S(1)}, u32[]{:S(2)}, u32[]{:S(2)}) collective-permute-start(bf16[1408,128]{1,0:T(8,128)(2,1)S(1)} %bitcast.4), channel_id=1, source_target_pairs={{0,64},{64,0},{1,65},{65,1},{2,66},{66,2},{3,67},{67,3},{4,68},{68... | collective-permute-start | bytes 1081352 | tf_op jit(solution)/shard_map/ppermute | solution.py:662
Sparse Core Ops, SparseCore 0:
  10.4 43.1 all-gather.1
  92.6 40.8 reduce-scatter.1
